TPU v7x, 128 devices: a whole 4x4x4 slice. The times are simulated.
128 devices in a mesh: leaf: 32 (over x, z, core), rhs: 4 (over y).
Axes of the slice: x: 4, y: 4, z: 4, core: 2. Of those that a mesh axis runs over, the one named last changes fastest.
Arguments:
- vectors: bfloat16 [128, 262144], P('rhs', 'leaf'), may hold values from -6 to 6
- near_blocks: bfloat16 [128, 2048, 2048], P(('leaf', 'rhs')), may hold values from -0.125 to 0.125
- leaf_basis: bfloat16 [128, 2048, 256], P(('leaf', 'rhs')), may hold values from -0.125 to 0.125
- lower_transfer: bfloat16 [128, 2, 256, 256], P(('leaf', 'rhs')), as said below
- lower_coupling: bfloat16 [128, 2, 256, 256], P(('leaf', 'rhs')), as said below
- upper_transfer: bfloat16 [62, 256, 256], replicated, may hold values from -0.3125 to 0.3125
- upper_coupling: bfloat16 [31, 256, 256], replicated, may hold values from -0.375 to 0.375
Outputs:
- product: float32 [128, 262144], P('rhs', 'leaf')
Inputs may be any that keep to these rules, and one draw needn't show every extreme that they name: lower_transfer[d, l] is the same matrix for all d with equal d >> l. lower_coupling[d, l] is the same matrix for all d with equal d >> (l + 1).
All inputs are finite; a program needn't handle non-finite values.
Results may differ from a plain program's by a relative error of at most 0.002.
Values may be sent and summed in bfloat16 or wider, within the bound.
No kernel may reach another device: no remote copies, remote signals or barrier semaphores. Data moves between devices by JAX's collectives and lax.ppermute only.
A program may use at most 128 MiB of HBM per device.

v0:
```python
import jax
import jax.numpy as jnp
from jax import lax
from jax.sharding import PartitionSpec as P


def from_partner(value, axis, apart):
    mask = 2**apart
    pairs = [(source, source ^ mask) for source in range(lax.axis_size(axis))]
    return lax.ppermute(value, axis, pairs)


def product_full(left_side, right_side):
    return jnp.dot(
        left_side, right_side, precision=lax.Precision.HIGHEST, preferred_element_type=jnp.float32
    )


def pick_row(table, position):
    return lax.dynamic_index_in_dim(table, position, 0, False)


def shards(
    vectors, near_blocks, leaf_basis, lower_transfer, lower_coupling, upper_transfer, upper_coupling
):
    leaf_cols = lax.all_to_all(vectors, "rhs", split_axis=1, concat_axis=0, tiled=True)
    block = near_blocks[0]
    basis = leaf_basis[0]
    coeffs = jnp.dot(leaf_cols, basis, preferred_element_type=jnp.float32)
    rhs_pos = lax.axis_index("rhs")
    leaf_pos = lax.axis_index("leaf")
    lower_levels = lax.axis_size("rhs").bit_length() - 1
    node_count = lax.axis_size("leaf")
    upper_levels = node_count.bit_length() - 1
    saved = []
    for height in range(lower_levels):
        transfer = lower_transfer[0, height].astype(jnp.float32)
        coupling = lower_coupling[0, height].astype(jnp.float32)
        is_right = rhs_pos >> height & 1 == 1
        projected = product_full(coeffs, transfer)
        sibling, sibling_proj = from_partner((coeffs, projected), "rhs", height)
        saved.append((transfer, product_full(sibling, jnp.where(is_right, coupling, coupling.T))))
        coeffs = projected + sibling_proj
    for height in range(upper_levels):
        node_id = node_count + leaf_pos >> height
        transfer = pick_row(upper_transfer, node_id - 2).astype(jnp.float32)
        coupling = pick_row(upper_coupling, (node_id >> 1) - 1).astype(jnp.float32)
        is_right = node_id & 1 == 1
        projected = product_full(coeffs, transfer)
        sibling, sibling_proj = from_partner((coeffs, projected), "leaf", height)
        saved.append((transfer, product_full(sibling, jnp.where(is_right, coupling, coupling.T))))
        coeffs = projected + sibling_proj
    downward = jnp.zeros(coeffs.shape, jnp.float32)
    for transfer, contrib in reversed(saved):
        downward = contrib + product_full(downward, transfer.T)
    far_coeffs = downward.astype(jnp.bfloat16)
    near = lax.dot_general(
        leaf_cols, block, (((1,), (1,)), ((), ())), preferred_element_type=jnp.float32
    )
    far = lax.dot_general(
        far_coeffs, basis, (((1,), (1,)), ((), ())), preferred_element_type=jnp.float32
    )
    return lax.all_to_all(near + far, "rhs", split_axis=0, concat_axis=1, tiled=True)


def solution(mesh):
    in_specs = (
        P("rhs", "leaf"),
        P(("leaf", "rhs"), None, None),
        P(("leaf", "rhs"), None, None),
        P(("leaf", "rhs"), None, None, None),
        P(("leaf", "rhs"), None, None, None),
        P(),
        P(),
    )
    out_specs = P("rhs", "leaf")
    return jax.shard_map(shards, mesh=mesh, in_specs=in_specs, out_specs=out_specs, check_vma=False)
```

profile of v0, /device:TPU:0, one launch (start us, length us, event | category | flops | bytes accessed | tf_op | source)
XLA Modules:
  0.0 107.8 jit_solution(3483411865443998882)
XLA Ops:
  1.2 13.8 %all_to_all.38 = bf16[32,4,2048]{2,0,1:T(8,128)(2,1)S(1)} all-to-all(bf16[32,4,2048]{2,0,1:T(8,128)(2,1)S(1)} %bitcast.141), channel_id=1, replica_groups=mesh['leaf'=32,'rhs'=4] {'rhs'}, dimensions={1} | all-to-all | bytes 1048576 | tf_op jit(solution)/shard_map/all_to_all | solution.py:26
  15.3 1.2 %fusion.30 = f32[128,256]{1,0:T(8,128)S(1)} fusion(f32[128,256]{1,0:T(8,128)S(1)} %fusion.4, bf16[1,2,256,256]{3,2,1,0:T(8,128)(2,1)} %param.10), kind=kOutput, calls=%fused_computation.52 | convolution fusion | flops 100663296 | bytes 393216 | tf_op jit(solution)/shard_map/dot_general | solution.py:14
  17.2 4.4 %collective-permute-done.1 = f32[128,256]{1,0:T(8,128)S(1)} collective-permute-done((f32[128,256]{1,0:T(8,128)S(1)}, f32[128,256]{1,0:T(8,128)S(1)}, u32[]{:S(2)}, u32[]{:S(2)}) %collective-permute-start.1) | collective-permute-done | bytes 131104 | tf_op jit(solution)/shard_map/ppermute | solution.py:10
  23.6 5.7 %collective-permute-done.3 = f32[128,256]{1,0:T(8,128)S(1)} collective-permute-done((f32[128,256]{1,0:T(8,128)S(1)}, f32[128,256]{1,0:T(8,128)S(1)}, u32[]{:S(2)}, u32[]{:S(2)}) %collective-permute-start.3) | collective-permute-done | bytes 131104 | tf_op jit(solution)/shard_map/ppermute | solution.py:10
  29.3 1.2 %fusion.22 = f32[128,256]{1,0:T(8,128)S(1)} fusion(f32[128,256]{1,0:T(8,128)S(1)} %add.112, bf16[62,256,256]{2,1,0:T(8,128)(2,1)} %param.12, s32[]{:T(128)S(6)} %select_n.83), kind=kOutput, calls=%fused_computation.42 | convolution fusion | flops 100663296 | bytes 393220 | tf_op jit(solution)/shard_map/dot_general | solution.py:14
  30.6 1.3 %collective-permute-done.5 = f32[128,256]{1,0:T(8,128)S(1)} collective-permute-done((f32[128,256]{1,0:T(8,128)S(1)}, f32[128,256]{1,0:T(8,128)S(1)}, u32[]{:S(2)}, u32[]{:S(2)}) %collective-permute-start.5) | collective-permute-done | bytes 131104 | tf_op jit(solution)/shard_map/ppermute | solution.py:10
  32.0 1.2 %fusion.18 = f32[128,256]{1,0:T(8,128)S(1)} fusion(f32[128,256]{1,0:T(8,128)S(1)} %add.116, bf16[62,256,256]{2,1,0:T(8,128)(2,1)} %param.12, s32[]{:T(128)S(6)} %select_n.87), kind=kOutput, calls=%fused_computation.37 | convolution fusion | flops 100663296 | bytes 393220 | tf_op jit(solution)/shard_map/dot_general | solution.py:14
  33.2 2.0 %collective-permute-start.7 = (f32[128,256]{1,0:T(8,128)S(1)}, f32[128,256]{1,0:T(8,128)S(1)}, u32[]{:S(2)}, u32[]{:S(2)}) collective-permute-start(f32[128,256]{1,0:T(8,128)S(1)} %fusion.18), channel_id=1, source_target_pairs={{0,8},{4,12},{8,0},{12,4},{16,24},{20,28},{24,16},{28,20},{32,40},... | collective-permute-start | bytes 393224 | tf_op jit(solution)/shard_map/ppermute | solution.py:10
  35.2 3.8 %collective-permute-done.7 = f32[128,256]{1,0:T(8,128)S(1)} collective-permute-done((f32[128,256]{1,0:T(8,128)S(1)}, f32[128,256]{1,0:T(8,128)S(1)}, u32[]{:S(2)}, u32[]{:S(2)}) %collective-permute-start.7) | collective-permute-done | bytes 131104 | tf_op jit(solution)/shard_map/ppermute | solution.py:10
  39.0 1.2 %fusion.14 = f32[128,256]{1,0:T(8,128)S(1)} fusion(f32[128,256]{1,0:T(8,128)S(1)} %add.119, bf16[62,256,256]{2,1,0:T(8,128)(2,1)} %param.12, s32[]{:T(128)S(6)} %select_n.91), kind=kOutput, calls=%fused_computation.32 | convolution fusion | flops 100663296 | bytes 393220 | tf_op jit(solution)/shard_map/dot_general | solution.py:14
  40.2 3.8 %collective-permute-start.9 = (f32[128,256]{1,0:T(8,128)S(1)}, f32[128,256]{1,0:T(8,128)S(1)}, u32[]{:S(2)}, u32[]{:S(2)}) collective-permute-start(f32[128,256]{1,0:T(8,128)S(1)} %fusion.14), channel_id=1, source_target_pairs={{0,16},{4,20},{8,24},{12,28},{16,0},{20,4},{24,8},{28,12},{32,48},... | collective-permute-start | bytes 393224 | tf_op jit(solution)/shard_map/ppermute | solution.py:10
  45.0 2.0 %collective-permute-done.9 = f32[128,256]{1,0:T(8,128)S(1)} collective-permute-done((f32[128,256]{1,0:T(8,128)S(1)}, f32[128,256]{1,0:T(8,128)S(1)}, u32[]{:S(2)}, u32[]{:S(2)}) %collective-permute-start.9) | collective-permute-done | bytes 131104 | tf_op jit(solution)/shard_map/ppermute | solution.py:10
  47.0 1.8 %fusion.10 = f32[128,256]{1,0:T(8,128)} fusion(f32[128,256]{1,0:T(8,128)S(1)} %add.122, bf16[62,256,256]{2,1,0:T(8,128)(2,1)} %param.12, s32[]{:T(128)S(6)} %select_n.95), kind=kOutput, calls=%fused_computation.27 | convolution fusion | flops 100663296 | bytes 393220 | tf_op jit(solution)/shard_map/dot_general | solution.py:14
  48.9 1.5 %collective-permute-start.11 = (f32[128,256]{1,0:T(8,128)}, f32[128,256]{1,0:T(8,128)}, u32[]{:S(2)}, u32[]{:S(2)}) collective-permute-start(f32[128,256]{1,0:T(8,128)} %fusion.10), channel_id=1, source_target_pairs={{0,32},{4,36},{8,40},{12,44},{16,48},{20,52},{24,56},{28,60},{32,0... | collective-permute-start | bytes 393224 | tf_op jit(solution)/shard_map/ppermute | solution.py:10
  50.4 1.3 %bitcast_convert_fusion.4 = (f32[256,256]{1,0:T(8,128)S(1)}, f32[256,256]{1,0:T(8,128)S(1)}, f32[256,256]{1,0:T(8,128)S(1)}, f32[256,256]{1,0:T(8,128)S(1)}, f32[256,256]{1,0:T(8,128)S(1)}) fusion(bf16[31,256,256]{2,1,0:T(8,128)(2,1)} %param.13, s32[]{:T(128)S(6)} %select_n.81, s32[]{:T(128)S(6)} %select_n.89, s32[]{:T(128)S(6)} %select_n.85, ...), kind=kLoop, calls=%fused_computation.44 | loop fusion | flops 327680 | bytes 1966100 | tf_op jit(solution)/shard_map/convert_element_type | solution.py:47
  54.1 1.3 %fusion.6 = f32[128,256]{1,0:T(8,128)S(1)} fusion(bf16[62,256,256]{2,1,0:T(8,128)(2,1)} %param.12, s32[]{:T(128)S(6)} %select_n.99), kind=kOutput, calls=%fused_computation.22 | convolution fusion | flops 100663296 | bytes 262148 | tf_op jit(solution)/shard_map/dot_general | solution.py:14
  57.0 2.8 %collective-permute-start.12 = (f32[128,256]{1,0:T(8,128)S(1)}, f32[128,256]{1,0:T(8,128)S(1)}, u32[]{:S(2)}, u32[]{:S(2)}) collective-permute-start(f32[128,256]{1,0:T(8,128)S(1)} %add.125), channel_id=1, source_target_pairs={{0,64},{4,68},{8,72},{12,76},{16,80},{20,84},{24,88},{28,92},{32,9... | collective-permute-start | bytes 393224 | tf_op jit(solution)/shard_map/ppermute | solution.py:10
  59.8 6.3 %fusion = f32[128,2048]{1,0:T(8,128)S(1)} fusion(bf16[128,2048]{1,0:T(8,128)(2,1)S(1)} %bitcast.138, bf16[1,2048,2048]{2,1,0:T(8,128)(2,1)} %param.8), kind=kOutput, calls=%fused_computation | convolution fusion | flops 1073741824 | bytes 9961472 | tf_op jit(solution)/shard_map/dot_general | solution.py:57
  66.1 2.1 %collective-permute-start.2 = (f32[128,256]{1,0:T(8,128)S(1)}, f32[128,256]{1,0:T(8,128)S(1)}, u32[]{:S(2)}, u32[]{:S(2)}) collective-permute-start(f32[128,256]{1,0:T(8,128)S(1)} %add.111), channel_id=1, source_target_pairs={{0,2},{1,3},{2,0},{3,1},{4,6},{5,7},{6,4},{7,5},{8,10},{9,11},{10,... | collective-permute-start | bytes 393224 | tf_op jit(solution)/shard_map/ppermute | solution.py:10
  68.2 1.6 %collective-permute-start.6 = (f32[128,256]{1,0:T(8,128)S(1)}, f32[128,256]{1,0:T(8,128)S(1)}, u32[]{:S(2)}, u32[]{:S(2)}) collective-permute-start(f32[128,256]{1,0:T(8,128)S(1)} %copy-done.8), channel_id=1, source_target_pairs={{0,8},{4,12},{8,0},{12,4},{16,24},{20,28},{24,16},{28,20},{32,40},... | collective-permute-start | bytes 393224 | tf_op jit(solution)/shard_map/ppermute | solution.py:10
  70.1 1.2 %convolution_add_fusion.1 = f32[128,256]{1,0:T(8,128)S(1)} fusion(f32[128,256]{1,0:T(8,128)S(1)} %fusion.6, f32[128,256]{1,0:T(8,128)S(1)} %collective-permute-done.12, f32[256,256]{0,1:T(8,128)S(1)} %copy-done.3, pred[]{:T(512)S(6)} %eq.27, bf16[31,256,256]{2,1,0:T(8,128)(2,1)} %param.13, s32[]{:T(128)S(6)} %select_n.97), kind=kOutput, calls=%fused_computation.3 | convolution fusion | flops 100827136 | bytes 786437 | tf_op jit(solution)/shard_map/dot_general | solution.py:14
  71.3 1.2 %fusion.8 = f32[128,256]{1,0:T(8,128)S(1)} fusion(f32[128,256]{1,0:T(8,128)S(1)} %convolution_add_fusion.1, bf16[62,256,256]{2,1,0:T(8,128)(2,1)} %param.12, s32[]{:T(128)S(6)} %select_n.95), kind=kOutput, calls=%fused_computation.25 | convolution fusion | flops 100663296 | bytes 393220 | tf_op jit(solution)/shard_map/dot_general | solution.py:14
  72.5 2.9 %collective-permute-done.10 = f32[128,256]{1,0:T(8,128)S(1)} collective-permute-done((f32[128,256]{1,0:T(8,128)S(1)}, f32[128,256]{1,0:T(8,128)S(1)}, u32[]{:S(2)}, u32[]{:S(2)}) %collective-permute-start.10) | collective-permute-done | bytes 131104 | tf_op jit(solution)/shard_map/ppermute | solution.py:10
  75.4 3.6 %collective-permute-start.8 = (f32[128,256]{1,0:T(8,128)S(1)}, f32[128,256]{1,0:T(8,128)S(1)}, u32[]{:S(2)}, u32[]{:S(2)}) collective-permute-start(f32[128,256]{1,0:T(8,128)S(1)} %copy-done.10), channel_id=1, source_target_pairs={{0,16},{4,20},{8,24},{12,28},{16,0},{20,4},{24,8},{28,12},{32,48},... | collective-permute-start | bytes 393224 | tf_op jit(solution)/shard_map/ppermute | solution.py:10
  79.0 1.2 %convolution_add_fusion.2 = f32[128,256]{1,0:T(8,128)S(1)} fusion(f32[128,256]{1,0:T(8,128)S(1)} %fusion.8, f32[128,256]{1,0:T(8,128)S(1)} %collective-permute-done.10, f32[256,256]{0,1:T(8,128)S(1)} %copy.39, pred[]{:T(512)S(6)} %eq.26, bf16[31,256,256]{2,1,0:T(8,128)(2,1)} %param.13, s32[]{:T(128)S(6)} %select_n.93), kind=kOutput, calls=%fused_computation.4 | convolution fusion | flops 100827136 | bytes 786437 | tf_op jit(solution)/shard_map/dot_general | solution.py:14
  80.2 1.2 %fusion.12 = f32[128,256]{1,0:T(8,128)S(1)} fusion(f32[128,256]{1,0:T(8,128)S(1)} %convolution_add_fusion.2, bf16[62,256,256]{2,1,0:T(8,128)(2,1)} %param.12, s32[]{:T(128)S(6)} %select_n.91), kind=kOutput, calls=%fused_computation.30 | convolution fusion | flops 100663296 | bytes 393220 | tf_op jit(solution)/shard_map/dot_general | solution.py:14
  82.0 1.2 %convolution_add_fusion.3 = f32[128,256]{1,0:T(8,128)S(1)} fusion(f32[128,256]{1,0:T(8,128)S(1)} %fusion.12, f32[128,256]{1,0:T(8,128)S(1)} %collective-permute-done.8, f32[256,256]{0,1:T(8,128)S(1)} %copy.38, pred[]{:T(512)S(6)} %eq.25, bf16[31,256,256]{2,1,0:T(8,128)(2,1)} %param.13, s32[]{:T(128)S(6)} %select_n.89), kind=kOutput, calls=%fused_computation.5 | convolution fusion | flops 100827136 | bytes 786437 | tf_op jit(solution)/shard_map/dot_general | solution.py:14
  83.2 1.2 %fusion.16 = f32[128,256]{1,0:T(8,128)S(1)} fusion(f32[128,256]{1,0:T(8,128)S(1)} %convolution_add_fusion.3, bf16[62,256,256]{2,1,0:T(8,128)(2,1)} %param.12, s32[]{:T(128)S(6)} %select_n.87), kind=kOutput, calls=%fused_computation.35 | convolution fusion | flops 100663296 | bytes 393220 | tf_op jit(solution)/shard_map/dot_general | solution.py:14
  84.4 1.2 %convolution_add_fusion.4 = f32[128,256]{1,0:T(8,128)S(1)} fusion(f32[128,256]{1,0:T(8,128)S(1)} %fusion.16, f32[128,256]{1,0:T(8,128)S(1)} %collective-permute-done.6, f32[256,256]{0,1:T(8,128)S(1)} %copy.37, pred[]{:T(512)S(6)} %eq.24, bf16[31,256,256]{2,1,0:T(8,128)(2,1)} %param.13, s32[]{:T(128)S(6)} %select_n.85), kind=kOutput, calls=%fused_computation.6 | convolution fusion | flops 100827136 | bytes 786437 | tf_op jit(solution)/shard_map/dot_general | solution.py:14
  85.6 1.2 %fusion.20 = f32[128,256]{1,0:T(8,128)S(1)} fusion(f32[128,256]{1,0:T(8,128)S(1)} %convolution_add_fusion.4, bf16[62,256,256]{2,1,0:T(8,128)(2,1)} %param.12, s32[]{:T(128)S(6)} %select_n.83), kind=kOutput, calls=%fused_computation.40 | convolution fusion | flops 100663296 | bytes 393220 | tf_op jit(solution)/shard_map/dot_general | solution.py:14
  86.8 1.2 %convolution_add_fusion.5 = f32[128,256]{1,0:T(8,128)S(1)} fusion(f32[128,256]{1,0:T(8,128)S(1)} %fusion.20, f32[128,256]{1,0:T(8,128)S(1)} %collective-permute-done.4, f32[256,256]{0,1:T(8,128)S(1)} %copy.36, pred[]{:T(512)S(6)} %eq.23, bf16[31,256,256]{2,1,0:T(8,128)(2,1)} %param.13, s32[]{:T(128)S(6)} %select_n.81), kind=kOutput, calls=%fused_computation.7 | convolution fusion | flops 100827136 | bytes 786437 | tf_op jit(solution)/shard_map/dot_general | solution.py:14
  89.8 16.9 %all_to_all.39 = f32[4,32,2048]{2,1,0:T(8,128)S(1)} all-to-all(f32[4,32,2048]{2,1,0:T(8,128)S(1)} %bitcast.139), channel_id=1, replica_groups=mesh['leaf'=32,'rhs'=4] {'rhs'}, dimensions={0} | all-to-all | bytes 2097152 | tf_op jit(solution)/shard_map/all_to_all | solution.py:63
  (64 shorter events, 12.9 us)
Async XLA Ops:
  0.0 15.0 %copy-start = (bf16[1,2048,256]{2,1,0:T(8,128)(2,1)S(1)}, bf16[1,2048,256]{2,1,0:T(8,128)(2,1)}, u32[]{:S(2)}) copy-start(bf16[1,2048,256]{2,1,0:T(8,128)(2,1)} %param.9) | copy-start | bytes 3145732
  15.3 1.8 %copy-start.13 = (f32[128,256]{1,0:T(8,128)}, f32[128,256]{1,0:T(8,128)S(1)}, u32[]{:S(2)}) copy-start(f32[128,256]{1,0:T(8,128)S(1)} %fusion.4) | copy-start | bytes 393220
  16.5 5.0 %collective-permute-start.1 = (f32[128,256]{1,0:T(8,128)S(1)}, f32[128,256]{1,0:T(8,128)S(1)}, u32[]{:S(2)}, u32[]{:S(2)}) collective-permute-start(f32[128,256]{1,0:T(8,128)S(1)} %fusion.30), channel_id=1, source_target_pairs={{0,1},{1,0},{2,3},{3,2},{4,5},{5,4},{6,7},{7,6},{8,9},{9,8},{10,11... | collective-permute-start | bytes 393224 | tf_op jit(solution)/shard_map/ppermute | solution.py:10
  22.7 6.6 %collective-permute-start.3 = (f32[128,256]{1,0:T(8,128)S(1)}, f32[128,256]{1,0:T(8,128)S(1)}, u32[]{:S(2)}, u32[]{:S(2)}) collective-permute-start(f32[128,256]{1,0:T(8,128)S(1)} %fusion.26), channel_id=1, source_target_pairs={{0,2},{1,3},{2,0},{3,1},{4,6},{5,7},{6,4},{7,5},{8,10},{9,11},{10,... | collective-permute-start | bytes 393224 | tf_op jit(solution)/shard_map/ppermute | solution.py:10
  29.3 10.9 %copy-start.5 = (f32[128,256]{1,0:T(8,128)}, f32[128,256]{1,0:T(8,128)S(1)}, u32[]{:S(2)}) copy-start(f32[128,256]{1,0:T(8,128)S(1)} %add.112) | copy-start | bytes 393220
  30.5 1.4 %collective-permute-start.5 = (f32[128,256]{1,0:T(8,128)S(1)}, f32[128,256]{1,0:T(8,128)S(1)}, u32[]{:S(2)}, u32[]{:S(2)}) collective-permute-start(f32[128,256]{1,0:T(8,128)S(1)} %fusion.22), channel_id=1, source_target_pairs={{0,4},{4,0},{8,12},{12,8},{16,20},{20,16},{24,28},{28,24},{32,36},... | collective-permute-start | bytes 393224 | tf_op jit(solution)/shard_map/ppermute | solution.py:10
  32.0 8.3 %copy-start.7 = (f32[128,256]{1,0:T(8,128)}, f32[128,256]{1,0:T(8,128)S(1)}, u32[]{:S(2)}) copy-start(f32[128,256]{1,0:T(8,128)S(1)} %add.116) | copy-start | bytes 393220
  33.2 5.8 %collective-permute-start.7 = (f32[128,256]{1,0:T(8,128)S(1)}, f32[128,256]{1,0:T(8,128)S(1)}, u32[]{:S(2)}, u32[]{:S(2)}) collective-permute-start(f32[128,256]{1,0:T(8,128)S(1)} %fusion.18), channel_id=1, source_target_pairs={{0,8},{4,12},{8,0},{12,4},{16,24},{20,28},{24,16},{28,20},{32,40},... | collective-permute-start | bytes 393224 | tf_op jit(solution)/shard_map/ppermute | solution.py:10
  39.0 1.2 %copy-start.9 = (f32[128,256]{1,0:T(8,128)}, f32[128,256]{1,0:T(8,128)S(1)}, u32[]{:S(2)}) copy-start(f32[128,256]{1,0:T(8,128)S(1)} %add.119) | copy-start | bytes 393220
  40.2 6.8 %collective-permute-start.9 = (f32[128,256]{1,0:T(8,128)S(1)}, f32[128,256]{1,0:T(8,128)S(1)}, u32[]{:S(2)}, u32[]{:S(2)}) collective-permute-start(f32[128,256]{1,0:T(8,128)S(1)} %fusion.14), channel_id=1, source_target_pairs={{0,16},{4,20},{8,24},{12,28},{16,0},{20,4},{24,8},{28,12},{32,48},... | collective-permute-start | bytes 393224 | tf_op jit(solution)/shard_map/ppermute | solution.py:10
  47.0 1.9 %copy-start.11 = (f32[128,256]{1,0:T(8,128)}, f32[128,256]{1,0:T(8,128)S(1)}, u32[]{:S(2)}) copy-start(f32[128,256]{1,0:T(8,128)S(1)} %add.122) | copy-start | bytes 393220
  48.9 7.2 %collective-permute-start.11 = (f32[128,256]{1,0:T(8,128)}, f32[128,256]{1,0:T(8,128)}, u32[]{:S(2)}, u32[]{:S(2)}) collective-permute-start(f32[128,256]{1,0:T(8,128)} %fusion.10), channel_id=1, source_target_pairs={{0,32},{4,36},{8,40},{12,44},{16,48},{20,52},{24,56},{28,60},{32,0... | collective-permute-start | bytes 393224 | tf_op jit(solution)/shard_map/ppermute | solution.py:10
  53.0 17.1 %copy-start.3 = (f32[256,256]{0,1:T(8,128)S(1)}, f32[256,256]{0,1:T(8,128)}, u32[]{:S(2)}) copy-start(f32[256,256]{0,1:T(8,128)} %copy.40) | copy-start | bytes 786436
  54.0 34.0 %copy-start.1 = (bf16[1,2,256,256]{3,2,1,0:T(8,128)(2,1)S(1)}, bf16[1,2,256,256]{3,2,1,0:T(8,128)(2,1)}, u32[]{:S(2)}) copy-start(bf16[1,2,256,256]{3,2,1,0:T(8,128)(2,1)} %param.10) | copy-start | bytes 786436
  54.0 14.2 %copy-start.6 = (f32[128,256]{1,0:T(8,128)S(1)}, f32[128,256]{1,0:T(8,128)}, u32[]{:S(2)}) copy-start(f32[128,256]{1,0:T(8,128)} %copy-done.5) | copy-start | bytes 393220
  54.0 14.2 %copy-start.8 = (f32[128,256]{1,0:T(8,128)S(1)}, f32[128,256]{1,0:T(8,128)}, u32[]{:S(2)}) copy-start(f32[128,256]{1,0:T(8,128)} %copy-done.7) | copy-start | bytes 393220
  54.1 15.8 %copy-start.12 = (f32[128,256]{1,0:T(8,128)S(1)}, f32[128,256]{1,0:T(8,128)}, u32[]{:S(2)}) copy-start(f32[128,256]{1,0:T(8,128)} %copy-done.11) | copy-start | bytes 393220
  54.1 21.3 %copy-start.10 = (f32[128,256]{1,0:T(8,128)S(1)}, f32[128,256]{1,0:T(8,128)}, u32[]{:S(2)}) copy-start(f32[128,256]{1,0:T(8,128)} %copy-done.9) | copy-start | bytes 393220
  55.4 33.0 %copy-start.2 = (bf16[1,2,256,256]{3,2,1,0:T(8,128)(2,1)S(1)}, bf16[1,2,256,256]{3,2,1,0:T(8,128)(2,1)}, u32[]{:S(2)}) copy-start(bf16[1,2,256,256]{3,2,1,0:T(8,128)(2,1)} %param.11) | copy-start | bytes 786436
  55.4 33.0 %copy-start.4 = (f32[256,256]{0,1:T(8,128)S(1)}, f32[256,256]{0,1:T(8,128)}, u32[]{:S(2)}) copy-start(f32[256,256]{0,1:T(8,128)} %copy.35) | copy-start | bytes 786436
  55.4 33.6 %collective-permute-start = (f32[128,256]{1,0:T(8,128)}, f32[128,256]{1,0:T(8,128)S(1)}, u32[]{:S(2)}, u32[]{:S(2)}) collective-permute-start(f32[128,256]{1,0:T(8,128)} %copy-done.13), channel_id=1, source_target_pairs={{0,1},{1,0},{2,3},{3,2},{4,5},{5,4},{6,7},{7,6},{8,9},{9,8},{10,11... | collective-permute-start | bytes 393224 | tf_op jit(solution)/shard_map/ppermute | solution.py:10
  57.0 12.8 %collective-permute-start.12 = (f32[128,256]{1,0:T(8,128)S(1)}, f32[128,256]{1,0:T(8,128)S(1)}, u32[]{:S(2)}, u32[]{:S(2)}) collective-permute-start(f32[128,256]{1,0:T(8,128)S(1)} %add.125), channel_id=1, source_target_pairs={{0,64},{4,68},{8,72},{12,76},{16,80},{20,84},{24,88},{28,92},{32,9... | collective-permute-start | bytes 393224 | tf_op jit(solution)/shard_map/ppermute | solution.py:10
  66.1 22.3 %collective-permute-start.2 = (f32[128,256]{1,0:T(8,128)S(1)}, f32[128,256]{1,0:T(8,128)S(1)}, u32[]{:S(2)}, u32[]{:S(2)}) collective-permute-start(f32[128,256]{1,0:T(8,128)S(1)} %add.111), channel_id=1, source_target_pairs={{0,2},{1,3},{2,0},{3,1},{4,6},{5,7},{6,4},{7,5},{8,10},{9,11},{10,... | collective-permute-start | bytes 393224 | tf_op jit(solution)/shard_map/ppermute | solution.py:10
  68.2 18.6 %collective-permute-start.4 = (f32[128,256]{1,0:T(8,128)S(1)}, f32[128,256]{1,0:T(8,128)S(1)}, u32[]{:S(2)}, u32[]{:S(2)}) collective-permute-start(f32[128,256]{1,0:T(8,128)S(1)} %copy-done.6), channel_id=1, source_target_pairs={{0,4},{4,0},{8,12},{12,8},{16,20},{20,16},{24,28},{28,24},{32,36},... | collective-permute-start | bytes 393224 | tf_op jit(solution)/shard_map/ppermute | solution.py:10
  68.2 16.2 %collective-permute-start.6 = (f32[128,256]{1,0:T(8,128)S(1)}, f32[128,256]{1,0:T(8,128)S(1)}, u32[]{:S(2)}, u32[]{:S(2)}) collective-permute-start(f32[128,256]{1,0:T(8,128)S(1)} %copy-done.8), channel_id=1, source_target_pairs={{0,8},{4,12},{8,0},{12,4},{16,24},{20,28},{24,16},{28,20},{32,40},... | collective-permute-start | bytes 393224 | tf_op jit(solution)/shard_map/ppermute | solution.py:10
  69.8 5.6 %collective-permute-start.10 = (f32[128,256]{1,0:T(8,128)S(1)}, f32[128,256]{1,0:T(8,128)S(1)}, u32[]{:S(2)}, u32[]{:S(2)}) collective-permute-start(f32[128,256]{1,0:T(8,128)S(1)} %copy-done.12), channel_id=1, source_target_pairs={{0,32},{4,36},{8,40},{12,44},{16,48},{20,52},{24,56},{28,60},{32,0... | collective-permute-start | bytes 393224 | tf_op jit(solution)/shard_map/ppermute | solution.py:10
  75.4 6.6 %collective-permute-start.8 = (f32[128,256]{1,0:T(8,128)S(1)}, f32[128,256]{1,0:T(8,128)S(1)}, u32[]{:S(2)}, u32[]{:S(2)}) collective-permute-start(f32[128,256]{1,0:T(8,128)S(1)} %copy-done.10), channel_id=1, source_target_pairs={{0,16},{4,20},{8,24},{12,28},{16,0},{20,4},{24,8},{28,12},{32,48},... | collective-permute-start | bytes 393224 | tf_op jit(solution)/shard_map/ppermute | solution.py:10
where the time goes:
time: 108 us
  blocking collectives  30.7 us (28%)
  matrix products  28 us (26%)
  waiting for transfers between devices  20.7 us (19%)
  starting transfers between devices  19.9 us (18%)
  local copies, waits for them, and re-layouts  4.62 us (4%)
  other arithmetic  3.35 us (3%)
    dot_general x20, matrix products, product_full(): jnp.dot(left_side, right_side, precision=lax.Precision.HIGHEST, preferred...  21 us
    ppermute x13, waiting for transfers between devices, from_partner(): return lax.ppermute(value, axis, pairs)  20.7 us
    ppermute x13, starting transfers between devices, from_partner(): return lax.ppermute(value, axis, pairs)  19.9 us
    all_to_all x1, blocking collectives, shards(): lax.all_to_all(near + far, 'rhs', split_axis=0, concat_axis=1, tiled=True)  16.9 us
    all_to_all x1, blocking collectives, shards(): lax.all_to_all(vectors, 'rhs', split_axis=1, concat_axis=0, tiled=True)  13.8 us
    dot_general x1, matrix products, shards(): lax.dot_general(leaf_cols, block, (((1,), (1,)), ((), ())), preferred_ele...  6.26 us
  transfers between devices with their start and end apart: 13, of which 7 were waited for; matrix products, arithmetic and copies ran while one was open for 23% of the time, Pallas kernels for 0%

commit v1 on v0

v1 whole, which is shorter than its diff:
```python
import jax
import jax.numpy as jnp
from jax import lax
from jax.experimental import pallas as pl
from jax.experimental.pallas import tpu as pltpu
from jax.sharding import PartitionSpec as P

F32 = jnp.float32
BF16 = jnp.bfloat16
F16 = jnp.float16
VMEM = pl.BlockSpec(memory_space=pltpu.VMEM)
LIMIT = 32 * 2**20
EXTRA = 16


def swap(value, axis, mask):
    pairs = [(source, source ^ mask) for source in range(lax.axis_size(axis))]
    return lax.ppermute(value, axis, pairs)


def split(value):
    high = value.astype(BF16)
    return high, (value - high.astype(F32)).astype(BF16)


def dot(a, b):
    return jnp.dot(a, b, preferred_element_type=F32)


def dot_narrow(value, matrix):
    high, low = split(value)
    return dot(high, matrix) + dot(low, matrix)


def dot_wide(value, high_matrix, low_matrix):
    high, low = split(value)
    return dot(high, high_matrix) + (dot(low, high_matrix) + dot(high, low_matrix))


def encode(value):
    largest = jnp.max(jnp.abs(value), axis=0, keepdims=True)
    power = jnp.ceil(jnp.log2(jnp.maximum(largest, 1e-30))) - 14.0
    scaled = value * jnp.exp2(-power)
    return scaled, jnp.broadcast_to(power, (EXTRA, value.shape[1]))


def put_encoded(ref, value, start=0):
    rows = value.shape[0]
    scaled, power = encode(value)
    ref[start : start + rows, :] = scaled
    ref[start + rows : start + rows + EXTRA, :] = power


def decode(ref, rows, start=0):
    power = ref[start + rows : start + rows + 1, :]
    return ref[start : start + rows, :] * jnp.exp2(power)


def call(body, outs, operands, flops=0, moved=0, **more):
    return pl.pallas_call(
        body,
        out_shape=outs,
        compiler_params=pltpu.CompilerParams(vmem_limit_bytes=LIMIT),
        cost_estimate=pl.CostEstimate(flops=flops, bytes_accessed=moved, transcendentals=0),
        **more,
    )(*operands)


def shape(*dims, dtype=F32):
    return jax.ShapeDtypeStruct(dims, dtype)


def compose_body(rank, place, *refs):
    lower_t, lower_b = refs[0], refs[1]
    uppers = [ref[0] for ref in refs[2:14]]
    couplings = [ref[0] for ref in refs[14:19]]
    pair_ref, up_high, up_low, acc_high, acc_low, top_high, top_low = refs[19:26]
    rhs_pos, node = place[0], place[1]
    own2, sib2 = uppers[0:2]
    level3 = uppers[2:6]
    own4, sib4 = uppers[6:8]
    own5, _, third5, fourth5 = uppers[8:12]

    def oriented(coupling, is_right):
        wide = coupling.astype(F32)
        return jnp.where(is_right == 1, wide, wide.T).astype(BF16)

    def put(high_ref, low_ref, slot, value):
        high, low = split(value)
        high_ref[slot * rank : (slot + 1) * rank, :] = high
        low_ref[slot * rank : (slot + 1) * rank, :] = low
        return high, low

    def transposed(matrix):
        return matrix.astype(F32).T.astype(BF16)

    def times(matrix, parts):
        return dot(matrix, parts[0]) + dot(matrix, parts[1])

    pair_ref[:rank, :] = own2
    pair_ref[rank:, :] = sib2
    for slot, matrix in enumerate(level3):
        put(up_high, up_low, slot, dot(matrix, own4 if slot < 2 else sib4))

    put(acc_high, acc_low, 0, oriented(lower_b[0, 0], rhs_pos & 1).astype(F32))
    down = split(transposed(lower_t[0, 0]).astype(F32))
    put(acc_high, acc_low, 1, times(oriented(lower_b[0, 1], rhs_pos >> 1 & 1), down))
    down = split(times(transposed(lower_t[0, 1]), down))
    put(acc_high, acc_low, 2, times(oriented(couplings[0], node & 1), down))
    down = split(times(transposed(own2), down))
    put(acc_high, acc_low, 3, times(oriented(couplings[1], node >> 1 & 1), down))
    down = split(times(transposed(level3[0]), down))
    across = split(times(oriented(couplings[2], node >> 2 & 1), down))
    put(acc_high, acc_low, 4, times(level3[2], across))
    put(acc_high, acc_low, 5, times(level3[3], across))
    down = split(times(transposed(own4), down))
    put(top_high, top_low, 0, times(oriented(couplings[3], node >> 3 & 1), down))
    down = split(times(transposed(own5), down))
    across = split(times(oriented(couplings[4], node >> 4 & 1), down))
    put(top_high, top_low, 1, times(third5, across))
    put(top_high, top_low, 2, times(fourth5, across))


def compose(place, lower_transfer, lower_coupling, upper_transfer, upper_coupling):
    rank = lower_transfer.shape[-1]

    def upper(height, mask):
        return pl.BlockSpec(
            (1, rank, rank), lambda i, place: (((place[1] >> height) ^ mask) - 2, 0, 0)
        )

    def coupling(height):
        return pl.BlockSpec(
            (1, rank, rank), lambda i, place: ((place[1] >> (height + 1)) - 1, 0, 0)
        )

    def whole(array):
        return pl.BlockSpec(array.shape, lambda i, place: (0,) * array.ndim)

    picks = [(0, 0), (0, 1), (1, 0), (1, 1), (1, 2), (1, 3), (2, 0), (2, 1), (3, 0), (3, 1), (3, 2), (3, 3)]
    outs = [shape(n * rank, rank, dtype=BF16) for n in (2, 4, 4, 6, 6, 3, 3)]
    spec = pltpu.PrefetchScalarGridSpec(
        num_scalar_prefetch=1,
        grid=(1,),
        in_specs=[whole(lower_transfer), whole(lower_coupling)]
        + [upper(*pick) for pick in picks]
        + [coupling(height) for height in range(5)],
        out_specs=[pl.BlockSpec(out.shape, lambda i, place: (0, 0)) for out in outs],
    )

    def body(place_ref, *refs):
        compose_body(rank, place_ref, *refs)

    return call(
        body,
        outs,
        (place, lower_transfer, lower_coupling) + (upper_transfer,) * 12 + (upper_coupling,) * 5,
        flops=34 * 2 * rank**3,
        moved=40 * 2 * rank**2,
        grid_spec=spec,
    )


def shards(
    vectors, near_blocks, leaf_basis, lower_transfer, lower_coupling, upper_transfer, upper_coupling
):
    rhs_pos = lax.axis_index("rhs")
    leaf_pos = lax.axis_index("leaf")
    part = vectors.shape[0]
    leaf, rank = leaf_basis.shape[1:]
    total = part * lax.axis_size("rhs")
    place = jnp.stack([rhs_pos, leaf_pos + lax.axis_size("leaf")]).astype(jnp.int32)
    masks = (1, 3, 2)

    blocks = [lax.dynamic_slice(vectors, (0, (rhs_pos ^ mask) * leaf), (part, leaf)) for mask in (0,) + masks]
    came = [swap(block, "rhs", mask) for block, mask in zip(blocks[1:], masks)]

    pair, up_high, up_low, acc_high, acc_low, top_high, top_low = compose(
        place, lower_transfer, lower_coupling, upper_transfer, upper_coupling
    )

    def leaf_body(place_ref, own, first, second, third, basis, transfer, cols, sibling_msg, cousin_msg, kept):
        position = place_ref[0]
        for mask, ref in zip((0,) + masks, (own, first, second, third)):
            cols[pl.ds(pl.multiple_of((position ^ mask) * part, part), part), :] = ref[...]
        coeffs = dot(cols[...], basis[0])
        middle = dot_narrow(coeffs, transfer[0, 0])
        upward = dot_narrow(middle, transfer[0, 1])
        put_encoded(sibling_msg, coeffs)
        put_encoded(cousin_msg, middle)
        put_encoded(sibling_msg, upward, total + EXTRA)
        put_encoded(cousin_msg, upward, total + EXTRA)
        kept[...] = upward

    smem = pl.BlockSpec(memory_space=pltpu.SMEM)
    message = shape(2 * (total + EXTRA), rank)
    cols, sibling_msg, cousin_msg, upward = call(
        leaf_body,
        (shape(total, leaf, dtype=BF16), message, message, shape(total, rank)),
        (place, blocks[0], *came, leaf_basis, lower_transfer),
        flops=2 * total * leaf * rank,
        moved=2**21,
        in_specs=[smem] + [VMEM] * 6,
        out_specs=[VMEM] * 4,
    )
    sibling_msg = sibling_msg.astype(F16)
    cousin_msg = cousin_msg.astype(F16)
    from_sibling = swap(sibling_msg, "rhs", 1).astype(F32)
    from_third = swap(cousin_msg, "rhs", 3).astype(F32)
    from_second = swap(cousin_msg, "rhs", 2).astype(F32)

    steps = 8

    def near_body(cols_ref, block_ref, out_ref):
        out_ref[...] = lax.dot_general(
            cols_ref[...], block_ref[0], (((1,), (1,)), ((), ())), preferred_element_type=F32
        )

    near = call(
        near_body,
        shape(total, leaf),
        (cols, near_blocks),
        flops=2 * total * leaf * leaf,
        moved=2 * leaf * leaf + 6 * total * leaf,
        grid=(steps,),
        in_specs=[
            pl.BlockSpec((total, leaf), lambda i: (0, 0)),
            pl.BlockSpec((1, leaf // steps, leaf), lambda i: (0, i, 0)),
        ],
        out_specs=pl.BlockSpec((total, leaf // steps), lambda i: (0, i)),
    )

    def group_body(own, a, b, c, out):
        start = total + EXTRA
        out[...] = own[...] + decode(a, total, start) + (decode(b, total, start) + decode(c, total, start))

    group = call(
        group_body,
        shape(total, rank),
        (upward, from_sibling, from_third, from_second),
        moved=2**20,
        in_specs=[VMEM] * 4,
        out_specs=VMEM,
    )
    group_sib = swap(group, "leaf", 1)

    def chip_body(own, sibling, matrices, out, kept):
        value = dot_narrow(own[...], matrices[:rank, :]) + dot_narrow(sibling[...], matrices[rank:, :])
        kept[...] = value
        put_encoded(out, value)

    chip_msg, chip = call(
        chip_body,
        (shape(total + EXTRA, rank), shape(total, rank)),
        (group, group_sib, pair),
        flops=8 * total * rank * rank,
        moved=2**20,
        in_specs=[VMEM] * 3,
        out_specs=[VMEM] * 2,
    )
    chip_msg = chip_msg.astype(F16)
    chips = [swap(chip_msg, "leaf", 2 * mask).astype(F32) for mask in (1, 2, 3)]

    def line_body(own, a, b, c, high, low, out):
        value = jnp.concatenate([own[...]] + [decode(ref, total) for ref in (a, b, c)], axis=1)
        put_encoded(out, dot_wide(value, high[...], low[...]))

    line_msg = call(
        line_body,
        shape(total + EXTRA, rank),
        (chip, *chips, up_high, up_low),
        flops=24 * total * rank * rank,
        moved=2**21,
        in_specs=[VMEM] * 6,
        out_specs=VMEM,
    )
    line_msg = line_msg.astype(F16)
    lines = [swap(line_msg, "leaf", 8 * mask).astype(F32) for mask in (1, 2, 3)]

    def near_tree_body(y1, y3, y2, core, z1, z2, z3, high, low, out):
        value = jnp.concatenate(
            [decode(y1, total), decode(y3, total) + decode(y2, total), core[...]]
            + [decode(ref, total) for ref in (z1, z2, z3)],
            axis=1,
        )
        out[...] = dot_wide(value, high[...], low[...])

    partial = call(
        near_tree_body,
        shape(total, rank),
        (from_sibling, from_third, from_second, group_sib, *chips, acc_high, acc_low),
        flops=36 * total * rank * rank,
        moved=2**21,
        in_specs=[VMEM] * 9,
        out_specs=VMEM,
    )

    def last_body(place_ref, part_ref, a, b, c, high, low, basis, near_ref, own, first, second, third, both):
        value = jnp.concatenate([decode(ref, total) for ref in (a, b, c)], axis=1)
        coeffs = (part_ref[...] + dot_wide(value, high[...], low[...])).astype(BF16)
        far = lax.dot_general(coeffs, basis[0], (((1,), (1,)), ((), ())), preferred_element_type=F32)
        both[...] = near_ref[...] + far
        position = place_ref[0]
        for mask, ref in zip((0,) + masks, (own, first, second, third)):
            rows = both[pl.ds(pl.multiple_of((position ^ mask) * part, part), part), :]
            ref[...] = rows.astype(ref.dtype)

    sent = shape(part, leaf, dtype=BF16)
    own, *blocks = call(
        last_body,
        (shape(part, leaf), sent, sent, sent),
        (place, partial, *lines, top_high, top_low, leaf_basis, near),
        flops=2 * total * leaf * rank,
        moved=2**22,
        in_specs=[smem] + [VMEM] * 8,
        out_specs=[VMEM] * 4,
        scratch_shapes=[pltpu.VMEM((total, leaf), F32)],
    )
    blocks = [swap(block, "rhs", mask) for block, mask in zip(blocks, masks)]

    def join(place_ref, own_ref, first, second, third, out):
        position = place_ref[0]
        for mask, ref in zip((0,) + masks, (own_ref, first, second, third)):
            out[:, pl.ds(pl.multiple_of((position ^ mask) * leaf, leaf), leaf)] = ref[...].astype(F32)

    return call(
        join,
        shape(part, 4 * leaf),
        (place, own, *blocks),
        moved=2**21,
        in_specs=[smem] + [VMEM] * 4,
        out_specs=VMEM,
    )


def solution(mesh):
    in_specs = (
        P("rhs", "leaf"),
        P(("leaf", "rhs"), None, None),
        P(("leaf", "rhs"), None, None),
        P(("leaf", "rhs"), None, None, None),
        P(("leaf", "rhs"), None, None, None),
        P(),
        P(),
    )
    out_specs = P("rhs", "leaf")
    return jax.shard_map(shards, mesh=mesh, in_specs=in_specs, out_specs=out_specs, check_vma=False)
```

time: 108 us -> 70.5 us (0.65)
  blocking collectives: 30.7 us -> 0 us
  matrix products: 28 us -> 0 us
  Pallas kernels: 0 us -> 12.7 us
  local copies, waits for them, and re-layouts: 4.62 us -> 10.7 us
  starting transfers between devices: 19.9 us -> 23.5 us
  other arithmetic: 3.35 us -> 0.27 us
  waiting for transfers between devices: 20.7 us -> 22.7 us
    all_to_all x2 -> x0, blocking collectives: 30.7 us -> none  [the longest x1 16.9 us: shards(): lax.all_to_all(near + far, 'rhs', split_axis=0, concat_axis=1, tiled=True)]
    dot_general x23 -> x0, matrix products: 28 us -> none  [the longest x20 21 us: product_full(): jnp.dot(left_side, right_side, precision=lax.Precision.HIGHEST, preferred...]
    pallas_call x0 -> x9, Pallas kernels: none -> 12.7 us  [call(): pl.pallas_call(body, out_shape=outs, compiler_params=pltpu.CompilerParams...]
    unnamed x28 -> x16, local copies, waits for them, and re-layouts: 0.07 us -> 9.54 us
    ppermute x13 -> x16, starting transfers between devices: 19.9 us -> 23.5 us  [swap(): return lax.ppermute(value, axis, pairs)]
    convert_element_type x7 -> x0, local copies, waits for them, and re-layouts: 2.33 us -> none  [the longest x5 1.35 us: shards(): coupling = pick_row(upper_coupling, (node_id >> 1) - 1).astype(jnp.float32)]
    all_to_all x2 -> x0, local copies, waits for them, and re-layouts: 2.23 us -> none  [the longest x1 1.16 us: shards(): lax.all_to_all(vectors, 'rhs', split_axis=1, concat_axis=0, tiled=True)]
    convert_element_type x2 -> x13, other arithmetic: 2.28 us -> 0.19 us  [the longest x3 0.04 us: shards(): lines = [swap(line_msg, 'leaf', 8 * mask).astype(F32) for mask in (1, 2, 3)]]
  transfers between devices with their start and end apart: 13 -> 16, of which waited for: 7 -> 12; matrix products, arithmetic and copies ran while one was open for 23% -> 0% of each run, Pallas kernels for 0% -> 11%
where the time goes in v1:
time: 70.5 us; the launch traced here: 70.1 us
  starting transfers between devices  23.5 us (33%)
  waiting for transfers between devices  22.7 us (32%)
  Pallas kernels  12.7 us (18%)
  local copies, waits for them, and re-layouts  10.7 us (15%)
    ppermute x16, starting transfers between devices, swap(): return lax.ppermute(value, axis, pairs)  23.5 us
    ppermute x16, waiting for transfers between devices, swap(): return lax.ppermute(value, axis, pairs)  22.7 us
    pallas_call x9, Pallas kernels, call(): pl.pallas_call(body, out_shape=outs, compiler_params=pltpu.CompilerParams...  12.7 us
    unnamed x16, local copies, waits for them, and re-layouts  9.54 us
  transfers between devices with their start and end apart: 16, of which 12 were waited for; matrix products, arithmetic and copies ran while one was open for 0% of the time, Pallas kernels for 11%

profile of v1, /device:TPU:0, one launch (start us, length us, event | category | flops | bytes accessed | tf_op | source)
XLA Modules:
  0.0 70.1 jit_solution(7026631053891712766)
XLA Ops:
  0.0 1.1 %constant_dynamic-slice_fusion = (bf16[32,2048]{1,0:T(8,128)(2,1)S(1)}, bf16[32,2048]{1,0:T(8,128)(2,1)S(1)}, bf16[32,2048]{1,0:T(8,128)(2,1)S(1)}, bf16[32,2048]{1,0:T(8,128)(2,1)S(1)}) fusion(bf16[32,8192]{1,0:T(8,128)(2,1)} %param.7, s32[]{:T(128)S(6)} %select_n.15, s32[]{:T(128)S(6)} %select_n.13, s32[]{:T(128)S(6)} %select_n.12, s32[]{:T(128)S(6)} %select_n.14), kind=kLoop, calls=%fused_computation | loop fusion | bytes 1048592 | tf_op jit(solution)/shard_map/dynamic_slice | solution.py:175
  1.1 1.7 %collective-permute-start = (bf16[32,2048]{1,0:T(8,128)(2,1)S(1)}, bf16[32,2048]{1,0:T(8,128)(2,1)S(1)}, u32[]{:S(2)}, u32[]{:S(2)}) collective-permute-start(bf16[32,2048]{1,0:T(8,128)(2,1)S(1)} %get-tuple-element.40), channel_id=1, source_target_pairs={{0,1},{1,0},{2,3},{3,2},{4,5},{5,4},{6,7},{7,6},{8,9},{9,8},{10,11... | collective-permute-start | bytes 393224 | tf_op jit(solution)/shard_map/ppermute | solution.py:18
  2.9 2.2 %collective-permute-start.1 = (bf16[32,2048]{1,0:T(8,128)(2,1)S(1)}, bf16[32,2048]{1,0:T(8,128)(2,1)S(1)}, u32[]{:S(2)}, u32[]{:S(2)}) collective-permute-start(bf16[32,2048]{1,0:T(8,128)(2,1)S(1)} %get-tuple-element.42), channel_id=1, source_target_pairs={{0,3},{1,2},{2,1},{3,0},{4,7},{5,6},{6,5},{7,4},{8,11},{9,10},{10,... | collective-permute-start | bytes 393224 | tf_op jit(solution)/shard_map/ppermute | solution.py:18
  6.4 4.0 %collective-permute-done.1.second = bf16[32,2048]{1,0:T(8,128)(2,1)S(1)} collective-permute-done((bf16[32,2048]{1,0:T(8,128)(2,1)S(1)}, bf16[32,2048]{1,0:T(8,128)(2,1)S(1)}, u32[]{:S(2)}, u32[]{:S(2)}) %collective-permute-start.1) | collective-permute-done | bytes 131104 | tf_op jit(solution)/shard_map/ppermute | solution.py:18
  10.3 1.5 %collective-permute-done.2.third = bf16[32,2048]{1,0:T(8,128)(2,1)S(1)} collective-permute-done((bf16[32,2048]{1,0:T(8,128)(2,1)S(1)}, bf16[32,2048]{1,0:T(8,128)(2,1)S(1)}, u32[]{:S(2)}, u32[]{:S(2)}) %collective-permute-start.2) | collective-permute-done | bytes 131104 | tf_op jit(solution)/shard_map/ppermute | solution.py:18
  11.9 1.2 %copy-done.3 = bf16[1,2048,256]{2,1,0:T(8,128)(2,1)S(1)} copy-done((bf16[1,2048,256]{2,1,0:T(8,128)(2,1)S(1)}, bf16[1,2048,256]{2,1,0:T(8,128)(2,1)}, u32[]{:S(2)}) %copy-start.3) | copy-done | bytes 1048600
  13.1 0.9 %copy-done.5 = bf16[1,2,256,256]{3,2,1,0:T(8,128)(2,1)S(1)} copy-done((bf16[1,2,256,256]{3,2,1,0:T(8,128)(2,1)S(1)}, bf16[1,2,256,256]{3,2,1,0:T(8,128)(2,1)}, u32[]{:S(2)}) %copy-start.5) | copy-done | bytes 262168
  14.0 1.3 %shard_map.73 = (bf16[128,2048]{1,0:T(8,128)(2,1)S(1)}, f32[288,256]{1,0:T(8,128)S(1)}, f32[288,256]{1,0:T(8,128)S(1)}, f32[128,256]{1,0:T(8,128)S(1)}) custom-call(s32[2]{0:T(128)S(1)} %pad_add_fusion.place_ref, bf16[32,2048]{1,0:T(8,128)(2,1)S(1)} %get-tuple-element.41.own, bf16[32,2048]{1,0:T(8,128)(2,1)S(1)} %collective-permute-done.first, ...), custom_call_target="tpu_custom_call" | custom-call | flops 134217728 | bytes 2097152 | tf_op jit(solution)/shard_map/pallas_call | solution.py:60
  15.8 2.0 %collective-permute-start.4 = (f16[288,256]{1,0:T(8,128)(2,1)S(1)}, f16[288,256]{1,0:T(8,128)(2,1)S(1)}, u32[]{:S(2)}, u32[]{:S(2)}) collective-permute-start(f16[288,256]{1,0:T(8,128)(2,1)S(1)} %convert_element_type.41), channel_id=1, source_target_pairs={{0,3},{1,2},{2,1},{3,0},{4,7},{5,6},{6,5},{7,4},{8,11},{9,10},{10,... | collective-permute-start | bytes 442376 | tf_op jit(solution)/shard_map/ppermute | solution.py:18
  17.8 1.8 %collective-permute-start.5 = (f16[288,256]{1,0:T(8,128)(2,1)S(1)}, f16[288,256]{1,0:T(8,128)(2,1)S(1)}, u32[]{:S(2)}, u32[]{:S(2)}) collective-permute-start(f16[288,256]{1,0:T(8,128)(2,1)S(1)} %convert_element_type.41), channel_id=1, source_target_pairs={{0,2},{1,3},{2,0},{3,1},{4,6},{5,7},{6,4},{7,5},{8,10},{9,11},{10,... | collective-permute-start | bytes 442376 | tf_op jit(solution)/shard_map/ppermute | solution.py:18
  19.6 2.3 %collective-permute-done.3 = f16[288,256]{1,0:T(8,128)(2,1)S(1)} collective-permute-done((f16[288,256]{1,0:T(8,128)(2,1)S(1)}, f16[288,256]{1,0:T(8,128)(2,1)S(1)}, u32[]{:S(2)}, u32[]{:S(2)}) %collective-permute-start.3) | collective-permute-done | bytes 147488 | tf_op jit(solution)/shard_map/ppermute | solution.py:18
  22.0 1.7 %collective-permute-done.4 = f16[288,256]{1,0:T(8,128)(2,1)S(1)} collective-permute-done((f16[288,256]{1,0:T(8,128)(2,1)S(1)}, f16[288,256]{1,0:T(8,128)(2,1)S(1)}, u32[]{:S(2)}, u32[]{:S(2)}) %collective-permute-start.4) | collective-permute-done | bytes 147488 | tf_op jit(solution)/shard_map/ppermute | solution.py:18
  23.6 1.5 %collective-permute-done.5 = f16[288,256]{1,0:T(8,128)(2,1)S(1)} collective-permute-done((f16[288,256]{1,0:T(8,128)(2,1)S(1)}, f16[288,256]{1,0:T(8,128)(2,1)S(1)}, u32[]{:S(2)}, u32[]{:S(2)}) %collective-permute-start.5) | collective-permute-done | bytes 147488 | tf_op jit(solution)/shard_map/ppermute | solution.py:18
  25.4 3.3 %copy-done = bf16[62,256,256]{2,1,0:T(8,128)(2,1)S(1)} copy-done((bf16[62,256,256]{2,1,0:T(8,128)(2,1)S(1)}, bf16[62,256,256]{2,1,0:T(8,128)(2,1)}, u32[]{:S(2)}) %copy-start) | copy-done | bytes 8126488
  28.7 2.1 %copy-done.1 = bf16[31,256,256]{2,1,0:T(8,128)(2,1)S(1)} copy-done((bf16[31,256,256]{2,1,0:T(8,128)(2,1)S(1)}, bf16[31,256,256]{2,1,0:T(8,128)(2,1)}, u32[]{:S(2)}) %copy-start.1) | copy-done | bytes 4063256
  30.8 0.9 %copy-done.6 = bf16[1,2,256,256]{3,2,1,0:T(8,128)(2,1)S(1)} copy-done((bf16[1,2,256,256]{3,2,1,0:T(8,128)(2,1)S(1)}, bf16[1,2,256,256]{3,2,1,0:T(8,128)(2,1)}, u32[]{:S(2)}) %copy-start.6) | copy-done | bytes 262168
  31.8 0.9 %copy-done.7 = bf16[1,2,256,256]{3,2,1,0:T(8,128)(2,1)S(1)} copy-done((bf16[1,2,256,256]{3,2,1,0:T(8,128)(2,1)S(1)}, bf16[1,2,256,256]{3,2,1,0:T(8,128)(2,1)}, u32[]{:S(2)}) %copy-start.7) | copy-done | bytes 262168
  32.7 3.1 %shard_map.75 = (bf16[512,256]{1,0:T(8,128)(2,1)S(1)}, bf16[1024,256]{1,0:T(8,128)(2,1)S(1)}, bf16[1024,256]{1,0:T(8,128)(2,1)S(1)}, bf16[1536,256]{1,0:T(8,128)...) custom-call(s32[2]{0:T(128)S(1)} %pad_add_fusion.place_ref, ...), custom_call_target="tpu_custom_call" | custom-call | flops 1140850688 | bytes 5242880 | tf_op jit(solution)/shard_map/pallas_call | solution.py:60
  36.1 2.0 %collective-permute-start.7 = (f16[144,256]{1,0:T(8,128)(2,1)S(1)}, f16[144,256]{1,0:T(8,128)(2,1)S(1)}, u32[]{:S(2)}, u32[]{:S(2)}) collective-permute-start(f16[144,256]{1,0:T(8,128)(2,1)S(1)} %convert_element_type.44), channel_id=1, source_target_pairs={{0,8},{4,12},{8,0},{12,4},{16,24},{20,28},{24,16},{28,20},{32,40},... | collective-permute-start | bytes 221192 | tf_op jit(solution)/shard_map/ppermute | solution.py:18
  38.1 3.6 %collective-permute-start.8 = (f16[144,256]{1,0:T(8,128)(2,1)S(1)}, f16[144,256]{1,0:T(8,128)(2,1)S(1)}, u32[]{:S(2)}, u32[]{:S(2)}) collective-permute-start(f16[144,256]{1,0:T(8,128)(2,1)S(1)} %convert_element_type.44), channel_id=1, source_target_pairs={{0,16},{4,20},{8,24},{12,28},{16,0},{20,4},{24,8},{28,12},{32,48},... | collective-permute-start | bytes 221192 | tf_op jit(solution)/shard_map/ppermute | solution.py:18
  41.8 4.2 %collective-permute-done.8 = f16[144,256]{1,0:T(8,128)(2,1)S(1)} collective-permute-done((f16[144,256]{1,0:T(8,128)(2,1)S(1)}, f16[144,256]{1,0:T(8,128)(2,1)S(1)}, u32[]{:S(2)}, u32[]{:S(2)}) %collective-permute-start.8) | collective-permute-done | bytes 73760 | tf_op jit(solution)/shard_map/ppermute | solution.py:18
  46.0 1.5 %collective-permute-done.9 = f16[144,256]{1,0:T(8,128)(2,1)S(1)} collective-permute-done((f16[144,256]{1,0:T(8,128)(2,1)S(1)}, f16[144,256]{1,0:T(8,128)(2,1)S(1)}, u32[]{:S(2)}, u32[]{:S(2)}) %collective-permute-start.9) | collective-permute-done | bytes 73760 | tf_op jit(solution)/shard_map/ppermute | solution.py:18
  48.0 1.6 %collective-permute-start.10 = (f16[144,256]{1,0:T(8,128)(2,1)S(1)}, f16[144,256]{1,0:T(8,128)(2,1)S(1)}, u32[]{:S(2)}, u32[]{:S(2)}) collective-permute-start(f16[144,256]{1,0:T(8,128)(2,1)S(1)} %convert_element_type.48), channel_id=1, source_target_pairs={{0,32},{4,36},{8,40},{12,44},{16,48},{20,52},{24,56},{28,60},{32,0... | collective-permute-start | bytes 221192 | tf_op jit(solution)/shard_map/ppermute | solution.py:18
  49.6 2.7 %collective-permute-start.11 = (f16[144,256]{1,0:T(8,128)(2,1)S(1)}, f16[144,256]{1,0:T(8,128)(2,1)S(1)}, u32[]{:S(2)}, u32[]{:S(2)}) collective-permute-start(f16[144,256]{1,0:T(8,128)(2,1)S(1)} %convert_element_type.48), channel_id=1, source_target_pairs={{0,64},{4,68},{8,72},{12,76},{16,80},{20,84},{24,88},{28,92},{32,9... | collective-permute-start | bytes 221192 | tf_op jit(solution)/shard_map/ppermute | solution.py:18
  52.8 4.0 %shard_map.79.near_ref = f32[128,2048]{1,0:T(8,128)S(1)} custom-call(bf16[128,2048]{1,0:T(8,128)(2,1)S(1)} %get-tuple-element.34.cols_ref, bf16[1,2048,2048]{2,1,0:T(8,128)(2,1)S(1)} %copy-done.2), custom_call_target="tpu_custom_call" | custom-call | flops 1073741824 | bytes 9961472 | tf_op jit(solution)/shard_map/pallas_call | solution.py:60
  57.9 1.5 %shard_map.80 = (f32[32,2048]{1,0:T(8,128)S(1)}, bf16[32,2048]{1,0:T(8,128)(2,1)S(1)}, bf16[32,2048]{1,0:T(8,128)(2,1)S(1)}, bf16[32,2048]{1,0:T(8,128)(2,1)S(1)}) custom-call(s32[2]{0:T(128)S(1)} %pad_add_fusion.place_ref, f32[128,256]{1,0:T(8,128)S(1)} %shard_map.77.part_ref, f32[144,256]{1,0:T(8,128)S(1)} %convert_element_type.49.a, ...), custom_call_target="tpu_custom_call" | custom-call | flops 134217728 | bytes 4194304 | tf_op jit(solution)/shard_map/pallas_call | solution.py:60
  60.2 1.9 %collective-permute-start.14 = (bf16[32,2048]{1,0:T(8,128)(2,1)S(1)}, bf16[32,2048]{1,0:T(8,128)(2,1)S(1)}, u32[]{:S(2)}, u32[]{:S(2)}) collective-permute-start(bf16[32,2048]{1,0:T(8,128)(2,1)S(1)} %get-tuple-element.37), channel_id=1, source_target_pairs={{0,3},{1,2},{2,1},{3,0},{4,7},{5,6},{6,5},{7,4},{8,11},{9,10},{10,... | collective-permute-start | bytes 393224 | tf_op jit(solution)/shard_map/ppermute | solution.py:18
  62.0 1.6 %collective-permute-start.15 = (bf16[32,2048]{1,0:T(8,128)(2,1)S(1)}, bf16[32,2048]{1,0:T(8,128)(2,1)S(1)}, u32[]{:S(2)}, u32[]{:S(2)}) collective-permute-start(bf16[32,2048]{1,0:T(8,128)(2,1)S(1)} %get-tuple-element.38), channel_id=1, source_target_pairs={{0,2},{1,3},{2,0},{3,1},{4,6},{5,7},{6,4},{7,5},{8,10},{9,11},{10,... | collective-permute-start | bytes 393224 | tf_op jit(solution)/shard_map/ppermute | solution.py:18
  63.6 1.8 %collective-permute-done.13.first = bf16[32,2048]{1,0:T(8,128)(2,1)S(1)} collective-permute-done((bf16[32,2048]{1,0:T(8,128)(2,1)S(1)}, bf16[32,2048]{1,0:T(8,128)(2,1)S(1)}, u32[]{:S(2)}, u32[]{:S(2)}) %collective-permute-start.13) | collective-permute-done | bytes 131104 | tf_op jit(solution)/shard_map/ppermute | solution.py:18
  65.4 1.7 %collective-permute-done.14.second = bf16[32,2048]{1,0:T(8,128)(2,1)S(1)} collective-permute-done((bf16[32,2048]{1,0:T(8,128)(2,1)S(1)}, bf16[32,2048]{1,0:T(8,128)(2,1)S(1)}, u32[]{:S(2)}, u32[]{:S(2)}) %collective-permute-start.14) | collective-permute-done | bytes 131104 | tf_op jit(solution)/shard_map/ppermute | solution.py:18
  67.2 1.4 %collective-permute-done.15.third = bf16[32,2048]{1,0:T(8,128)(2,1)S(1)} collective-permute-done((bf16[32,2048]{1,0:T(8,128)(2,1)S(1)}, bf16[32,2048]{1,0:T(8,128)(2,1)S(1)}, u32[]{:S(2)}, u32[]{:S(2)}) %collective-permute-start.15) | collective-permute-done | bytes 131104 | tf_op jit(solution)/shard_map/ppermute | solution.py:18
  68.5 1.6 %shard_map.81 = f32[32,8192]{1,0:T(8,128)} custom-call(s32[2]{0:T(128)S(1)} %pad_add_fusion.place_ref, f32[32,2048]{1,0:T(8,128)S(1)} %get-tuple-element.35.own_ref, bf16[32,2048]{1,0:T(8,128)(2,1)S(1)} %collective-permute-done.13.first, bf16[32,2048]{1,0:T(8,128)(2,1)S(1)} %collective-permute-done.14.second, bf16[32,2048]{1,0:T(8,128)(2,1)S(1)} %collective-permute-done.15.third), custom_call_target="tpu_custom_call" | custom-call | bytes 2097152 | tf_op jit(solution)/shard_map/pallas_call | solution.py:60
  (40 shorter events, 5.0 us)
Async XLA Ops:
  1.1 5.2 %collective-permute-start = (bf16[32,2048]{1,0:T(8,128)(2,1)S(1)}, bf16[32,2048]{1,0:T(8,128)(2,1)S(1)}, u32[]{:S(2)}, u32[]{:S(2)}) collective-permute-start(bf16[32,2048]{1,0:T(8,128)(2,1)S(1)} %get-tuple-element.40), channel_id=1, source_target_pairs={{0,1},{1,0},{2,3},{3,2},{4,5},{5,4},{6,7},{7,6},{8,9},{9,8},{10,11... | collective-permute-start | bytes 393224 | tf_op jit(solution)/shard_map/ppermute | solution.py:18
  2.9 7.5 %collective-permute-start.1 = (bf16[32,2048]{1,0:T(8,128)(2,1)S(1)}, bf16[32,2048]{1,0:T(8,128)(2,1)S(1)}, u32[]{:S(2)}, u32[]{:S(2)}) collective-permute-start(bf16[32,2048]{1,0:T(8,128)(2,1)S(1)} %get-tuple-element.42), channel_id=1, source_target_pairs={{0,3},{1,2},{2,1},{3,0},{4,7},{5,6},{6,5},{7,4},{8,11},{9,10},{10,... | collective-permute-start | bytes 393224 | tf_op jit(solution)/shard_map/ppermute | solution.py:18
  5.1 6.8 %collective-permute-start.2 = (bf16[32,2048]{1,0:T(8,128)(2,1)S(1)}, bf16[32,2048]{1,0:T(8,128)(2,1)S(1)}, u32[]{:S(2)}, u32[]{:S(2)}) collective-permute-start(bf16[32,2048]{1,0:T(8,128)(2,1)S(1)} %get-tuple-element.39), channel_id=1, source_target_pairs={{0,2},{1,3},{2,0},{3,1},{4,6},{5,7},{6,4},{7,5},{8,10},{9,11},{10,... | collective-permute-start | bytes 393224 | tf_op jit(solution)/shard_map/ppermute | solution.py:18
  11.9 1.2 %copy-start.3 = (bf16[1,2048,256]{2,1,0:T(8,128)(2,1)S(1)}, bf16[1,2048,256]{2,1,0:T(8,128)(2,1)}, u32[]{:S(2)}) copy-start(bf16[1,2048,256]{2,1,0:T(8,128)(2,1)} %basis.3) | copy-start | bytes 3145732
  13.1 0.9 %copy-start.5 = (bf16[1,2,256,256]{3,2,1,0:T(8,128)(2,1)S(1)}, bf16[1,2,256,256]{3,2,1,0:T(8,128)(2,1)}, u32[]{:S(2)}) copy-start(bf16[1,2,256,256]{3,2,1,0:T(8,128)(2,1)} %refs_0_.1) | copy-start | bytes 786436
  15.3 6.6 %collective-permute-start.3 = (f16[288,256]{1,0:T(8,128)(2,1)S(1)}, f16[288,256]{1,0:T(8,128)(2,1)S(1)}, u32[]{:S(2)}, u32[]{:S(2)}) collective-permute-start(f16[288,256]{1,0:T(8,128)(2,1)S(1)} %convert_element_type.39), channel_id=1, source_target_pairs={{0,1},{1,0},{2,3},{3,2},{4,5},{5,4},{6,7},{7,6},{8,9},{9,8},{10,11... | collective-permute-start | bytes 442376 | tf_op jit(solution)/shard_map/ppermute | solution.py:18
  15.8 7.8 %collective-permute-start.4 = (f16[288,256]{1,0:T(8,128)(2,1)S(1)}, f16[288,256]{1,0:T(8,128)(2,1)S(1)}, u32[]{:S(2)}, u32[]{:S(2)}) collective-permute-start(f16[288,256]{1,0:T(8,128)(2,1)S(1)} %convert_element_type.41), channel_id=1, source_target_pairs={{0,3},{1,2},{2,1},{3,0},{4,7},{5,6},{6,5},{7,4},{8,11},{9,10},{10,... | collective-permute-start | bytes 442376 | tf_op jit(solution)/shard_map/ppermute | solution.py:18
  17.8 7.4 %collective-permute-start.5 = (f16[288,256]{1,0:T(8,128)(2,1)S(1)}, f16[288,256]{1,0:T(8,128)(2,1)S(1)}, u32[]{:S(2)}, u32[]{:S(2)}) collective-permute-start(f16[288,256]{1,0:T(8,128)(2,1)S(1)} %convert_element_type.41), channel_id=1, source_target_pairs={{0,2},{1,3},{2,0},{3,1},{4,6},{5,7},{6,4},{7,5},{8,10},{9,11},{10,... | collective-permute-start | bytes 442376 | tf_op jit(solution)/shard_map/ppermute | solution.py:18
  25.3 10.6 %collective-permute-start.6 = (f32[128,256]{1,0:T(8,128)S(1)}, f32[128,256]{1,0:T(8,128)S(1)}, u32[]{:S(2)}, u32[]{:S(2)}) collective-permute-start(f32[128,256]{1,0:T(8,128)S(1)} %shard_map.74.own), channel_id=1, source_target_pairs={{0,4},{4,0},{8,12},{12,8},{16,20},{20,16},{24,28},{28,24},{32,36},... | collective-permute-start | bytes 393224 | tf_op jit(solution)/shard_map/ppermute | solution.py:18
  25.3 3.3 %copy-start = (bf16[62,256,256]{2,1,0:T(8,128)(2,1)S(1)}, bf16[62,256,256]{2,1,0:T(8,128)(2,1)}, u32[]{:S(2)}) copy-start(bf16[62,256,256]{2,1,0:T(8,128)(2,1)} %refs_13_.1) | copy-start | bytes 24379396
  28.7 2.2 %copy-start.1 = (bf16[31,256,256]{2,1,0:T(8,128)(2,1)S(1)}, bf16[31,256,256]{2,1,0:T(8,128)(2,1)}, u32[]{:S(2)}) copy-start(bf16[31,256,256]{2,1,0:T(8,128)(2,1)} %refs_18_.1) | copy-start | bytes 12189700
  30.8 0.9 %copy-start.6 = (bf16[1,2,256,256]{3,2,1,0:T(8,128)(2,1)S(1)}, bf16[1,2,256,256]{3,2,1,0:T(8,128)(2,1)}, u32[]{:S(2)}) copy-start(bf16[1,2,256,256]{3,2,1,0:T(8,128)(2,1)} %refs_0_.1) | copy-start | bytes 786436
  31.8 0.9 %copy-start.7 = (bf16[1,2,256,256]{3,2,1,0:T(8,128)(2,1)S(1)}, bf16[1,2,256,256]{3,2,1,0:T(8,128)(2,1)}, u32[]{:S(2)}) copy-start(bf16[1,2,256,256]{3,2,1,0:T(8,128)(2,1)} %refs_1_.1) | copy-start | bytes 786436
  32.7 20.1 %copy-start.2 = (bf16[1,2048,2048]{2,1,0:T(8,128)(2,1)S(1)}, bf16[1,2048,2048]{2,1,0:T(8,128)(2,1)}, u32[]{:S(2)}) copy-start(bf16[1,2048,2048]{2,1,0:T(8,128)(2,1)} %block_ref.1) | copy-start | bytes 25165828
  36.1 5.6 %collective-permute-start.7 = (f16[144,256]{1,0:T(8,128)(2,1)S(1)}, f16[144,256]{1,0:T(8,128)(2,1)S(1)}, u32[]{:S(2)}, u32[]{:S(2)}) collective-permute-start(f16[144,256]{1,0:T(8,128)(2,1)S(1)} %convert_element_type.44), channel_id=1, source_target_pairs={{0,8},{4,12},{8,0},{12,4},{16,24},{20,28},{24,16},{28,20},{32,40},... | collective-permute-start | bytes 221192 | tf_op jit(solution)/shard_map/ppermute | solution.py:18
  38.1 7.9 %collective-permute-start.8 = (f16[144,256]{1,0:T(8,128)(2,1)S(1)}, f16[144,256]{1,0:T(8,128)(2,1)S(1)}, u32[]{:S(2)}, u32[]{:S(2)}) collective-permute-start(f16[144,256]{1,0:T(8,128)(2,1)S(1)} %convert_element_type.44), channel_id=1, source_target_pairs={{0,16},{4,20},{8,24},{12,28},{16,0},{20,4},{24,8},{28,12},{32,48},... | collective-permute-start | bytes 221192 | tf_op jit(solution)/shard_map/ppermute | solution.py:18
  41.7 5.8 %collective-permute-start.9 = (f16[144,256]{1,0:T(8,128)(2,1)S(1)}, f16[144,256]{1,0:T(8,128)(2,1)S(1)}, u32[]{:S(2)}, u32[]{:S(2)}) collective-permute-start(f16[144,256]{1,0:T(8,128)(2,1)S(1)} %convert_element_type.44), channel_id=1, source_target_pairs={{0,24},{4,28},{8,16},{12,20},{16,8},{20,12},{24,0},{28,4},{32,56},... | collective-permute-start | bytes 221192 | tf_op jit(solution)/shard_map/ppermute | solution.py:18
  41.8 16.1 %copy-start.4 = (bf16[1,2048,256]{2,1,0:T(8,128)(2,1)S(1)}, bf16[1,2048,256]{2,1,0:T(8,128)(2,1)}, u32[]{:S(2)}) copy-start(bf16[1,2048,256]{2,1,0:T(8,128)(2,1)} %basis.3) | copy-start | bytes 3145732
  48.0 9.3 %collective-permute-start.10 = (f16[144,256]{1,0:T(8,128)(2,1)S(1)}, f16[144,256]{1,0:T(8,128)(2,1)S(1)}, u32[]{:S(2)}, u32[]{:S(2)}) collective-permute-start(f16[144,256]{1,0:T(8,128)(2,1)S(1)} %convert_element_type.48), channel_id=1, source_target_pairs={{0,32},{4,36},{8,40},{12,44},{16,48},{20,52},{24,56},{28,60},{32,0... | collective-permute-start | bytes 221192 | tf_op jit(solution)/shard_map/ppermute | solution.py:18
  49.6 7.8 %collective-permute-start.11 = (f16[144,256]{1,0:T(8,128)(2,1)S(1)}, f16[144,256]{1,0:T(8,128)(2,1)S(1)}, u32[]{:S(2)}, u32[]{:S(2)}) collective-permute-start(f16[144,256]{1,0:T(8,128)(2,1)S(1)} %convert_element_type.48), channel_id=1, source_target_pairs={{0,64},{4,68},{8,72},{12,76},{16,80},{20,84},{24,88},{28,92},{32,9... | collective-permute-start | bytes 221192 | tf_op jit(solution)/shard_map/ppermute | solution.py:18
  52.3 5.6 %collective-permute-start.12 = (f16[144,256]{1,0:T(8,128)(2,1)S(1)}, f16[144,256]{1,0:T(8,128)(2,1)S(1)}, u32[]{:S(2)}, u32[]{:S(2)}) collective-permute-start(f16[144,256]{1,0:T(8,128)(2,1)S(1)} %convert_element_type.48), channel_id=1, source_target_pairs={{0,96},{4,100},{8,104},{12,108},{16,112},{20,116},{24,120},{28,124... | collective-permute-start | bytes 221192 | tf_op jit(solution)/shard_map/ppermute | solution.py:18
  59.4 6.0 %collective-permute-start.13 = (bf16[32,2048]{1,0:T(8,128)(2,1)S(1)}, bf16[32,2048]{1,0:T(8,128)(2,1)S(1)}, u32[]{:S(2)}, u32[]{:S(2)}) collective-permute-start(bf16[32,2048]{1,0:T(8,128)(2,1)S(1)} %get-tuple-element.36), channel_id=1, source_target_pairs={{0,1},{1,0},{2,3},{3,2},{4,5},{5,4},{6,7},{7,6},{8,9},{9,8},{10,11... | collective-permute-start | bytes 393224 | tf_op jit(solution)/shard_map/ppermute | solution.py:18
  60.2 7.0 %collective-permute-start.14 = (bf16[32,2048]{1,0:T(8,128)(2,1)S(1)}, bf16[32,2048]{1,0:T(8,128)(2,1)S(1)}, u32[]{:S(2)}, u32[]{:S(2)}) collective-permute-start(bf16[32,2048]{1,0:T(8,128)(2,1)S(1)} %get-tuple-element.37), channel_id=1, source_target_pairs={{0,3},{1,2},{2,1},{3,0},{4,7},{5,6},{6,5},{7,4},{8,11},{9,10},{10,... | collective-permute-start | bytes 393224 | tf_op jit(solution)/shard_map/ppermute | solution.py:18
  62.0 6.5 %collective-permute-start.15 = (bf16[32,2048]{1,0:T(8,128)(2,1)S(1)}, bf16[32,2048]{1,0:T(8,128)(2,1)S(1)}, u32[]{:S(2)}, u32[]{:S(2)}) collective-permute-start(bf16[32,2048]{1,0:T(8,128)(2,1)S(1)} %get-tuple-element.38), channel_id=1, source_target_pairs={{0,2},{1,3},{2,0},{3,1},{4,6},{5,7},{6,4},{7,5},{8,10},{9,11},{10,... | collective-permute-start | bytes 393224 | tf_op jit(solution)/shard_map/ppermute | solution.py:18

commit v2 on v0

v2 whole, which is shorter than its diff:
```python
import jax
import jax.numpy as jnp
from jax import lax
from jax.experimental import pallas as pl
from jax.experimental.pallas import tpu as pltpu
from jax.sharding import PartitionSpec as P

F32 = jnp.float32
BF16 = jnp.bfloat16
F16 = jnp.float16
VMEM = pl.BlockSpec(memory_space=pltpu.VMEM)
HBM = pl.BlockSpec(memory_space=pltpu.HBM)
LIMIT = 32 * 2**20
EXTRA = 16


def swap(value, axis, mask):
    pairs = [(source, source ^ mask) for source in range(lax.axis_size(axis))]
    return lax.ppermute(value, axis, pairs)


def split(value):
    high = value.astype(BF16)
    return high, (value - high.astype(F32)).astype(BF16)


def dot(a, b):
    return jnp.dot(a, b, preferred_element_type=F32)


def dot_narrow(value, matrix):
    high, low = split(value)
    return dot(high, matrix) + dot(low, matrix)


def dot_wide(value, high_matrix, low_matrix):
    high, low = split(value)
    return dot(high, high_matrix) + (dot(low, high_matrix) + dot(high, low_matrix))


def encode(value):
    largest = jnp.max(jnp.abs(value), axis=0, keepdims=True)
    power = jnp.ceil(jnp.log2(jnp.maximum(largest, 1e-30))) - 14.0
    scaled = value * jnp.exp2(-power)
    return scaled, jnp.broadcast_to(power, (EXTRA, value.shape[1]))


def put_encoded(ref, value):
    rows = value.shape[0]
    ref[:rows, :], ref[rows:, :] = encode(value)


def decode(ref):
    rows = ref.shape[0] - EXTRA
    return ref[:rows, :] * jnp.exp2(ref[rows : rows + 1, :])


def call(body, outs, operands, flops=0, moved=0, **more):
    return pl.pallas_call(
        body,
        out_shape=outs,
        compiler_params=pltpu.CompilerParams(vmem_limit_bytes=LIMIT),
        cost_estimate=pl.CostEstimate(flops=flops, bytes_accessed=moved, transcendentals=0),
        **more,
    )(*operands)


def shape(*dims, dtype=F32):
    return jax.ShapeDtypeStruct(dims, dtype)


def aligned(index, size):
    return pl.ds(pl.multiple_of(index * size, size), size)


def cut(vectors, leaf, masks):
    part = vectors.shape[0]

    def body(source, *rest):
        blocks, sems = rest[:-1], rest[-1]
        position = lax.axis_index("rhs")
        copies = [
            pltpu.make_async_copy(source.at[:, aligned(position ^ mask, leaf)], block, sems.at[slot])
            for slot, (mask, block) in enumerate(zip(masks, blocks))
        ]
        for copy in copies:
            copy.start()
        for copy in copies:
            copy.wait()

    count = len(masks)
    return call(
        body,
        [shape(part, leaf, dtype=BF16)] * count,
        (vectors,),
        moved=4 * count * part * leaf,
        in_specs=[HBM],
        out_specs=[VMEM] * count,
        scratch_shapes=[pltpu.SemaphoreType.DMA((count,))],
    )


def oriented(coupling, is_right):
    wide = coupling.astype(F32)
    return jnp.where(is_right == 1, wide, wide.T).astype(BF16)


def transposed(matrix):
    return matrix.astype(F32).T.astype(BF16)


def times(matrix, parts):
    return dot(matrix, parts[0]) + dot(matrix, parts[1])


PICKS = [(0, 0), (0, 1), (1, 0), (1, 1), (1, 2), (1, 3), (2, 0), (2, 1), (3, 0), (3, 2), (3, 3)]
COUPLED = 5


def compose(leaf_basis, lower_transfer, lower_coupling, upper_transfer, upper_coupling):
    leaf, rank = leaf_basis.shape[1:]
    n_up = len(PICKS)
    n_all = n_up + COUPLED

    def body(basis_hbm, low_t_hbm, low_b_hbm, up_t_hbm, up_b_hbm, *rest):
        basis, lower_t, pair, up_high, up_low, acc_high, acc_low, top_high, top_low = rest[:9]
        lower_b, uppers, couplings, sems = rest[9:]
        rhs_pos = lax.axis_index("rhs")
        node = lax.axis_index("leaf") + lax.axis_size("leaf")
        copies = []
        for slot, (height, mask) in enumerate(PICKS):
            copies.append((up_t_hbm.at[((node >> height) ^ mask) - 2], uppers.at[slot]))
        for height in range(COUPLED):
            copies.append((up_b_hbm.at[(node >> (height + 1)) - 1], couplings.at[height]))
        copies += [(low_t_hbm.at[0], lower_t), (low_b_hbm.at[0], lower_b), (basis_hbm.at[0], basis)]
        copies = [pltpu.make_async_copy(*pair_, sems.at[i]) for i, pair_ in enumerate(copies)]
        for copy in copies:
            copy.start()
        for copy in copies:
            copy.wait()

        def put(high_ref, low_ref, slot, value):
            high, low = split(value)
            high_ref[slot * rank : (slot + 1) * rank, :] = high
            low_ref[slot * rank : (slot + 1) * rank, :] = low

        own2, sib2 = uppers[0], uppers[1]
        level3 = [uppers[slot] for slot in range(2, 6)]
        own4, sib4, own5, third5, fourth5 = [uppers[slot] for slot in range(6, 11)]
        pair[:rank, :] = own2
        pair[rank:, :] = sib2
        for slot, matrix in enumerate(level3):
            put(up_high, up_low, slot, dot(matrix, own4 if slot < 2 else sib4))
        put(acc_high, acc_low, 0, oriented(lower_b[0], rhs_pos & 1).astype(F32))
        down = split(transposed(lower_t[0]).astype(F32))
        put(acc_high, acc_low, 1, times(oriented(lower_b[1], rhs_pos >> 1 & 1), down))
        down = split(times(transposed(lower_t[1]), down))
        put(acc_high, acc_low, 2, times(oriented(couplings[0], node & 1), down))
        down = split(times(transposed(own2), down))
        put(acc_high, acc_low, 3, times(oriented(couplings[1], node >> 1 & 1), down))
        down = split(times(transposed(level3[0]), down))
        across = split(times(oriented(couplings[2], node >> 2 & 1), down))
        put(acc_high, acc_low, 4, times(level3[2], across))
        put(acc_high, acc_low, 5, times(level3[3], across))
        down = split(times(transposed(own4), down))
        put(top_high, top_low, 0, times(oriented(couplings[3], node >> 3 & 1), down))
        down = split(times(transposed(own5), down))
        across = split(times(oriented(couplings[4], node >> 4 & 1), down))
        put(top_high, top_low, 1, times(third5, across))
        put(top_high, top_low, 2, times(fourth5, across))

    stacked = [shape(n * rank, rank, dtype=BF16) for n in (2, 4, 4, 6, 6, 3, 3)]
    return call(
        body,
        [shape(leaf, rank, dtype=BF16), shape(2, rank, rank, dtype=BF16)] + stacked,
        (leaf_basis, lower_transfer, lower_coupling, upper_transfer, upper_coupling),
        flops=34 * 2 * rank**3,
        moved=2**22,
        in_specs=[HBM] * 5,
        out_specs=[VMEM] * 9,
        scratch_shapes=[
            pltpu.VMEM((2, rank, rank), BF16),
            pltpu.VMEM((n_up, rank, rank), BF16),
            pltpu.VMEM((COUPLED, rank, rank), BF16),
            pltpu.SemaphoreType.DMA((n_all + 3,)),
        ],
    )


def shards(
    vectors, near_blocks, leaf_basis, lower_transfer, lower_coupling, upper_transfer, upper_coupling
):
    part = vectors.shape[0]
    leaf, rank = leaf_basis.shape[1:]
    total = part * lax.axis_size("rhs")
    masks = (0, 1, 3, 2)

    vectors = pltpu.with_memory_space_constraint(vectors, pltpu.HBM)
    blocks = cut(vectors, leaf, masks)
    came = [swap(block, "rhs", mask) for block, mask in zip(blocks[1:], masks[1:])]
    leaf_basis, lower_transfer, lower_coupling, upper_transfer, upper_coupling = [
        pltpu.with_memory_space_constraint(array, pltpu.HBM)
        for array in (leaf_basis, lower_transfer, lower_coupling, upper_transfer, upper_coupling)
    ]
    basis, low, pair, up_high, up_low, acc_high, acc_low, top_high, top_low = compose(
        leaf_basis, lower_transfer, lower_coupling, upper_transfer, upper_coupling
    )
    message = shape(total + EXTRA, rank)

    def leaf_body(own, first, second, third, basis_ref, transfer, cols, up_msg, own_msg, mid_msg, kept):
        position = lax.axis_index("rhs")
        for slot, ref in enumerate((own, first, second, third)):
            cols[slot * part : (slot + 1) * part, :] = ref[...]
        coeffs = dot(cols[...], basis_ref[...])
        middle = dot_narrow(coeffs, transfer[0])
        upward = dot_narrow(middle, transfer[1])
        for msg, value in ((up_msg, upward), (own_msg, coeffs), (mid_msg, middle)):
            scaled, power = encode(value)
            for slot, mask in enumerate(masks):
                msg[aligned(position ^ mask, part), :] = scaled[slot * part : (slot + 1) * part, :]
            msg[total:, :] = power
        for slot, mask in enumerate(masks):
            kept[aligned(position ^ mask, part), :] = upward[slot * part : (slot + 1) * part, :]

    cols, up_msg, own_msg, mid_msg, upward = call(
        leaf_body,
        (shape(total, leaf, dtype=BF16), message, message, message, shape(total, rank)),
        (blocks[0], *came, basis, low),
        flops=2 * total * leaf * rank,
        moved=2**21,
        in_specs=[VMEM] * 6,
        out_specs=[VMEM] * 5,
    )
    up_msg, own_msg, mid_msg = [msg.astype(F16) for msg in (up_msg, own_msg, mid_msg)]
    ups = [swap(up_msg, "rhs", mask).astype(F32) for mask in masks[1:]]
    def group_body(own, a, b, c, out):
        out[...] = own[...] + decode(a) + (decode(b) + decode(c))

    group = call(
        group_body,
        shape(total, rank),
        (upward, *ups),
        moved=2**20,
        in_specs=[VMEM] * 4,
        out_specs=VMEM,
    )
    group_sib = swap(group, "leaf", 1)

    def chip_body(own, sibling, matrices, out, kept):
        value = dot_narrow(own[...], matrices[:rank, :]) + dot_narrow(sibling[...], matrices[rank:, :])
        kept[...] = value
        put_encoded(out, value)

    chip_msg, chip = call(
        chip_body,
        (message, shape(total, rank)),
        (group, group_sib, pair),
        flops=8 * total * rank * rank,
        moved=2**20,
        in_specs=[VMEM] * 3,
        out_specs=[VMEM] * 2,
    )
    chip_msg = chip_msg.astype(F16)
    chips = [swap(chip_msg, "leaf", 2 * mask) for mask in (1, 3, 2)]
    own_msg, mid_msg, chips[0] = lax.optimization_barrier((own_msg, mid_msg, chips[0]))
    chips = [chips[slot].astype(F32) for slot in (0, 2, 1)]
    mids = [swap(own_msg, "rhs", 1).astype(F32)] + [swap(mid_msg, "rhs", mask).astype(F32) for mask in (3, 2)]


    def line_body(own, a, b, c, high, low, out):
        value = jnp.concatenate([own[...]] + [decode(ref) for ref in (a, b, c)], axis=1)
        put_encoded(out, dot_wide(value, high[...], low[...]))

    line_msg = call(
        line_body,
        message,
        (chip, *chips, up_high, up_low),
        flops=24 * total * rank * rank,
        moved=2**21,
        in_specs=[VMEM] * 6,
        out_specs=VMEM,
    )
    line_msg, cols = lax.optimization_barrier((line_msg.astype(F16), cols))
    lines = [swap(line_msg, "leaf", 8 * mask).astype(F32) for mask in (1, 2, 3)]

    steps = 8

    def near_body(cols_ref, block_ref, y1, y3, y2, core, z1, z2, z3, high, low, out_ref, part_out):
        out_ref[...] = lax.dot_general(
            cols_ref[...], block_ref[0], (((1,), (1,)), ((), ())), preferred_element_type=F32
        )

        @pl.when(pl.program_id(0) == 0)
        def _():
            value = jnp.concatenate(
                [decode(y1), decode(y3) + decode(y2), core[...]] + [decode(ref) for ref in (z1, z2, z3)],
                axis=1,
            )
            part_out[...] = dot_wide(value, high[...], low[...])

    near, partial = call(
        near_body,
        (shape(total, leaf), shape(total, rank)),
        (cols, near_blocks, *mids, group_sib, *chips, acc_high, acc_low),
        flops=2 * total * leaf * leaf,
        moved=2 * leaf * leaf + 6 * total * leaf,
        grid=(steps,),
        in_specs=[VMEM, pl.BlockSpec((1, leaf // steps, leaf), lambda i: (0, i, 0))] + [VMEM] * 9,
        out_specs=[pl.BlockSpec((total, leaf // steps), lambda i: (0, i)), VMEM],
    )

    def last_body(part_ref, a, b, c, high, low, basis_ref, near_ref, own, first, second, third, inner):
        position = lax.axis_index("rhs")
        value = jnp.concatenate([decode(ref) for ref in (a, b, c)], axis=1)
        inner[...] = part_ref[...] + dot_wide(value, high[...], low[...])
        coeffs = jnp.concatenate([inner[aligned(position ^ mask, part), :] for mask in masks], axis=0)
        far = lax.dot_general(
            coeffs.astype(BF16), basis_ref[...], (((1,), (1,)), ((), ())), preferred_element_type=F32
        )
        for slot, ref in enumerate((own, first, second, third)):
            rows = slice(slot * part, (slot + 1) * part)
            ref[...] = (near_ref[rows, :] + far[rows, :]).astype(ref.dtype)

    sent = shape(part, leaf, dtype=BF16)
    own, *blocks = call(
        last_body,
        (shape(part, leaf), sent, sent, sent),
        (partial, *lines, top_high, top_low, basis, near),
        flops=2 * total * leaf * rank,
        moved=2**22,
        in_specs=[VMEM] * 8,
        out_specs=[VMEM] * 4,
        scratch_shapes=[pltpu.VMEM((total, rank), F32)],
    )
    blocks = [swap(block, "rhs", mask) for block, mask in zip(blocks, masks[1:])]

    def join_body(count, slots, *refs):
        blocks, out, wide, sems = refs[:count], refs[-3], refs[-2], refs[-1]
        position = lax.axis_index("rhs")
        copies = []
        for i, (block, slot) in enumerate(zip(blocks, slots)):
            wide[i] = block[...].astype(F32)
            target = out.at[:, aligned(position ^ masks[slot], leaf)]
            copies.append(pltpu.make_async_copy(wide.at[i], target, sems.at[i]))
            copies[-1].start()
        for copy in copies:
            copy.wait()

    def join(blocks, slots, under=None):
        count = len(blocks)

        def body(*refs):
            join_body(count, slots, *refs)

        return call(
            body,
            shape(part, 4 * leaf),
            (*blocks,) if under is None else (*blocks, under),
            moved=6 * part * leaf * count,
            in_specs=[VMEM] * count + ([] if under is None else [HBM]),
            out_specs=HBM,
            scratch_shapes=[pltpu.VMEM((count, part, leaf), F32), pltpu.SemaphoreType.DMA((count,))],
            input_output_aliases={} if under is None else {count: 0},
        )

    most = join((own, blocks[0], blocks[1]), (0, 1, 2))
    return join((blocks[2],), (3,), most)


def solution(mesh):
    in_specs = (
        P("rhs", "leaf"),
        P(("leaf", "rhs"), None, None),
        P(("leaf", "rhs"), None, None),
        P(("leaf", "rhs"), None, None, None),
        P(("leaf", "rhs"), None, None, None),
        P(),
        P(),
    )
    out_specs = P("rhs", "leaf")
    return jax.shard_map(shards, mesh=mesh, in_specs=in_specs, out_specs=out_specs, check_vma=False)
```

time: 108 us -> 60.4 us (0.56)
  blocking collectives: 30.7 us -> 0 us
  matrix products: 28 us -> 0 us
  Pallas kernels: 0 us -> 14.9 us
  starting transfers between devices: 19.9 us -> 26.9 us
  local copies, waits for them, and re-layouts: 4.62 us -> 0.01 us
  other arithmetic: 3.35 us -> 0.2 us
  waiting for transfers between devices: 20.7 us -> 18 us
    all_to_all x2 -> x0, blocking collectives: 30.7 us -> none  [the longest x1 16.9 us: shards(): lax.all_to_all(near + far, 'rhs', split_axis=0, concat_axis=1, tiled=True)]
    dot_general x23 -> x0, matrix products: 28 us -> none  [the longest x20 21 us: product_full(): jnp.dot(left_side, right_side, precision=lax.Precision.HIGHEST, preferred...]
    pallas_call x0 -> x10, Pallas kernels: none -> 14.9 us  [call(): pl.pallas_call(body, out_shape=outs, compiler_params=pltpu.CompilerParams...]
    ppermute x13 -> x19, starting transfers between devices: 19.9 us -> 26.9 us  [swap(): return lax.ppermute(value, axis, pairs)]
    ppermute x13 -> x19, waiting for transfers between devices: 20.7 us -> 18 us  [swap(): return lax.ppermute(value, axis, pairs)]
    convert_element_type x7 -> x0, local copies, waits for them, and re-layouts: 2.33 us -> none  [the longest x5 1.35 us: shards(): coupling = pick_row(upper_coupling, (node_id >> 1) - 1).astype(jnp.float32)]
    all_to_all x2 -> x0, local copies, waits for them, and re-layouts: 2.23 us -> none  [the longest x1 1.16 us: shards(): lax.all_to_all(vectors, 'rhs', split_axis=1, concat_axis=0, tiled=True)]
    convert_element_type x2 -> x17, other arithmetic: 2.28 us -> 0.2 us  [the longest x3 0.04 us: shards(): lines = [swap(line_msg, 'leaf', 8 * mask).astype(F32) for mask in (1, 2, 3)]]
  transfers between devices with their start and end apart: 13 -> 19, of which waited for: 7 -> 12; matrix products, arithmetic and copies ran while one was open for 23% -> 0% of each run, Pallas kernels for 0% -> 10%
where the time goes in v2:
time: 60.4 us; the launch traced here: 60.3 us
  starting transfers between devices  26.9 us (45%)
  waiting for transfers between devices  18 us (30%)
  Pallas kernels  14.9 us (25%)
    ppermute x19, starting transfers between devices, swap(): return lax.ppermute(value, axis, pairs)  26.9 us
    ppermute x19, waiting for transfers between devices, swap(): return lax.ppermute(value, axis, pairs)  18 us
    pallas_call x10, Pallas kernels, call(): pl.pallas_call(body, out_shape=outs, compiler_params=pltpu.CompilerParams...  14.9 us
  transfers between devices with their start and end apart: 19, of which 12 were waited for; matrix products, arithmetic and copies ran while one was open for 0% of the time, Pallas kernels for 10%

profile of v2, /device:TPU:0, one launch (start us, length us, event | category | flops | bytes accessed | tf_op | source)
XLA Modules:
  0.0 60.3 jit_solution(13544147774166604531)
XLA Ops:
  0.0 1.1 %shard_map.73 = (bf16[32,2048]{1,0:T(8,128)(2,1)S(1)}, bf16[32,2048]{1,0:T(8,128)(2,1)S(1)}, bf16[32,2048]{1,0:T(8,128)(2,1)S(1)}, bf16[32,2048]{1,0:T(8,128)(2,1)S(1)}) custom-call(bf16[32,8192]{1,0:T(8,128)(2,1)} %source.1), custom_call_target="tpu_custom_call" | custom-call | bytes 1048576 | tf_op jit(solution)/shard_map/pallas_call | solution.py:59
  1.1 1.7 %collective-permute-start = (bf16[32,2048]{1,0:T(8,128)(2,1)S(1)}, bf16[32,2048]{1,0:T(8,128)(2,1)S(1)}, u32[]{:S(2)}, u32[]{:S(2)}) collective-permute-start(bf16[32,2048]{1,0:T(8,128)(2,1)S(1)} %get-tuple-element.37), channel_id=1, source_target_pairs={{0,1},{1,0},{2,3},{3,2},{4,5},{5,4},{6,7},{7,6},{8,9},{9,8},{10,11... | collective-permute-start | bytes 393224 | tf_op jit(solution)/shard_map/ppermute | solution.py:19
  2.9 2.2 %collective-permute-start.1 = (bf16[32,2048]{1,0:T(8,128)(2,1)S(1)}, bf16[32,2048]{1,0:T(8,128)(2,1)S(1)}, u32[]{:S(2)}, u32[]{:S(2)}) collective-permute-start(bf16[32,2048]{1,0:T(8,128)(2,1)S(1)} %get-tuple-element.38), channel_id=1, source_target_pairs={{0,3},{1,2},{2,1},{3,0},{4,7},{5,6},{6,5},{7,4},{8,11},{9,10},{10,... | collective-permute-start | bytes 393224 | tf_op jit(solution)/shard_map/ppermute | solution.py:19
  5.1 0.7 %collective-permute-start.2 = (bf16[32,2048]{1,0:T(8,128)(2,1)S(1)}, bf16[32,2048]{1,0:T(8,128)(2,1)S(1)}, u32[]{:S(2)}, u32[]{:S(2)}) collective-permute-start(bf16[32,2048]{1,0:T(8,128)(2,1)S(1)} %get-tuple-element.39), channel_id=1, source_target_pairs={{0,2},{1,3},{2,0},{3,1},{4,6},{5,7},{6,4},{7,5},{8,10},{9,11},{10,... | collective-permute-start | bytes 393224 | tf_op jit(solution)/shard_map/ppermute | solution.py:19
  5.8 5.2 %shard_map.74 = (bf16[2048,256]{1,0:T(8,128)(2,1)S(1)}, bf16[2,256,256]{2,1,0:T(8,128)(2,1)S(1)}, bf16[512,256]{1,0:T(8,128)(2,1)S(1)}, bf16[1024,256]{1,0:T(8,1...) custom-call(bf16[1,2048,256]{2,1,0:T(8,128)(2,1)} %basis_hbm.1, ...), custom_call_target="tpu_custom_call" | custom-call | flops 1140850688 | bytes 4194304 | tf_op jit(solution)/shard_map/pallas_call | solution.py:59
  11.0 0.9 %collective-permute-done.2.third = bf16[32,2048]{1,0:T(8,128)(2,1)S(1)} collective-permute-done((bf16[32,2048]{1,0:T(8,128)(2,1)S(1)}, bf16[32,2048]{1,0:T(8,128)(2,1)S(1)}, u32[]{:S(2)}, u32[]{:S(2)}) %collective-permute-start.2) | collective-permute-done | bytes 131104 | tf_op jit(solution)/shard_map/ppermute | solution.py:19
  11.9 0.7 %shard_map.75 = (bf16[128,2048]{1,0:T(8,128)(2,1)S(1)}, f32[144,256]{1,0:T(8,128)S(1)}, f32[144,256]{1,0:T(8,128)S(1)}, f32[144,256]{1,0:T(8,128)S(1)}, f32[128,256]{1,0:T(8,128)S(1)}) custom-call(bf16[32,2048]{1,0:T(8,128)(2,1)S(1)} %get-tuple-element.36.own, bf16[32,2048]{1,0:T(8,128)(2,1)S(1)} %collective-permute-done.first, ...), custom_call_target="tpu_custom_call" | custom-call | flops 134217728 | bytes 2097152 | tf_op jit(solution)/shard_map/pallas_call | solution.py:59
  12.6 1.8 %collective-permute-start.5 = (f16[144,256]{1,0:T(8,128)(2,1)S(1)}, f16[144,256]{1,0:T(8,128)(2,1)S(1)}, u32[]{:S(2)}, u32[]{:S(2)}) collective-permute-start(f16[144,256]{1,0:T(8,128)(2,1)S(1)} %convert_element_type.51), channel_id=1, source_target_pairs={{0,2},{1,3},{2,0},{3,1},{4,6},{5,7},{6,4},{7,5},{8,10},{9,11},{10,... | collective-permute-start | bytes 221192 | tf_op jit(solution)/shard_map/ppermute | solution.py:19
  14.4 1.5 %collective-permute-start.4 = (f16[144,256]{1,0:T(8,128)(2,1)S(1)}, f16[144,256]{1,0:T(8,128)(2,1)S(1)}, u32[]{:S(2)}, u32[]{:S(2)}) collective-permute-start(f16[144,256]{1,0:T(8,128)(2,1)S(1)} %convert_element_type.51), channel_id=1, source_target_pairs={{0,3},{1,2},{2,1},{3,0},{4,7},{5,6},{6,5},{7,4},{8,11},{9,10},{10,... | collective-permute-start | bytes 221192 | tf_op jit(solution)/shard_map/ppermute | solution.py:19
  16.2 2.8 %collective-permute-done.5 = f16[144,256]{1,0:T(8,128)(2,1)S(1)} collective-permute-done((f16[144,256]{1,0:T(8,128)(2,1)S(1)}, f16[144,256]{1,0:T(8,128)(2,1)S(1)}, u32[]{:S(2)}, u32[]{:S(2)}) %collective-permute-start.5) | collective-permute-done | bytes 73760 | tf_op jit(solution)/shard_map/ppermute | solution.py:19
  19.0 0.9 %collective-permute-done.4 = f16[144,256]{1,0:T(8,128)(2,1)S(1)} collective-permute-done((f16[144,256]{1,0:T(8,128)(2,1)S(1)}, f16[144,256]{1,0:T(8,128)(2,1)S(1)}, u32[]{:S(2)}, u32[]{:S(2)}) %collective-permute-start.4) | collective-permute-done | bytes 73760 | tf_op jit(solution)/shard_map/ppermute | solution.py:19
  20.4 1.3 %collective-permute-done.6.sibling.core = f32[128,256]{1,0:T(8,128)S(1)} collective-permute-done((f32[128,256]{1,0:T(8,128)S(1)}, f32[128,256]{1,0:T(8,128)S(1)}, u32[]{:S(2)}, u32[]{:S(2)}) %collective-permute-start.6) | collective-permute-done | bytes 131104 | tf_op jit(solution)/shard_map/ppermute | solution.py:19
  22.1 2.0 %collective-permute-start.7 = (f16[144,256]{1,0:T(8,128)(2,1)S(1)}, f16[144,256]{1,0:T(8,128)(2,1)S(1)}, u32[]{:S(2)}, u32[]{:S(2)}) collective-permute-start(f16[144,256]{1,0:T(8,128)(2,1)S(1)} %convert_element_type.57), channel_id=1, source_target_pairs={{0,8},{4,12},{8,0},{12,4},{16,24},{20,28},{24,16},{28,20},{32,40},... | collective-permute-start | bytes 221192 | tf_op jit(solution)/shard_map/ppermute | solution.py:19
  24.0 2.5 %collective-permute-start.9 = (f16[144,256]{1,0:T(8,128)(2,1)S(1)}, f16[144,256]{1,0:T(8,128)(2,1)S(1)}, u32[]{:S(2)}, u32[]{:S(2)}) collective-permute-start(f16[144,256]{1,0:T(8,128)(2,1)S(1)} %convert_element_type.57), channel_id=1, source_target_pairs={{0,24},{4,28},{8,16},{12,20},{16,8},{20,12},{24,0},{28,4},{32,56},... | collective-permute-start | bytes 221192 | tf_op jit(solution)/shard_map/ppermute | solution.py:19
  26.6 1.1 %collective-permute-start.8 = (f16[144,256]{1,0:T(8,128)(2,1)S(1)}, f16[144,256]{1,0:T(8,128)(2,1)S(1)}, u32[]{:S(2)}, u32[]{:S(2)}) collective-permute-start(f16[144,256]{1,0:T(8,128)(2,1)S(1)} %convert_element_type.57), channel_id=1, source_target_pairs={{0,16},{4,20},{8,24},{12,28},{16,0},{20,4},{24,8},{28,12},{32,48},... | collective-permute-start | bytes 221192 | tf_op jit(solution)/shard_map/ppermute | solution.py:19
  27.7 2.1 %collective-permute-done.9 = f16[144,256]{1,0:T(8,128)(2,1)S(1)} collective-permute-done((f16[144,256]{1,0:T(8,128)(2,1)S(1)}, f16[144,256]{1,0:T(8,128)(2,1)S(1)}, u32[]{:S(2)}, u32[]{:S(2)}) %collective-permute-start.9) | collective-permute-done | bytes 73760 | tf_op jit(solution)/shard_map/ppermute | solution.py:19
  29.8 2.7 %collective-permute-done.8 = f16[144,256]{1,0:T(8,128)(2,1)S(1)} collective-permute-done((f16[144,256]{1,0:T(8,128)(2,1)S(1)}, f16[144,256]{1,0:T(8,128)(2,1)S(1)}, u32[]{:S(2)}, u32[]{:S(2)}) %collective-permute-start.8) | collective-permute-done | bytes 73760 | tf_op jit(solution)/shard_map/ppermute | solution.py:19
  32.9 2.8 %collective-permute-start.15 = (f16[144,256]{1,0:T(8,128)(2,1)S(1)}, f16[144,256]{1,0:T(8,128)(2,1)S(1)}, u32[]{:S(2)}, u32[]{:S(2)}) collective-permute-start(f16[144,256]{1,0:T(8,128)(2,1)S(1)} %convert_element_type.61), channel_id=1, source_target_pairs={{0,96},{4,100},{8,104},{12,108},{16,112},{20,116},{24,120},{28,124... | collective-permute-start | bytes 221192 | tf_op jit(solution)/shard_map/ppermute | solution.py:19
  35.7 0.8 %collective-permute-start.14 = (f16[144,256]{1,0:T(8,128)(2,1)S(1)}, f16[144,256]{1,0:T(8,128)(2,1)S(1)}, u32[]{:S(2)}, u32[]{:S(2)}) collective-permute-start(f16[144,256]{1,0:T(8,128)(2,1)S(1)} %convert_element_type.61), channel_id=1, source_target_pairs={{0,64},{4,68},{8,72},{12,76},{16,80},{20,84},{24,88},{28,92},{32,9... | collective-permute-start | bytes 221192 | tf_op jit(solution)/shard_map/ppermute | solution.py:19
  37.3 2.9 %collective-permute-start.12 = (f16[144,256]{1,0:T(8,128)(2,1)S(1)}, f16[144,256]{1,0:T(8,128)(2,1)S(1)}, u32[]{:S(2)}, u32[]{:S(2)}) collective-permute-start(f16[144,256]{1,0:T(8,128)(2,1)S(1)} %convert_element_type.56), channel_id=1, source_target_pairs={{0,2},{1,3},{2,0},{3,1},{4,6},{5,7},{6,4},{7,5},{8,10},{9,11},{10,... | collective-permute-start | bytes 221192 | tf_op jit(solution)/shard_map/ppermute | solution.py:19
  40.2 1.5 %collective-permute-start.11 = (f16[144,256]{1,0:T(8,128)(2,1)S(1)}, f16[144,256]{1,0:T(8,128)(2,1)S(1)}, u32[]{:S(2)}, u32[]{:S(2)}) collective-permute-start(f16[144,256]{1,0:T(8,128)(2,1)S(1)} %convert_element_type.56), channel_id=1, source_target_pairs={{0,3},{1,2},{2,1},{3,0},{4,7},{5,6},{6,5},{7,4},{8,11},{9,10},{10,... | collective-permute-start | bytes 221192 | tf_op jit(solution)/shard_map/ppermute | solution.py:19
  41.9 1.5 %collective-permute-done.12 = f16[144,256]{1,0:T(8,128)(2,1)S(1)} collective-permute-done((f16[144,256]{1,0:T(8,128)(2,1)S(1)}, f16[144,256]{1,0:T(8,128)(2,1)S(1)}, u32[]{:S(2)}, u32[]{:S(2)}) %collective-permute-start.12) | collective-permute-done | bytes 73760 | tf_op jit(solution)/shard_map/ppermute | solution.py:19
  43.4 2.4 %collective-permute-done.11 = f16[144,256]{1,0:T(8,128)(2,1)S(1)} collective-permute-done((f16[144,256]{1,0:T(8,128)(2,1)S(1)}, f16[144,256]{1,0:T(8,128)(2,1)S(1)}, u32[]{:S(2)}, u32[]{:S(2)}) %collective-permute-start.11) | collective-permute-done | bytes 73760 | tf_op jit(solution)/shard_map/ppermute | solution.py:19
  45.8 4.6 %shard_map.79 = (f32[128,2048]{1,0:T(8,128)S(1)}, f32[128,256]{1,0:T(8,128)S(1)}) custom-call(bf16[128,2048]{1,0:T(8,128)(2,1)S(1)} %get-tuple-element.53.cols_ref, bf16[1,2048,2048]{2,1,0:T(8,128)(2,1)S(1)} %bitcast.1, f32[144,256]{1,0:T(8,128)S(1)} %convert_element_type.62.y1, f32[144,256]{1,0:T(8,128)S(1)} %convert_element_type.63.y3, ...), custom_call_target="tpu_custom_call" | custom-call | flops 1073741824 | bytes 9961472 | tf_op jit(solution)/shard_map/pallas_call | solution.py:59
  50.4 1.0 %shard_map.80 = (f32[32,2048]{1,0:T(8,128)S(1)}, bf16[32,2048]{1,0:T(8,128)(2,1)S(1)}, bf16[32,2048]{1,0:T(8,128)(2,1)S(1)}, bf16[32,2048]{1,0:T(8,128)(2,1)S(1)}) custom-call(f32[128,256]{1,0:T(8,128)S(1)} %get-tuple-element.58.part_ref, f32[144,256]{1,0:T(8,128)S(1)} %convert_element_type.65.a, f32[144,256]{1,0:T(8,128)S(1)} %convert_element_type.66.b, ...), custom_call_target="tpu_custom_call" | custom-call | flops 134217728 | bytes 4194304 | tf_op jit(solution)/shard_map/pallas_call | solution.py:59
  51.5 1.6 %collective-permute-start.18 = (bf16[32,2048]{1,0:T(8,128)(2,1)S(1)}, bf16[32,2048]{1,0:T(8,128)(2,1)S(1)}, u32[]{:S(2)}, u32[]{:S(2)}) collective-permute-start(bf16[32,2048]{1,0:T(8,128)(2,1)S(1)} %get-tuple-element.66), channel_id=1, source_target_pairs={{0,3},{1,2},{2,1},{3,0},{4,7},{5,6},{6,5},{7,4},{8,11},{9,10},{10,... | collective-permute-start | bytes 393224 | tf_op jit(solution)/shard_map/ppermute | solution.py:19
  53.1 2.5 %collective-permute-start.16 = (bf16[32,2048]{1,0:T(8,128)(2,1)S(1)}, bf16[32,2048]{1,0:T(8,128)(2,1)S(1)}, u32[]{:S(2)}, u32[]{:S(2)}) collective-permute-start(bf16[32,2048]{1,0:T(8,128)(2,1)S(1)} %get-tuple-element.63), channel_id=1, source_target_pairs={{0,2},{1,3},{2,0},{3,1},{4,6},{5,7},{6,4},{7,5},{8,10},{9,11},{10,... | collective-permute-start | bytes 393224 | tf_op jit(solution)/shard_map/ppermute | solution.py:19
  55.6 0.9 %collective-permute-done.17.refs_1_ = bf16[32,2048]{1,0:T(8,128)(2,1)S(1)} collective-permute-done((bf16[32,2048]{1,0:T(8,128)(2,1)S(1)}, bf16[32,2048]{1,0:T(8,128)(2,1)S(1)}, u32[]{:S(2)}, u32[]{:S(2)}) %collective-permute-start.17) | collective-permute-done | bytes 131104 | tf_op jit(solution)/shard_map/ppermute | solution.py:19
  56.4 1.3 %collective-permute-done.18.refs_2_ = bf16[32,2048]{1,0:T(8,128)(2,1)S(1)} collective-permute-done((bf16[32,2048]{1,0:T(8,128)(2,1)S(1)}, bf16[32,2048]{1,0:T(8,128)(2,1)S(1)}, u32[]{:S(2)}, u32[]{:S(2)}) %collective-permute-start.18) | collective-permute-done | bytes 131104 | tf_op jit(solution)/shard_map/ppermute | solution.py:19
  57.7 0.9 %shard_map.81.refs_1_ = f32[32,8192]{1,0:T(8,128)} custom-call(f32[32,2048]{1,0:T(8,128)S(1)} %get-tuple-element.64.refs_0_, bf16[32,2048]{1,0:T(8,128)(2,1)S(1)} %collective-permute-done.17.refs_1_, bf16[32,2048]{1,0:T(8,128)(2,1)S(1)} %collective-permute-done.18.refs_2_), custom_call_target="tpu_custom_call" | custom-call | bytes 1179648 | tf_op jit(solution)/shard_map/pallas_call | solution.py:59
  58.7 0.9 %collective-permute-done.16.refs_0_ = bf16[32,2048]{1,0:T(8,128)(2,1)S(1)} collective-permute-done((bf16[32,2048]{1,0:T(8,128)(2,1)S(1)}, bf16[32,2048]{1,0:T(8,128)(2,1)S(1)}, u32[]{:S(2)}, u32[]{:S(2)}) %collective-permute-start.16) | collective-permute-done | bytes 131104 | tf_op jit(solution)/shard_map/ppermute | solution.py:19
  59.6 0.7 %shard_map.82 = f32[32,8192]{1,0:T(8,128)} custom-call(bf16[32,2048]{1,0:T(8,128)(2,1)S(1)} %collective-permute-done.16.refs_0_, f32[32,8192]{1,0:T(8,128)} %shard_map.81.refs_1_), custom_call_target="tpu_custom_call", output_to_operand_aliasing={{}: (1, {})} | custom-call | bytes 393216 | tf_op jit(solution)/shard_map/pallas_call | solution.py:59
  (38 shorter events, 2.5 us)
Async XLA Ops:
  1.1 9.8 %collective-permute-start = (bf16[32,2048]{1,0:T(8,128)(2,1)S(1)}, bf16[32,2048]{1,0:T(8,128)(2,1)S(1)}, u32[]{:S(2)}, u32[]{:S(2)}) collective-permute-start(bf16[32,2048]{1,0:T(8,128)(2,1)S(1)} %get-tuple-element.37), channel_id=1, source_target_pairs={{0,1},{1,0},{2,3},{3,2},{4,5},{5,4},{6,7},{7,6},{8,9},{9,8},{10,11... | collective-permute-start | bytes 393224 | tf_op jit(solution)/shard_map/ppermute | solution.py:19
  2.9 8.1 %collective-permute-start.1 = (bf16[32,2048]{1,0:T(8,128)(2,1)S(1)}, bf16[32,2048]{1,0:T(8,128)(2,1)S(1)}, u32[]{:S(2)}, u32[]{:S(2)}) collective-permute-start(bf16[32,2048]{1,0:T(8,128)(2,1)S(1)} %get-tuple-element.38), channel_id=1, source_target_pairs={{0,3},{1,2},{2,1},{3,0},{4,7},{5,6},{6,5},{7,4},{8,11},{9,10},{10,... | collective-permute-start | bytes 393224 | tf_op jit(solution)/shard_map/ppermute | solution.py:19
  5.1 40.8 %slice-start = ((s8[8388608]{0:T(1024)(128)(4,1)}), s8[4194304]{0:T(1024)(128)(4,1)S(1)}, s32[]{:S(2)}) async-start(s8[8388608]{0:T(1024)(128)(4,1)} %bitcast), calls=%async_computation | async-start | bytes 8388608
  5.1 40.8 %slice-start.1 = ((s8[8388608]{0:T(1024)(128)(4,1)}), s8[4194304]{0:T(1024)(128)(4,1)S(1)}, s32[]{:S(2)}) async-start(s8[8388608]{0:T(1024)(128)(4,1)} %bitcast), calls=%async_computation.1 | async-start | bytes 8388608
  5.1 6.8 %collective-permute-start.2 = (bf16[32,2048]{1,0:T(8,128)(2,1)S(1)}, bf16[32,2048]{1,0:T(8,128)(2,1)S(1)}, u32[]{:S(2)}, u32[]{:S(2)}) collective-permute-start(bf16[32,2048]{1,0:T(8,128)(2,1)S(1)} %get-tuple-element.39), channel_id=1, source_target_pairs={{0,2},{1,3},{2,0},{3,1},{4,6},{5,7},{6,4},{7,5},{8,10},{9,11},{10,... | collective-permute-start | bytes 393224 | tf_op jit(solution)/shard_map/ppermute | solution.py:19
  12.6 6.4 %collective-permute-start.5 = (f16[144,256]{1,0:T(8,128)(2,1)S(1)}, f16[144,256]{1,0:T(8,128)(2,1)S(1)}, u32[]{:S(2)}, u32[]{:S(2)}) collective-permute-start(f16[144,256]{1,0:T(8,128)(2,1)S(1)} %convert_element_type.51), channel_id=1, source_target_pairs={{0,2},{1,3},{2,0},{3,1},{4,6},{5,7},{6,4},{7,5},{8,10},{9,11},{10,... | collective-permute-start | bytes 221192 | tf_op jit(solution)/shard_map/ppermute | solution.py:19
  14.4 5.6 %collective-permute-start.4 = (f16[144,256]{1,0:T(8,128)(2,1)S(1)}, f16[144,256]{1,0:T(8,128)(2,1)S(1)}, u32[]{:S(2)}, u32[]{:S(2)}) collective-permute-start(f16[144,256]{1,0:T(8,128)(2,1)S(1)} %convert_element_type.51), channel_id=1, source_target_pairs={{0,3},{1,2},{2,1},{3,0},{4,7},{5,6},{6,5},{7,4},{8,11},{9,10},{10,... | collective-permute-start | bytes 221192 | tf_op jit(solution)/shard_map/ppermute | solution.py:19
  15.9 4.4 %collective-permute-start.3 = (f16[144,256]{1,0:T(8,128)(2,1)S(1)}, f16[144,256]{1,0:T(8,128)(2,1)S(1)}, u32[]{:S(2)}, u32[]{:S(2)}) collective-permute-start(f16[144,256]{1,0:T(8,128)(2,1)S(1)} %convert_element_type.51), channel_id=1, source_target_pairs={{0,1},{1,0},{2,3},{3,2},{4,5},{5,4},{6,7},{7,6},{8,9},{9,8},{10,11... | collective-permute-start | bytes 221192 | tf_op jit(solution)/shard_map/ppermute | solution.py:19
  20.3 1.4 %collective-permute-start.6 = (f32[128,256]{1,0:T(8,128)S(1)}, f32[128,256]{1,0:T(8,128)S(1)}, u32[]{:S(2)}, u32[]{:S(2)}) collective-permute-start(f32[128,256]{1,0:T(8,128)S(1)} %shard_map.76.own), channel_id=1, source_target_pairs={{0,4},{4,0},{8,12},{12,8},{16,20},{20,16},{24,28},{28,24},{32,36},... | collective-permute-start | bytes 393224 | tf_op jit(solution)/shard_map/ppermute | solution.py:19
  22.1 5.6 %collective-permute-start.7 = (f16[144,256]{1,0:T(8,128)(2,1)S(1)}, f16[144,256]{1,0:T(8,128)(2,1)S(1)}, u32[]{:S(2)}, u32[]{:S(2)}) collective-permute-start(f16[144,256]{1,0:T(8,128)(2,1)S(1)} %convert_element_type.57), channel_id=1, source_target_pairs={{0,8},{4,12},{8,0},{12,4},{16,24},{20,28},{24,16},{28,20},{32,40},... | collective-permute-start | bytes 221192 | tf_op jit(solution)/shard_map/ppermute | solution.py:19
  24.0 5.7 %collective-permute-start.9 = (f16[144,256]{1,0:T(8,128)(2,1)S(1)}, f16[144,256]{1,0:T(8,128)(2,1)S(1)}, u32[]{:S(2)}, u32[]{:S(2)}) collective-permute-start(f16[144,256]{1,0:T(8,128)(2,1)S(1)} %convert_element_type.57), channel_id=1, source_target_pairs={{0,24},{4,28},{8,16},{12,20},{16,8},{20,12},{24,0},{28,4},{32,56},... | collective-permute-start | bytes 221192 | tf_op jit(solution)/shard_map/ppermute | solution.py:19
  26.6 5.9 %collective-permute-start.8 = (f16[144,256]{1,0:T(8,128)(2,1)S(1)}, f16[144,256]{1,0:T(8,128)(2,1)S(1)}, u32[]{:S(2)}, u32[]{:S(2)}) collective-permute-start(f16[144,256]{1,0:T(8,128)(2,1)S(1)} %convert_element_type.57), channel_id=1, source_target_pairs={{0,16},{4,20},{8,24},{12,28},{16,0},{20,4},{24,8},{28,12},{32,48},... | collective-permute-start | bytes 221192 | tf_op jit(solution)/shard_map/ppermute | solution.py:19
  32.9 7.3 %collective-permute-start.15 = (f16[144,256]{1,0:T(8,128)(2,1)S(1)}, f16[144,256]{1,0:T(8,128)(2,1)S(1)}, u32[]{:S(2)}, u32[]{:S(2)}) collective-permute-start(f16[144,256]{1,0:T(8,128)(2,1)S(1)} %convert_element_type.61), channel_id=1, source_target_pairs={{0,96},{4,100},{8,104},{12,108},{16,112},{20,116},{24,120},{28,124... | collective-permute-start | bytes 221192 | tf_op jit(solution)/shard_map/ppermute | solution.py:19
  35.7 6.1 %collective-permute-start.14 = (f16[144,256]{1,0:T(8,128)(2,1)S(1)}, f16[144,256]{1,0:T(8,128)(2,1)S(1)}, u32[]{:S(2)}, u32[]{:S(2)}) collective-permute-start(f16[144,256]{1,0:T(8,128)(2,1)S(1)} %convert_element_type.61), channel_id=1, source_target_pairs={{0,64},{4,68},{8,72},{12,76},{16,80},{20,84},{24,88},{28,92},{32,9... | collective-permute-start | bytes 221192 | tf_op jit(solution)/shard_map/ppermute | solution.py:19
  36.5 5.3 %collective-permute-start.13 = (f16[144,256]{1,0:T(8,128)(2,1)S(1)}, f16[144,256]{1,0:T(8,128)(2,1)S(1)}, u32[]{:S(2)}, u32[]{:S(2)}) collective-permute-start(f16[144,256]{1,0:T(8,128)(2,1)S(1)} %convert_element_type.61), channel_id=1, source_target_pairs={{0,32},{4,36},{8,40},{12,44},{16,48},{20,52},{24,56},{28,60},{32,0... | collective-permute-start | bytes 221192 | tf_op jit(solution)/shard_map/ppermute | solution.py:19
  37.1 4.8 %collective-permute-start.10 = (f16[144,256]{1,0:T(8,128)(2,1)S(1)}, f16[144,256]{1,0:T(8,128)(2,1)S(1)}, u32[]{:S(2)}, u32[]{:S(2)}) collective-permute-start(f16[144,256]{1,0:T(8,128)(2,1)S(1)} %convert_element_type.55), channel_id=1, source_target_pairs={{0,1},{1,0},{2,3},{3,2},{4,5},{5,4},{6,7},{7,6},{8,9},{9,8},{10,11... | collective-permute-start | bytes 221192 | tf_op jit(solution)/shard_map/ppermute | solution.py:19
  37.3 6.0 %collective-permute-start.12 = (f16[144,256]{1,0:T(8,128)(2,1)S(1)}, f16[144,256]{1,0:T(8,128)(2,1)S(1)}, u32[]{:S(2)}, u32[]{:S(2)}) collective-permute-start(f16[144,256]{1,0:T(8,128)(2,1)S(1)} %convert_element_type.56), channel_id=1, source_target_pairs={{0,2},{1,3},{2,0},{3,1},{4,6},{5,7},{6,4},{7,5},{8,10},{9,11},{10,... | collective-permute-start | bytes 221192 | tf_op jit(solution)/shard_map/ppermute | solution.py:19
  40.2 5.6 %collective-permute-start.11 = (f16[144,256]{1,0:T(8,128)(2,1)S(1)}, f16[144,256]{1,0:T(8,128)(2,1)S(1)}, u32[]{:S(2)}, u32[]{:S(2)}) collective-permute-start(f16[144,256]{1,0:T(8,128)(2,1)S(1)} %convert_element_type.56), channel_id=1, source_target_pairs={{0,3},{1,2},{2,1},{3,0},{4,7},{5,6},{6,5},{7,4},{8,11},{9,10},{10,... | collective-permute-start | bytes 221192 | tf_op jit(solution)/shard_map/ppermute | solution.py:19
  51.4 5.0 %collective-permute-start.17 = (bf16[32,2048]{1,0:T(8,128)(2,1)S(1)}, bf16[32,2048]{1,0:T(8,128)(2,1)S(1)}, u32[]{:S(2)}, u32[]{:S(2)}) collective-permute-start(bf16[32,2048]{1,0:T(8,128)(2,1)S(1)} %get-tuple-element.65), channel_id=1, source_target_pairs={{0,1},{1,0},{2,3},{3,2},{4,5},{5,4},{6,7},{7,6},{8,9},{9,8},{10,11... | collective-permute-start | bytes 393224 | tf_op jit(solution)/shard_map/ppermute | solution.py:19
  51.5 6.3 %collective-permute-start.18 = (bf16[32,2048]{1,0:T(8,128)(2,1)S(1)}, bf16[32,2048]{1,0:T(8,128)(2,1)S(1)}, u32[]{:S(2)}, u32[]{:S(2)}) collective-permute-start(bf16[32,2048]{1,0:T(8,128)(2,1)S(1)} %get-tuple-element.66), channel_id=1, source_target_pairs={{0,3},{1,2},{2,1},{3,0},{4,7},{5,6},{6,5},{7,4},{8,11},{9,10},{10,... | collective-permute-start | bytes 393224 | tf_op jit(solution)/shard_map/ppermute | solution.py:19
  53.1 6.5 %collective-permute-start.16 = (bf16[32,2048]{1,0:T(8,128)(2,1)S(1)}, bf16[32,2048]{1,0:T(8,128)(2,1)S(1)}, u32[]{:S(2)}, u32[]{:S(2)}) collective-permute-start(bf16[32,2048]{1,0:T(8,128)(2,1)S(1)} %get-tuple-element.63), channel_id=1, source_target_pairs={{0,2},{1,3},{2,0},{3,1},{4,6},{5,7},{6,4},{7,5},{8,10},{9,11},{10,... | collective-permute-start | bytes 393224 | tf_op jit(solution)/shard_map/ppermute | solution.py:19

commit v3 on v2

--- a/solution.py
+++ b/solution.py
@@ -207,38 +207,69 @@
     )
     message = shape(total + EXTRA, rank)
 
-    def leaf_body(own, first, second, third, basis_ref, transfer, cols, up_msg, own_msg, mid_msg, kept):
+    def leaf_body(own, first, second, third, basis_ref, transfer, cols, up_msg, low_msg, up_ref, mid_ref):
         position = lax.axis_index("rhs")
         for slot, ref in enumerate((own, first, second, third)):
             cols[slot * part : (slot + 1) * part, :] = ref[...]
         coeffs = dot(cols[...], basis_ref[...])
         middle = dot_narrow(coeffs, transfer[0])
         upward = dot_narrow(middle, transfer[1])
-        for msg, value in ((up_msg, upward), (own_msg, coeffs), (mid_msg, middle)):
+
+        def place(ref, value, start=0):
+            for slot, mask in enumerate(masks):
+                rows = value[slot * part : (slot + 1) * part, :]
+                ref[pl.ds(pl.multiple_of(start + (position ^ mask) * part, 16), part), :] = rows
+
+        for msg, value, start in ((up_msg, upward, 0), (low_msg, coeffs, 0), (low_msg, middle, total + EXTRA)):
             scaled, power = encode(value)
-            for slot, mask in enumerate(masks):
-                msg[aligned(position ^ mask, part), :] = scaled[slot * part : (slot + 1) * part, :]
-            msg[total:, :] = power
-        for slot, mask in enumerate(masks):
-            kept[aligned(position ^ mask, part), :] = upward[slot * part : (slot + 1) * part, :]
-
-    cols, up_msg, own_msg, mid_msg, upward = call(
+            place(msg, scaled, start)
+            msg[start + total : start + total + EXTRA, :] = power
+        place(up_ref, upward)
+        place(mid_ref, middle)
+
+    plain = shape(total, rank)
+    cols, up_msg, low_msg, upward, middle = call(
         leaf_body,
-        (shape(total, leaf, dtype=BF16), message, message, message, shape(total, rank)),
+        (shape(total, leaf, dtype=BF16), message, shape(2 * (total + EXTRA), rank), plain, plain),
         (blocks[0], *came, basis, low),
         flops=2 * total * leaf * rank,
         moved=2**21,
         in_specs=[VMEM] * 6,
         out_specs=[VMEM] * 5,
     )
-    up_msg, own_msg, mid_msg = [msg.astype(F16) for msg in (up_msg, own_msg, mid_msg)]
+    up_msg, low_msg = up_msg.astype(F16), low_msg.astype(F16)
     ups = [swap(up_msg, "rhs", mask).astype(F32) for mask in masks[1:]]
+    low_sib = swap(low_msg, "rhs", 1).astype(F32)
+
+    def near_half(cols, half):
+        width = leaf // 8
+
+        def body(cols_ref, block_ref, out_ref):
+            for step in range(4):
+                rows = block_ref[0, (4 * half + step) * width : (4 * half + step + 1) * width, :]
+                out_ref[:, step * width : (step + 1) * width] = lax.dot_general(
+                    cols_ref[...], rows, (((1,), (1,)), ((), ())), preferred_element_type=F32
+                )
+
+        return call(
+            body,
+            shape(total, leaf // 2),
+            (cols, near_blocks),
+            flops=total * leaf * leaf,
+            moved=leaf * leaf + 3 * total * leaf,
+            in_specs=[VMEM] * 2,
+            out_specs=VMEM,
+        )
+
+    near_left = near_half(cols, 0)
+    ups, near_left = lax.optimization_barrier((ups, near_left))
+
     def group_body(own, a, b, c, out):
         out[...] = own[...] + decode(a) + (decode(b) + decode(c))
 
     group = call(
         group_body,
-        shape(total, rank),
+        plain,
         (upward, *ups),
         moved=2**20,
         in_specs=[VMEM] * 4,
@@ -246,26 +277,26 @@
     )
     group_sib = swap(group, "leaf", 1)
 
-    def chip_body(own, sibling, matrices, out, kept):
+    def chip_body(own, sibling, matrices, mid_ref, low_ref, out, kept, cousin_msg):
         value = dot_narrow(own[...], matrices[:rank, :]) + dot_narrow(sibling[...], matrices[rank:, :])
         kept[...] = value
         put_encoded(out, value)
-
-    chip_msg, chip = call(
+        put_encoded(cousin_msg, mid_ref[...] + decode(low_ref.at[total + EXTRA :, :]))
+
+    chip_msg, chip, cousin_msg = call(
         chip_body,
-        (message, shape(total, rank)),
-        (group, group_sib, pair),
+        (message, plain, message),
+        (group, group_sib, pair, middle, low_sib),
         flops=8 * total * rank * rank,
         moved=2**20,
-        in_specs=[VMEM] * 3,
-        out_specs=[VMEM] * 2,
-    )
-    chip_msg = chip_msg.astype(F16)
-    chips = [swap(chip_msg, "leaf", 2 * mask) for mask in (1, 3, 2)]
-    own_msg, mid_msg, chips[0] = lax.optimization_barrier((own_msg, mid_msg, chips[0]))
-    chips = [chips[slot].astype(F32) for slot in (0, 2, 1)]
-    mids = [swap(own_msg, "rhs", 1).astype(F32)] + [swap(mid_msg, "rhs", mask).astype(F32) for mask in (3, 2)]
-
+        in_specs=[VMEM] * 5,
+        out_specs=[VMEM] * 3,
+    )
+    chip_msg, cols = lax.optimization_barrier((chip_msg.astype(F16), cols))
+    chips = [swap(chip_msg, "leaf", 2 * mask).astype(F32) for mask in (1, 2, 3)]
+    cousin = swap(cousin_msg.astype(F16), "rhs", 3).astype(F32)
+    near_right = near_half(cols, 1)
+    chips, cousin, near_right = lax.optimization_barrier((chips, cousin, near_right))
 
     def line_body(own, a, b, c, high, low, out):
         value = jnp.concatenate([own[...]] + [decode(ref) for ref in (a, b, c)], axis=1)
@@ -280,36 +311,28 @@
         in_specs=[VMEM] * 6,
         out_specs=VMEM,
     )
-    line_msg, cols = lax.optimization_barrier((line_msg.astype(F16), cols))
+    line_msg = line_msg.astype(F16)
     lines = [swap(line_msg, "leaf", 8 * mask).astype(F32) for mask in (1, 2, 3)]
 
-    steps = 8
-
-    def near_body(cols_ref, block_ref, y1, y3, y2, core, z1, z2, z3, high, low, out_ref, part_out):
-        out_ref[...] = lax.dot_general(
-            cols_ref[...], block_ref[0], (((1,), (1,)), ((), ())), preferred_element_type=F32
+    def partial_body(sibling, others, core, z1, z2, z3, high, low, out):
+        value = jnp.concatenate(
+            [decode(sibling.at[: total + EXTRA, :]), decode(others), core[...]]
+            + [decode(ref) for ref in (z1, z2, z3)],
+            axis=1,
         )
-
-        @pl.when(pl.program_id(0) == 0)
-        def _():
-            value = jnp.concatenate(
-                [decode(y1), decode(y3) + decode(y2), core[...]] + [decode(ref) for ref in (z1, z2, z3)],
-                axis=1,
-            )
-            part_out[...] = dot_wide(value, high[...], low[...])
-
-    near, partial = call(
-        near_body,
-        (shape(total, leaf), shape(total, rank)),
-        (cols, near_blocks, *mids, group_sib, *chips, acc_high, acc_low),
-        flops=2 * total * leaf * leaf,
-        moved=2 * leaf * leaf + 6 * total * leaf,
-        grid=(steps,),
-        in_specs=[VMEM, pl.BlockSpec((1, leaf // steps, leaf), lambda i: (0, i, 0))] + [VMEM] * 9,
-        out_specs=[pl.BlockSpec((total, leaf // steps), lambda i: (0, i)), VMEM],
-    )
-
-    def last_body(part_ref, a, b, c, high, low, basis_ref, near_ref, own, first, second, third, inner):
+        out[...] = dot_wide(value, high[...], low[...])
+
+    partial = call(
+        partial_body,
+        plain,
+        (low_sib, cousin, group_sib, *chips, acc_high, acc_low),
+        flops=36 * total * rank * rank,
+        moved=2**21,
+        in_specs=[VMEM] * 8,
+        out_specs=VMEM,
+    )
+
+    def last_body(part_ref, a, b, c, high, low, basis_ref, left, right, own, first, second, third, inner):
         position = lax.axis_index("rhs")
         value = jnp.concatenate([decode(ref) for ref in (a, b, c)], axis=1)
         inner[...] = part_ref[...] + dot_wide(value, high[...], low[...])
@@ -319,16 +342,17 @@
         )
         for slot, ref in enumerate((own, first, second, third)):
             rows = slice(slot * part, (slot + 1) * part)
-            ref[...] = (near_ref[rows, :] + far[rows, :]).astype(ref.dtype)
+            ref[:, : leaf // 2] = (left[rows, :] + far[rows, : leaf // 2]).astype(ref.dtype)
+            ref[:, leaf // 2 :] = (right[rows, :] + far[rows, leaf // 2 :]).astype(ref.dtype)
 
     sent = shape(part, leaf, dtype=BF16)
     own, *blocks = call(
         last_body,
         (shape(part, leaf), sent, sent, sent),
-        (partial, *lines, top_high, top_low, basis, near),
+        (partial, *lines, top_high, top_low, basis, near_left, near_right),
         flops=2 * total * leaf * rank,
         moved=2**22,
-        in_specs=[VMEM] * 8,
+        in_specs=[VMEM] * 9,
         out_specs=[VMEM] * 4,
         scratch_shapes=[pltpu.VMEM((total, rank), F32)],
     )

time: 60.4 us -> 53.8 us (0.89)
  waiting for transfers between devices: 18 us -> 14.4 us
  starting transfers between devices: 26.9 us -> 24.9 us
  Pallas kernels: 14.9 us -> 13.9 us
    ppermute x19 -> x18, waiting for transfers between devices: 18 us -> 14.4 us  [swap(): return lax.ppermute(value, axis, pairs)]
    ppermute x19 -> x18, starting transfers between devices: 26.9 us -> 24.9 us  [swap(): return lax.ppermute(value, axis, pairs)]
    pallas_call x10 -> x12, Pallas kernels: 14.9 us -> 13.9 us  [call(): pl.pallas_call(body, out_shape=outs, compiler_params=pltpu.CompilerParams...]
  transfers between devices with their start and end apart: 19 -> 18, of which waited for: 12 -> 11; matrix products, arithmetic and copies ran while one was open for 0% -> 0% of each run, Pallas kernels for 10% -> 18%
where the time goes in v3:
time: 53.8 us; the launch traced here: 53.6 us
  starting transfers between devices  24.9 us (46%)
  waiting for transfers between devices  14.4 us (27%)
  Pallas kernels  13.9 us (26%)
    ppermute x18, starting transfers between devices, swap(): return lax.ppermute(value, axis, pairs)  24.9 us
    ppermute x18, waiting for transfers between devices, swap(): return lax.ppermute(value, axis, pairs)  14.4 us
    pallas_call x12, Pallas kernels, call(): pl.pallas_call(body, out_shape=outs, compiler_params=pltpu.CompilerParams...  13.9 us
  transfers between devices with their start and end apart: 18, of which 11 were waited for; matrix products, arithmetic and copies ran while one was open for 0% of the time, Pallas kernels for 18%

profile of v3, /device:TPU:0, one launch (start us, length us, event | category | flops | bytes accessed | tf_op | source)
XLA Modules:
  0.0 53.6 jit_solution(1221451410461211030)
XLA Ops:
  0.0 1.1 %shard_map.73 = (bf16[32,2048]{1,0:T(8,128)(2,1)S(1)}, bf16[32,2048]{1,0:T(8,128)(2,1)S(1)}, bf16[32,2048]{1,0:T(8,128)(2,1)S(1)}, bf16[32,2048]{1,0:T(8,128)(2,1)S(1)}) custom-call(bf16[32,8192]{1,0:T(8,128)(2,1)} %source.1), custom_call_target="tpu_custom_call" | custom-call | bytes 1048576 | tf_op jit(solution)/shard_map/pallas_call | solution.py:59
  1.1 1.7 %collective-permute-start = (bf16[32,2048]{1,0:T(8,128)(2,1)S(1)}, bf16[32,2048]{1,0:T(8,128)(2,1)S(1)}, u32[]{:S(2)}, u32[]{:S(2)}) collective-permute-start(bf16[32,2048]{1,0:T(8,128)(2,1)S(1)} %get-tuple-element.42), channel_id=1, source_target_pairs={{0,1},{1,0},{2,3},{3,2},{4,5},{5,4},{6,7},{7,6},{8,9},{9,8},{10,11... | collective-permute-start | bytes 393224 | tf_op jit(solution)/shard_map/ppermute | solution.py:19
  2.9 2.2 %collective-permute-start.1 = (bf16[32,2048]{1,0:T(8,128)(2,1)S(1)}, bf16[32,2048]{1,0:T(8,128)(2,1)S(1)}, u32[]{:S(2)}, u32[]{:S(2)}) collective-permute-start(bf16[32,2048]{1,0:T(8,128)(2,1)S(1)} %get-tuple-element.43), channel_id=1, source_target_pairs={{0,3},{1,2},{2,1},{3,0},{4,7},{5,6},{6,5},{7,4},{8,11},{9,10},{10,... | collective-permute-start | bytes 393224 | tf_op jit(solution)/shard_map/ppermute | solution.py:19
  5.1 0.7 %collective-permute-start.2 = (bf16[32,2048]{1,0:T(8,128)(2,1)S(1)}, bf16[32,2048]{1,0:T(8,128)(2,1)S(1)}, u32[]{:S(2)}, u32[]{:S(2)}) collective-permute-start(bf16[32,2048]{1,0:T(8,128)(2,1)S(1)} %get-tuple-element.44), channel_id=1, source_target_pairs={{0,2},{1,3},{2,0},{3,1},{4,6},{5,7},{6,4},{7,5},{8,10},{9,11},{10,... | collective-permute-start | bytes 393224 | tf_op jit(solution)/shard_map/ppermute | solution.py:19
  5.8 5.2 %shard_map.74 = (bf16[2048,256]{1,0:T(8,128)(2,1)S(1)}, bf16[2,256,256]{2,1,0:T(8,128)(2,1)S(1)}, bf16[512,256]{1,0:T(8,128)(2,1)S(1)}, bf16[1024,256]{1,0:T(8,1...) custom-call(bf16[1,2048,256]{2,1,0:T(8,128)(2,1)} %basis_hbm.1, ...), custom_call_target="tpu_custom_call" | custom-call | flops 1140850688 | bytes 4194304 | tf_op jit(solution)/shard_map/pallas_call | solution.py:59
  11.0 0.9 %collective-permute-done.2.third = bf16[32,2048]{1,0:T(8,128)(2,1)S(1)} collective-permute-done((bf16[32,2048]{1,0:T(8,128)(2,1)S(1)}, bf16[32,2048]{1,0:T(8,128)(2,1)S(1)}, u32[]{:S(2)}, u32[]{:S(2)}) %collective-permute-start.2) | collective-permute-done | bytes 131104 | tf_op jit(solution)/shard_map/ppermute | solution.py:19
  11.9 0.7 %shard_map.75 = (bf16[128,2048]{1,0:T(8,128)(2,1)S(1)}, f32[144,256]{1,0:T(8,128)S(1)}, f32[288,256]{1,0:T(8,128)S(1)}, f32[128,256]{1,0:T(8,128)S(1)}, f32[128,256]{1,0:T(8,128)S(1)}) custom-call(bf16[32,2048]{1,0:T(8,128)(2,1)S(1)} %get-tuple-element.41.own, bf16[32,2048]{1,0:T(8,128)(2,1)S(1)} %collective-permute-done.first, ...), custom_call_target="tpu_custom_call" | custom-call | flops 134217728 | bytes 2097152 | tf_op jit(solution)/shard_map/pallas_call | solution.py:59
  12.6 1.8 %collective-permute-start.6 = (f16[144,256]{1,0:T(8,128)(2,1)S(1)}, f16[144,256]{1,0:T(8,128)(2,1)S(1)}, u32[]{:S(2)}, u32[]{:S(2)}) collective-permute-start(f16[144,256]{1,0:T(8,128)(2,1)S(1)} %convert_element_type.50), channel_id=1, source_target_pairs={{0,2},{1,3},{2,0},{3,1},{4,6},{5,7},{6,4},{7,5},{8,10},{9,11},{10,... | collective-permute-start | bytes 221192 | tf_op jit(solution)/shard_map/ppermute | solution.py:19
  14.4 1.5 %collective-permute-start.5 = (f16[144,256]{1,0:T(8,128)(2,1)S(1)}, f16[144,256]{1,0:T(8,128)(2,1)S(1)}, u32[]{:S(2)}, u32[]{:S(2)}) collective-permute-start(f16[144,256]{1,0:T(8,128)(2,1)S(1)} %convert_element_type.50), channel_id=1, source_target_pairs={{0,3},{1,2},{2,1},{3,0},{4,7},{5,6},{6,5},{7,4},{8,11},{9,10},{10,... | collective-permute-start | bytes 221192 | tf_op jit(solution)/shard_map/ppermute | solution.py:19
  16.2 1.8 %collective-permute-start.3 = (f16[288,256]{1,0:T(8,128)(2,1)S(1)}, f16[288,256]{1,0:T(8,128)(2,1)S(1)}, u32[]{:S(2)}, u32[]{:S(2)}) collective-permute-start(f16[288,256]{1,0:T(8,128)(2,1)S(1)} %convert_element_type.48), channel_id=1, source_target_pairs={{0,1},{1,0},{2,3},{3,2},{4,5},{5,4},{6,7},{7,6},{8,9},{9,8},{10,11... | collective-permute-start | bytes 442376 | tf_op jit(solution)/shard_map/ppermute | solution.py:19
  18.1 1.5 %shard_map.76.left = f32[128,1024]{1,0:T(8,128)S(1)} custom-call(bf16[128,2048]{1,0:T(8,128)(2,1)S(1)} %get-tuple-element.59.cols_ref, bf16[1,2048,2048]{2,1,0:T(8,128)(2,1)S(1)} %bitcast.1), custom_call_target="tpu_custom_call" | custom-call | flops 536870912 | bytes 4980736 | tf_op jit(solution)/shard_map/pallas_call | solution.py:59
  20.0 0.8 %collective-permute-done.4 = f16[144,256]{1,0:T(8,128)(2,1)S(1)} collective-permute-done((f16[144,256]{1,0:T(8,128)(2,1)S(1)}, f16[144,256]{1,0:T(8,128)(2,1)S(1)}, u32[]{:S(2)}, u32[]{:S(2)}) %collective-permute-start.4) | collective-permute-done | bytes 73760 | tf_op jit(solution)/shard_map/ppermute | solution.py:19
  20.9 1.4 %collective-permute-done.3 = f16[288,256]{1,0:T(8,128)(2,1)S(1)} collective-permute-done((f16[288,256]{1,0:T(8,128)(2,1)S(1)}, f16[288,256]{1,0:T(8,128)(2,1)S(1)}, u32[]{:S(2)}, u32[]{:S(2)}) %collective-permute-start.3) | collective-permute-done | bytes 147488 | tf_op jit(solution)/shard_map/ppermute | solution.py:19
  22.7 1.6 %collective-permute-start.11 = (f16[144,256]{1,0:T(8,128)(2,1)S(1)}, f16[144,256]{1,0:T(8,128)(2,1)S(1)}, u32[]{:S(2)}, u32[]{:S(2)}) collective-permute-start(f16[144,256]{1,0:T(8,128)(2,1)S(1)} %convert_element_type.58), channel_id=1, source_target_pairs={{0,3},{1,2},{2,1},{3,0},{4,7},{5,6},{6,5},{7,4},{8,11},{9,10},{10,... | collective-permute-start | bytes 221192 | tf_op jit(solution)/shard_map/ppermute | solution.py:19
  24.3 4.0 %collective-permute-start.10 = (f16[144,256]{1,0:T(8,128)(2,1)S(1)}, f16[144,256]{1,0:T(8,128)(2,1)S(1)}, u32[]{:S(2)}, u32[]{:S(2)}) collective-permute-start(f16[144,256]{1,0:T(8,128)(2,1)S(1)} %convert_element_type.54), channel_id=1, source_target_pairs={{0,24},{4,28},{8,16},{12,20},{16,8},{20,12},{24,0},{28,4},{32,56},... | collective-permute-start | bytes 221192 | tf_op jit(solution)/shard_map/ppermute | solution.py:19
  28.3 0.9 %collective-permute-start.8 = (f16[144,256]{1,0:T(8,128)(2,1)S(1)}, f16[144,256]{1,0:T(8,128)(2,1)S(1)}, u32[]{:S(2)}, u32[]{:S(2)}) collective-permute-start(f16[144,256]{1,0:T(8,128)(2,1)S(1)} %convert_element_type.54), channel_id=1, source_target_pairs={{0,8},{4,12},{8,0},{12,4},{16,24},{20,28},{24,16},{28,20},{32,40},... | collective-permute-start | bytes 221192 | tf_op jit(solution)/shard_map/ppermute | solution.py:19
  29.2 1.5 %shard_map.79.right = f32[128,1024]{1,0:T(8,128)S(1)} custom-call(bf16[128,2048]{1,0:T(8,128)(2,1)S(1)} %get-tuple-element.59.cols_ref, bf16[1,2048,2048]{2,1,0:T(8,128)(2,1)S(1)} %bitcast.1), custom_call_target="tpu_custom_call" | custom-call | flops 536870912 | bytes 4980736 | tf_op jit(solution)/shard_map/pallas_call | solution.py:59
  30.7 0.6 %collective-permute-done.10 = f16[144,256]{1,0:T(8,128)(2,1)S(1)} collective-permute-done((f16[144,256]{1,0:T(8,128)(2,1)S(1)}, f16[144,256]{1,0:T(8,128)(2,1)S(1)}, u32[]{:S(2)}, u32[]{:S(2)}) %collective-permute-start.10) | collective-permute-done | bytes 73760 | tf_op jit(solution)/shard_map/ppermute | solution.py:19
  31.4 2.9 %collective-permute-done.9 = f16[144,256]{1,0:T(8,128)(2,1)S(1)} collective-permute-done((f16[144,256]{1,0:T(8,128)(2,1)S(1)}, f16[144,256]{1,0:T(8,128)(2,1)S(1)}, u32[]{:S(2)}, u32[]{:S(2)}) %collective-permute-start.9) | collective-permute-done | bytes 73760 | tf_op jit(solution)/shard_map/ppermute | solution.py:19
  34.7 2.8 %collective-permute-start.14 = (f16[144,256]{1,0:T(8,128)(2,1)S(1)}, f16[144,256]{1,0:T(8,128)(2,1)S(1)}, u32[]{:S(2)}, u32[]{:S(2)}) collective-permute-start(f16[144,256]{1,0:T(8,128)(2,1)S(1)} %convert_element_type.60), channel_id=1, source_target_pairs={{0,96},{4,100},{8,104},{12,108},{16,112},{20,116},{24,120},{28,124... | collective-permute-start | bytes 221192 | tf_op jit(solution)/shard_map/ppermute | solution.py:19
  37.6 0.8 %collective-permute-start.13 = (f16[144,256]{1,0:T(8,128)(2,1)S(1)}, f16[144,256]{1,0:T(8,128)(2,1)S(1)}, u32[]{:S(2)}, u32[]{:S(2)}) collective-permute-start(f16[144,256]{1,0:T(8,128)(2,1)S(1)} %convert_element_type.60), channel_id=1, source_target_pairs={{0,64},{4,68},{8,72},{12,76},{16,80},{20,84},{24,88},{28,92},{32,9... | collective-permute-start | bytes 221192 | tf_op jit(solution)/shard_map/ppermute | solution.py:19
  38.4 0.5 collective-permute-start.12
  39.4 1.8 %collective-permute-done.14 = f16[144,256]{1,0:T(8,128)(2,1)S(1)} collective-permute-done((f16[144,256]{1,0:T(8,128)(2,1)S(1)}, f16[144,256]{1,0:T(8,128)(2,1)S(1)}, u32[]{:S(2)}, u32[]{:S(2)}) %collective-permute-start.14) | collective-permute-done | bytes 73760 | tf_op jit(solution)/shard_map/ppermute | solution.py:19
  41.2 2.2 %collective-permute-done.13 = f16[144,256]{1,0:T(8,128)(2,1)S(1)} collective-permute-done((f16[144,256]{1,0:T(8,128)(2,1)S(1)}, f16[144,256]{1,0:T(8,128)(2,1)S(1)}, u32[]{:S(2)}, u32[]{:S(2)}) %collective-permute-start.13) | collective-permute-done | bytes 73760 | tf_op jit(solution)/shard_map/ppermute | solution.py:19
  43.5 1.0 %shard_map.82 = (f32[32,2048]{1,0:T(8,128)S(1)}, bf16[32,2048]{1,0:T(8,128)(2,1)S(1)}, bf16[32,2048]{1,0:T(8,128)(2,1)S(1)}, bf16[32,2048]{1,0:T(8,128)(2,1)S(1)}) custom-call(f32[128,256]{1,0:T(8,128)S(1)} %shard_map.80.part_ref, f32[144,256]{1,0:T(8,128)S(1)} %convert_element_type.61.a, f32[144,256]{1,0:T(8,128)S(1)} %convert_element_type.62.b, ...), custom_call_target="tpu_custom_call" | custom-call | flops 134217728 | bytes 4194304 | tf_op jit(solution)/shard_map/pallas_call | solution.py:59
  44.9 1.5 %collective-permute-start.17 = (bf16[32,2048]{1,0:T(8,128)(2,1)S(1)}, bf16[32,2048]{1,0:T(8,128)(2,1)S(1)}, u32[]{:S(2)}, u32[]{:S(2)}) collective-permute-start(bf16[32,2048]{1,0:T(8,128)(2,1)S(1)} %get-tuple-element.76), channel_id=1, source_target_pairs={{0,3},{1,2},{2,1},{3,0},{4,7},{5,6},{6,5},{7,4},{8,11},{9,10},{10,... | collective-permute-start | bytes 393224 | tf_op jit(solution)/shard_map/ppermute | solution.py:19
  46.4 2.2 %collective-permute-start.15 = (bf16[32,2048]{1,0:T(8,128)(2,1)S(1)}, bf16[32,2048]{1,0:T(8,128)(2,1)S(1)}, u32[]{:S(2)}, u32[]{:S(2)}) collective-permute-start(bf16[32,2048]{1,0:T(8,128)(2,1)S(1)} %get-tuple-element.73), channel_id=1, source_target_pairs={{0,2},{1,3},{2,0},{3,1},{4,6},{5,7},{6,4},{7,5},{8,10},{9,11},{10,... | collective-permute-start | bytes 393224 | tf_op jit(solution)/shard_map/ppermute | solution.py:19
  48.6 0.9 %collective-permute-done.16.refs_1_ = bf16[32,2048]{1,0:T(8,128)(2,1)S(1)} collective-permute-done((bf16[32,2048]{1,0:T(8,128)(2,1)S(1)}, bf16[32,2048]{1,0:T(8,128)(2,1)S(1)}, u32[]{:S(2)}, u32[]{:S(2)}) %collective-permute-start.16) | collective-permute-done | bytes 131104 | tf_op jit(solution)/shard_map/ppermute | solution.py:19
  49.5 1.6 %collective-permute-done.17.refs_2_ = bf16[32,2048]{1,0:T(8,128)(2,1)S(1)} collective-permute-done((bf16[32,2048]{1,0:T(8,128)(2,1)S(1)}, bf16[32,2048]{1,0:T(8,128)(2,1)S(1)}, u32[]{:S(2)}, u32[]{:S(2)}) %collective-permute-start.17) | collective-permute-done | bytes 131104 | tf_op jit(solution)/shard_map/ppermute | solution.py:19
  51.1 0.9 %shard_map.83.refs_1_ = f32[32,8192]{1,0:T(8,128)} custom-call(f32[32,2048]{1,0:T(8,128)S(1)} %get-tuple-element.74.refs_0_, bf16[32,2048]{1,0:T(8,128)(2,1)S(1)} %collective-permute-done.16.refs_1_, bf16[32,2048]{1,0:T(8,128)(2,1)S(1)} %collective-permute-done.17.refs_2_), custom_call_target="tpu_custom_call" | custom-call | bytes 1179648 | tf_op jit(solution)/shard_map/pallas_call | solution.py:59
  52.0 0.9 %collective-permute-done.15.refs_0_ = bf16[32,2048]{1,0:T(8,128)(2,1)S(1)} collective-permute-done((bf16[32,2048]{1,0:T(8,128)(2,1)S(1)}, bf16[32,2048]{1,0:T(8,128)(2,1)S(1)}, u32[]{:S(2)}, u32[]{:S(2)}) %collective-permute-start.15) | collective-permute-done | bytes 131104 | tf_op jit(solution)/shard_map/ppermute | solution.py:19
  52.9 0.7 %shard_map.84 = f32[32,8192]{1,0:T(8,128)} custom-call(bf16[32,2048]{1,0:T(8,128)(2,1)S(1)} %collective-permute-done.15.refs_0_, f32[32,8192]{1,0:T(8,128)} %shard_map.83.refs_1_), custom_call_target="tpu_custom_call", output_to_operand_aliasing={{}: (1, {})} | custom-call | bytes 393216 | tf_op jit(solution)/shard_map/pallas_call | solution.py:59
  (37 shorter events, 2.6 us)
Async XLA Ops:
  1.1 9.8 %collective-permute-start = (bf16[32,2048]{1,0:T(8,128)(2,1)S(1)}, bf16[32,2048]{1,0:T(8,128)(2,1)S(1)}, u32[]{:S(2)}, u32[]{:S(2)}) collective-permute-start(bf16[32,2048]{1,0:T(8,128)(2,1)S(1)} %get-tuple-element.42), channel_id=1, source_target_pairs={{0,1},{1,0},{2,3},{3,2},{4,5},{5,4},{6,7},{7,6},{8,9},{9,8},{10,11... | collective-permute-start | bytes 393224 | tf_op jit(solution)/shard_map/ppermute | solution.py:19
  2.9 8.1 %collective-permute-start.1 = (bf16[32,2048]{1,0:T(8,128)(2,1)S(1)}, bf16[32,2048]{1,0:T(8,128)(2,1)S(1)}, u32[]{:S(2)}, u32[]{:S(2)}) collective-permute-start(bf16[32,2048]{1,0:T(8,128)(2,1)S(1)} %get-tuple-element.43), channel_id=1, source_target_pairs={{0,3},{1,2},{2,1},{3,0},{4,7},{5,6},{6,5},{7,4},{8,11},{9,10},{10,... | collective-permute-start | bytes 393224 | tf_op jit(solution)/shard_map/ppermute | solution.py:19
  5.1 13.0 %slice-start = ((s8[8388608]{0:T(1024)(128)(4,1)}), s8[4194304]{0:T(1024)(128)(4,1)S(1)}, s32[]{:S(2)}) async-start(s8[8388608]{0:T(1024)(128)(4,1)} %bitcast), calls=%async_computation | async-start | bytes 8388608
  5.1 13.0 %slice-start.1 = ((s8[8388608]{0:T(1024)(128)(4,1)}), s8[4194304]{0:T(1024)(128)(4,1)S(1)}, s32[]{:S(2)}) async-start(s8[8388608]{0:T(1024)(128)(4,1)} %bitcast), calls=%async_computation.1 | async-start | bytes 8388608
  5.1 6.8 %collective-permute-start.2 = (bf16[32,2048]{1,0:T(8,128)(2,1)S(1)}, bf16[32,2048]{1,0:T(8,128)(2,1)S(1)}, u32[]{:S(2)}, u32[]{:S(2)}) collective-permute-start(bf16[32,2048]{1,0:T(8,128)(2,1)S(1)} %get-tuple-element.44), channel_id=1, source_target_pairs={{0,2},{1,3},{2,0},{3,1},{4,6},{5,7},{6,4},{7,5},{8,10},{9,11},{10,... | collective-permute-start | bytes 393224 | tf_op jit(solution)/shard_map/ppermute | solution.py:19
  12.6 7.0 %collective-permute-start.6 = (f16[144,256]{1,0:T(8,128)(2,1)S(1)}, f16[144,256]{1,0:T(8,128)(2,1)S(1)}, u32[]{:S(2)}, u32[]{:S(2)}) collective-permute-start(f16[144,256]{1,0:T(8,128)(2,1)S(1)} %convert_element_type.50), channel_id=1, source_target_pairs={{0,2},{1,3},{2,0},{3,1},{4,6},{5,7},{6,4},{7,5},{8,10},{9,11},{10,... | collective-permute-start | bytes 221192 | tf_op jit(solution)/shard_map/ppermute | solution.py:19
  14.4 5.6 %collective-permute-start.5 = (f16[144,256]{1,0:T(8,128)(2,1)S(1)}, f16[144,256]{1,0:T(8,128)(2,1)S(1)}, u32[]{:S(2)}, u32[]{:S(2)}) collective-permute-start(f16[144,256]{1,0:T(8,128)(2,1)S(1)} %convert_element_type.50), channel_id=1, source_target_pairs={{0,3},{1,2},{2,1},{3,0},{4,7},{5,6},{6,5},{7,4},{8,11},{9,10},{10,... | collective-permute-start | bytes 221192 | tf_op jit(solution)/shard_map/ppermute | solution.py:19
  15.9 4.9 %collective-permute-start.4 = (f16[144,256]{1,0:T(8,128)(2,1)S(1)}, f16[144,256]{1,0:T(8,128)(2,1)S(1)}, u32[]{:S(2)}, u32[]{:S(2)}) collective-permute-start(f16[144,256]{1,0:T(8,128)(2,1)S(1)} %convert_element_type.50), channel_id=1, source_target_pairs={{0,1},{1,0},{2,3},{3,2},{4,5},{5,4},{6,7},{7,6},{8,9},{9,8},{10,11... | collective-permute-start | bytes 221192 | tf_op jit(solution)/shard_map/ppermute | solution.py:19
  16.2 6.2 %collective-permute-start.3 = (f16[288,256]{1,0:T(8,128)(2,1)S(1)}, f16[288,256]{1,0:T(8,128)(2,1)S(1)}, u32[]{:S(2)}, u32[]{:S(2)}) collective-permute-start(f16[288,256]{1,0:T(8,128)(2,1)S(1)} %convert_element_type.48), channel_id=1, source_target_pairs={{0,1},{1,0},{2,3},{3,2},{4,5},{5,4},{6,7},{7,6},{8,9},{9,8},{10,11... | collective-permute-start | bytes 442376 | tf_op jit(solution)/shard_map/ppermute | solution.py:19
  20.9 1.5 %collective-permute-start.7 = (f32[128,256]{1,0:T(8,128)S(1)}, f32[128,256]{1,0:T(8,128)S(1)}, u32[]{:S(2)}, u32[]{:S(2)}) collective-permute-start(f32[128,256]{1,0:T(8,128)S(1)} %shard_map.77.own), channel_id=1, source_target_pairs={{0,4},{4,0},{8,12},{12,8},{16,20},{20,16},{24,28},{28,24},{32,36},... | collective-permute-start | bytes 393224 | tf_op jit(solution)/shard_map/ppermute | solution.py:19
  22.7 8.0 %collective-permute-start.11 = (f16[144,256]{1,0:T(8,128)(2,1)S(1)}, f16[144,256]{1,0:T(8,128)(2,1)S(1)}, u32[]{:S(2)}, u32[]{:S(2)}) collective-permute-start(f16[144,256]{1,0:T(8,128)(2,1)S(1)} %convert_element_type.58), channel_id=1, source_target_pairs={{0,3},{1,2},{2,1},{3,0},{4,7},{5,6},{6,5},{7,4},{8,11},{9,10},{10,... | collective-permute-start | bytes 221192 | tf_op jit(solution)/shard_map/ppermute | solution.py:19
  24.3 7.1 %collective-permute-start.10 = (f16[144,256]{1,0:T(8,128)(2,1)S(1)}, f16[144,256]{1,0:T(8,128)(2,1)S(1)}, u32[]{:S(2)}, u32[]{:S(2)}) collective-permute-start(f16[144,256]{1,0:T(8,128)(2,1)S(1)} %convert_element_type.54), channel_id=1, source_target_pairs={{0,24},{4,28},{8,16},{12,20},{16,8},{20,12},{24,0},{28,4},{32,56},... | collective-permute-start | bytes 221192 | tf_op jit(solution)/shard_map/ppermute | solution.py:19
  28.3 5.9 %collective-permute-start.9 = (f16[144,256]{1,0:T(8,128)(2,1)S(1)}, f16[144,256]{1,0:T(8,128)(2,1)S(1)}, u32[]{:S(2)}, u32[]{:S(2)}) collective-permute-start(f16[144,256]{1,0:T(8,128)(2,1)S(1)} %convert_element_type.54), channel_id=1, source_target_pairs={{0,16},{4,20},{8,24},{12,28},{16,0},{20,4},{24,8},{28,12},{32,48},... | collective-permute-start | bytes 221192 | tf_op jit(solution)/shard_map/ppermute | solution.py:19
  28.3 5.9 %collective-permute-start.8 = (f16[144,256]{1,0:T(8,128)(2,1)S(1)}, f16[144,256]{1,0:T(8,128)(2,1)S(1)}, u32[]{:S(2)}, u32[]{:S(2)}) collective-permute-start(f16[144,256]{1,0:T(8,128)(2,1)S(1)} %convert_element_type.54), channel_id=1, source_target_pairs={{0,8},{4,12},{8,0},{12,4},{16,24},{20,28},{24,16},{28,20},{32,40},... | collective-permute-start | bytes 221192 | tf_op jit(solution)/shard_map/ppermute | solution.py:19
  34.7 6.4 %collective-permute-start.14 = (f16[144,256]{1,0:T(8,128)(2,1)S(1)}, f16[144,256]{1,0:T(8,128)(2,1)S(1)}, u32[]{:S(2)}, u32[]{:S(2)}) collective-permute-start(f16[144,256]{1,0:T(8,128)(2,1)S(1)} %convert_element_type.60), channel_id=1, source_target_pairs={{0,96},{4,100},{8,104},{12,108},{16,112},{20,116},{24,120},{28,124... | collective-permute-start | bytes 221192 | tf_op jit(solution)/shard_map/ppermute | solution.py:19
  37.6 5.9 %collective-permute-start.13 = (f16[144,256]{1,0:T(8,128)(2,1)S(1)}, f16[144,256]{1,0:T(8,128)(2,1)S(1)}, u32[]{:S(2)}, u32[]{:S(2)}) collective-permute-start(f16[144,256]{1,0:T(8,128)(2,1)S(1)} %convert_element_type.60), channel_id=1, source_target_pairs={{0,64},{4,68},{8,72},{12,76},{16,80},{20,84},{24,88},{28,92},{32,9... | collective-permute-start | bytes 221192 | tf_op jit(solution)/shard_map/ppermute | solution.py:19
  38.4 5.1 %collective-permute-start.12 = (f16[144,256]{1,0:T(8,128)(2,1)S(1)}, f16[144,256]{1,0:T(8,128)(2,1)S(1)}, u32[]{:S(2)}, u32[]{:S(2)}) collective-permute-start(f16[144,256]{1,0:T(8,128)(2,1)S(1)} %convert_element_type.60), channel_id=1, source_target_pairs={{0,32},{4,36},{8,40},{12,44},{16,48},{20,52},{24,56},{28,60},{32,0... | collective-permute-start | bytes 221192 | tf_op jit(solution)/shard_map/ppermute | solution.py:19
  44.5 5.0 %collective-permute-start.16 = (bf16[32,2048]{1,0:T(8,128)(2,1)S(1)}, bf16[32,2048]{1,0:T(8,128)(2,1)S(1)}, u32[]{:S(2)}, u32[]{:S(2)}) collective-permute-start(bf16[32,2048]{1,0:T(8,128)(2,1)S(1)} %get-tuple-element.75), channel_id=1, source_target_pairs={{0,1},{1,0},{2,3},{3,2},{4,5},{5,4},{6,7},{7,6},{8,9},{9,8},{10,11... | collective-permute-start | bytes 393224 | tf_op jit(solution)/shard_map/ppermute | solution.py:19
  44.9 6.2 %collective-permute-start.17 = (bf16[32,2048]{1,0:T(8,128)(2,1)S(1)}, bf16[32,2048]{1,0:T(8,128)(2,1)S(1)}, u32[]{:S(2)}, u32[]{:S(2)}) collective-permute-start(bf16[32,2048]{1,0:T(8,128)(2,1)S(1)} %get-tuple-element.76), channel_id=1, source_target_pairs={{0,3},{1,2},{2,1},{3,0},{4,7},{5,6},{6,5},{7,4},{8,11},{9,10},{10,... | collective-permute-start | bytes 393224 | tf_op jit(solution)/shard_map/ppermute | solution.py:19
  46.4 6.5 %collective-permute-start.15 = (bf16[32,2048]{1,0:T(8,128)(2,1)S(1)}, bf16[32,2048]{1,0:T(8,128)(2,1)S(1)}, u32[]{:S(2)}, u32[]{:S(2)}) collective-permute-start(bf16[32,2048]{1,0:T(8,128)(2,1)S(1)} %get-tuple-element.73), channel_id=1, source_target_pairs={{0,2},{1,3},{2,0},{3,1},{4,6},{5,7},{6,4},{7,5},{8,10},{9,11},{10,... | collective-permute-start | bytes 393224 | tf_op jit(solution)/shard_map/ppermute | solution.py:19

commit v4 on v3

--- a/solution.py
+++ b/solution.py
@@ -67,6 +67,20 @@
 
 def shape(*dims, dtype=F32):
     return jax.ShapeDtypeStruct(dims, dtype)
+
+
+def line(message, axis, step, beside=None):
+    leaves, group = lax.axis_size("leaf"), lax.axis_size("rhs")
+    if axis == "leaf":
+        pairs = [(i, i ^ step * (1 + (i & 1))) for i in range(leaves)]
+    else:
+        axis = ("leaf", "rhs")
+        pairs = [(i * group + j, i * group + (j ^ (1 + (i & 1)))) for i in range(leaves) for j in range(group)]
+    mine = lax.ppermute(message, axis, pairs)
+    third = swap(message, "leaf" if axis == "leaf" else "rhs", 3 * step)
+    if beside is not None:
+        mine, beside = lax.optimization_barrier((mine, beside))
+    return [mine, swap(mine, "leaf", 1), third], beside
 
 
 def aligned(index, size):
@@ -127,47 +141,65 @@
         lower_b, uppers, couplings, sems = rest[9:]
         rhs_pos = lax.axis_index("rhs")
         node = lax.axis_index("leaf") + lax.axis_size("leaf")
-        copies = []
+        copies = {}
+
+        def start(name, source, target):
+            copies[name] = pltpu.make_async_copy(source, target, sems.at[len(copies)])
+            copies[name].start()
+
+        start("t", low_t_hbm.at[0], lower_t)
+        start("b", low_b_hbm.at[0], lower_b)
         for slot, (height, mask) in enumerate(PICKS):
-            copies.append((up_t_hbm.at[((node >> height) ^ mask) - 2], uppers.at[slot]))
+            start(slot, up_t_hbm.at[((node >> height) ^ mask) - 2], uppers.at[slot])
         for height in range(COUPLED):
-            copies.append((up_b_hbm.at[(node >> (height + 1)) - 1], couplings.at[height]))
-        copies += [(low_t_hbm.at[0], lower_t), (low_b_hbm.at[0], lower_b), (basis_hbm.at[0], basis)]
-        copies = [pltpu.make_async_copy(*pair_, sems.at[i]) for i, pair_ in enumerate(copies)]
-        for copy in copies:
-            copy.start()
-        for copy in copies:
-            copy.wait()
+            start(n_up + height, up_b_hbm.at[(node >> (height + 1)) - 1], couplings.at[height])
+        start("basis", basis_hbm.at[0], basis)
+
+        def upper(slot):
+            copies[slot].wait()
+            return uppers[slot]
+
+        def coupling(height):
+            copies[n_up + height].wait()
+            return couplings[height]
 
         def put(high_ref, low_ref, slot, value):
             high, low = split(value)
-            high_ref[slot * rank : (slot + 1) * rank, :] = high
-            low_ref[slot * rank : (slot + 1) * rank, :] = low
-
-        own2, sib2 = uppers[0], uppers[1]
-        level3 = [uppers[slot] for slot in range(2, 6)]
-        own4, sib4, own5, third5, fourth5 = [uppers[slot] for slot in range(6, 11)]
-        pair[:rank, :] = own2
-        pair[rank:, :] = sib2
-        for slot, matrix in enumerate(level3):
-            put(up_high, up_low, slot, dot(matrix, own4 if slot < 2 else sib4))
+            high_ref[aligned(slot, rank), :] = high
+            low_ref[aligned(slot, rank), :] = low
+
+        first = node & 1
+        second = 1 - first
+
+        copies["t"].wait()
+        copies["b"].wait()
         put(acc_high, acc_low, 0, oriented(lower_b[0], rhs_pos & 1).astype(F32))
         down = split(transposed(lower_t[0]).astype(F32))
         put(acc_high, acc_low, 1, times(oriented(lower_b[1], rhs_pos >> 1 & 1), down))
         down = split(times(transposed(lower_t[1]), down))
-        put(acc_high, acc_low, 2, times(oriented(couplings[0], node & 1), down))
+        own2 = upper(0)
+        pair[:rank, :] = own2
+        pair[rank:, :] = upper(1)
+        level3 = [upper(slot) for slot in range(2, 6)]
+        own4, sib4, own5, third5, fourth5 = [upper(slot) for slot in range(6, 11)]
+        put(acc_high, acc_low, 2, times(oriented(coupling(0), node & 1), down))
         down = split(times(transposed(own2), down))
-        put(acc_high, acc_low, 3, times(oriented(couplings[1], node >> 1 & 1), down))
+        put(acc_high, acc_low, 3 + first, times(oriented(coupling(1), node >> 1 & 1), down))
         down = split(times(transposed(level3[0]), down))
-        across = split(times(oriented(couplings[2], node >> 2 & 1), down))
-        put(acc_high, acc_low, 4, times(level3[2], across))
+        across = split(times(oriented(coupling(2), node >> 2 & 1), down))
+        put(acc_high, acc_low, 3 + second, times(level3[2], across))
         put(acc_high, acc_low, 5, times(level3[3], across))
         down = split(times(transposed(own4), down))
-        put(top_high, top_low, 0, times(oriented(couplings[3], node >> 3 & 1), down))
+        put(top_high, top_low, first, times(oriented(coupling(3), node >> 3 & 1), down))
         down = split(times(transposed(own5), down))
-        across = split(times(oriented(couplings[4], node >> 4 & 1), down))
-        put(top_high, top_low, 1, times(third5, across))
+        across = split(times(oriented(coupling(4), node >> 4 & 1), down))
+        put(top_high, top_low, second, times(third5, across))
         put(top_high, top_low, 2, times(fourth5, across))
+        put(up_high, up_low, 0, dot(level3[0], own4))
+        put(up_high, up_low, 1 + first, dot(level3[1], own4))
+        put(up_high, up_low, 1 + second, dot(level3[2], sib4))
+        put(up_high, up_low, 3, dot(level3[3], sib4))
+        copies["basis"].wait()
 
     stacked = [shape(n * rank, rank, dtype=BF16) for n in (2, 4, 4, 6, 6, 3, 3)]
     return call(
@@ -292,11 +324,12 @@
         in_specs=[VMEM] * 5,
         out_specs=[VMEM] * 3,
     )
-    chip_msg, cols = lax.optimization_barrier((chip_msg.astype(F16), cols))
-    chips = [swap(chip_msg, "leaf", 2 * mask).astype(F32) for mask in (1, 2, 3)]
-    cousin = swap(cousin_msg.astype(F16), "rhs", 3).astype(F32)
-    near_right = near_half(cols, 1)
-    chips, cousin, near_right = lax.optimization_barrier((chips, cousin, near_right))
+    chip_msg = chip_msg.astype(F16)
+    chips, _ = line(chip_msg, "leaf", 2)
+    chips = [got.astype(F32) for got in chips]
+
+    cousin_msg = cousin_msg.astype(F16)
+    cousin = swap(cousin_msg, "rhs", 3).astype(F32)
 
     def line_body(own, a, b, c, high, low, out):
         value = jnp.concatenate([own[...]] + [decode(ref) for ref in (a, b, c)], axis=1)
@@ -311,9 +344,7 @@
         in_specs=[VMEM] * 6,
         out_specs=VMEM,
     )
-    line_msg = line_msg.astype(F16)
-    lines = [swap(line_msg, "leaf", 8 * mask).astype(F32) for mask in (1, 2, 3)]
-
+    line_msg, cols = lax.optimization_barrier((line_msg.astype(F16), cols))
     def partial_body(sibling, others, core, z1, z2, z3, high, low, out):
         value = jnp.concatenate(
             [decode(sibling.at[: total + EXTRA, :]), decode(others), core[...]]
@@ -332,6 +363,12 @@
         out_specs=VMEM,
     )
 
+    lines, _ = line(line_msg, "leaf", 8)
+    lines = [got.astype(F32) for got in lines]
+    near_right = near_half(cols, 1)
+
+    out_masks = (0, 2, 1, 3)
+
     def last_body(part_ref, a, b, c, high, low, basis_ref, left, right, own, first, second, third, inner):
         position = lax.axis_index("rhs")
         value = jnp.concatenate([decode(ref) for ref in (a, b, c)], axis=1)
@@ -340,7 +377,8 @@
         far = lax.dot_general(
             coeffs.astype(BF16), basis_ref[...], (((1,), (1,)), ((), ())), preferred_element_type=F32
         )
-        for slot, ref in enumerate((own, first, second, third)):
+        for mask, ref in zip(out_masks, (own, first, second, third)):
+            slot = masks.index(mask)
             rows = slice(slot * part, (slot + 1) * part)
             ref[:, : leaf // 2] = (left[rows, :] + far[rows, : leaf // 2]).astype(ref.dtype)
             ref[:, leaf // 2 :] = (right[rows, :] + far[rows, leaf // 2 :]).astype(ref.dtype)
@@ -356,7 +394,7 @@
         out_specs=[VMEM] * 4,
         scratch_shapes=[pltpu.VMEM((total, rank), F32)],
     )
-    blocks = [swap(block, "rhs", mask) for block, mask in zip(blocks, masks[1:])]
+    blocks = [swap(block, "rhs", mask) for block, mask in zip(blocks, out_masks[1:])]
 
     def join_body(count, slots, *refs):
         blocks, out, wide, sems = refs[:count], refs[-3], refs[-2], refs[-1]
@@ -364,7 +402,7 @@
         copies = []
         for i, (block, slot) in enumerate(zip(blocks, slots)):
             wide[i] = block[...].astype(F32)
-            target = out.at[:, aligned(position ^ masks[slot], leaf)]
+            target = out.at[:, aligned(position ^ out_masks[slot], leaf)]
             copies.append(pltpu.make_async_copy(wide.at[i], target, sems.at[i]))
             copies[-1].start()
         for copy in copies:

time: 53.8 us -> 50.7 us (0.942)
  waiting for transfers between devices: 14.4 us -> 10.7 us
  starting transfers between devices: 24.9 us -> 26 us
    ppermute x18 -> x16, waiting for transfers between devices: 14.4 us -> 10.7 us  [swap(): return lax.ppermute(value, axis, pairs)]
    ppermute x0 -> x2, starting transfers between devices: none -> 3.6 us  [line(): mine = lax.ppermute(message, axis, pairs)]
    ppermute x18 -> x16, starting transfers between devices: 24.9 us -> 22.4 us  [swap(): return lax.ppermute(value, axis, pairs)]
  transfers between devices with their start and end apart: 18 -> 18, of which waited for: 11 -> 10; matrix products, arithmetic and copies ran while one was open for 0% -> 0% of each run, Pallas kernels for 18% -> 19%
where the time goes in v4:
time: 50.7 us; the launch traced here: 50.6 us
  starting transfers between devices  26 us (51%)
  Pallas kernels  13.4 us (26%)
  waiting for transfers between devices  10.7 us (21%)
    ppermute x16, starting transfers between devices, swap(): return lax.ppermute(value, axis, pairs)  22.4 us
    pallas_call x12, Pallas kernels, call(): pl.pallas_call(body, out_shape=outs, compiler_params=pltpu.CompilerParams...  13.4 us
    ppermute x16, waiting for transfers between devices, swap(): return lax.ppermute(value, axis, pairs)  10.7 us
    ppermute x2, starting transfers between devices, line(): mine = lax.ppermute(message, axis, pairs)  3.6 us
  transfers between devices with their start and end apart: 18, of which 10 were waited for; matrix products, arithmetic and copies ran while one was open for 0% of the time, Pallas kernels for 19%

profile of v4, /device:TPU:0, one launch (start us, length us, event | category | flops | bytes accessed | tf_op | source)
XLA Modules:
  0.0 50.6 jit_solution(8010776631055493156)
XLA Ops:
  0.0 1.1 %shard_map.73 = (bf16[32,2048]{1,0:T(8,128)(2,1)S(1)}, bf16[32,2048]{1,0:T(8,128)(2,1)S(1)}, bf16[32,2048]{1,0:T(8,128)(2,1)S(1)}, bf16[32,2048]{1,0:T(8,128)(2,1)S(1)}) custom-call(bf16[32,8192]{1,0:T(8,128)(2,1)} %source.1), custom_call_target="tpu_custom_call" | custom-call | bytes 1048576 | tf_op jit(solution)/shard_map/pallas_call | solution.py:59
  1.1 1.7 %collective-permute-start = (bf16[32,2048]{1,0:T(8,128)(2,1)S(1)}, bf16[32,2048]{1,0:T(8,128)(2,1)S(1)}, u32[]{:S(2)}, u32[]{:S(2)}) collective-permute-start(bf16[32,2048]{1,0:T(8,128)(2,1)S(1)} %get-tuple-element.37), channel_id=1, source_target_pairs={{0,1},{1,0},{2,3},{3,2},{4,5},{5,4},{6,7},{7,6},{8,9},{9,8},{10,11... | collective-permute-start | bytes 393224 | tf_op jit(solution)/shard_map/ppermute | solution.py:19
  2.9 2.2 %collective-permute-start.1 = (bf16[32,2048]{1,0:T(8,128)(2,1)S(1)}, bf16[32,2048]{1,0:T(8,128)(2,1)S(1)}, u32[]{:S(2)}, u32[]{:S(2)}) collective-permute-start(bf16[32,2048]{1,0:T(8,128)(2,1)S(1)} %get-tuple-element.38), channel_id=1, source_target_pairs={{0,3},{1,2},{2,1},{3,0},{4,7},{5,6},{6,5},{7,4},{8,11},{9,10},{10,... | collective-permute-start | bytes 393224 | tf_op jit(solution)/shard_map/ppermute | solution.py:19
  5.1 0.7 %collective-permute-start.2 = (bf16[32,2048]{1,0:T(8,128)(2,1)S(1)}, bf16[32,2048]{1,0:T(8,128)(2,1)S(1)}, u32[]{:S(2)}, u32[]{:S(2)}) collective-permute-start(bf16[32,2048]{1,0:T(8,128)(2,1)S(1)} %get-tuple-element.39), channel_id=1, source_target_pairs={{0,2},{1,3},{2,0},{3,1},{4,6},{5,7},{6,4},{7,5},{8,10},{9,11},{10,... | collective-permute-start | bytes 393224 | tf_op jit(solution)/shard_map/ppermute | solution.py:19
  5.8 4.7 %shard_map.74 = (bf16[2048,256]{1,0:T(8,128)(2,1)S(1)}, bf16[2,256,256]{2,1,0:T(8,128)(2,1)S(1)}, bf16[512,256]{1,0:T(8,128)(2,1)S(1)}, bf16[1024,256]{1,0:T(8,1...) custom-call(bf16[1,2048,256]{2,1,0:T(8,128)(2,1)} %basis_hbm.1, ...), custom_call_target="tpu_custom_call" | custom-call | flops 1140850688 | bytes 4194304 | tf_op jit(solution)/shard_map/pallas_call | solution.py:59
  10.6 1.3 %collective-permute-done.2.third = bf16[32,2048]{1,0:T(8,128)(2,1)S(1)} collective-permute-done((bf16[32,2048]{1,0:T(8,128)(2,1)S(1)}, bf16[32,2048]{1,0:T(8,128)(2,1)S(1)}, u32[]{:S(2)}, u32[]{:S(2)}) %collective-permute-start.2) | collective-permute-done | bytes 131104 | tf_op jit(solution)/shard_map/ppermute | solution.py:19
  11.9 0.7 %shard_map.75 = (bf16[128,2048]{1,0:T(8,128)(2,1)S(1)}, f32[144,256]{1,0:T(8,128)S(1)}, f32[288,256]{1,0:T(8,128)S(1)}, f32[128,256]{1,0:T(8,128)S(1)}, f32[128,256]{1,0:T(8,128)S(1)}) custom-call(bf16[32,2048]{1,0:T(8,128)(2,1)S(1)} %get-tuple-element.36.own, bf16[32,2048]{1,0:T(8,128)(2,1)S(1)} %collective-permute-done.first, ...), custom_call_target="tpu_custom_call" | custom-call | flops 134217728 | bytes 2097152 | tf_op jit(solution)/shard_map/pallas_call | solution.py:59
  12.6 1.8 %collective-permute-start.6 = (f16[144,256]{1,0:T(8,128)(2,1)S(1)}, f16[144,256]{1,0:T(8,128)(2,1)S(1)}, u32[]{:S(2)}, u32[]{:S(2)}) collective-permute-start(f16[144,256]{1,0:T(8,128)(2,1)S(1)} %convert_element_type.50), channel_id=1, source_target_pairs={{0,2},{1,3},{2,0},{3,1},{4,6},{5,7},{6,4},{7,5},{8,10},{9,11},{10,... | collective-permute-start | bytes 221192 | tf_op jit(solution)/shard_map/ppermute | solution.py:19
  14.4 1.3 %collective-permute-start.5 = (f16[144,256]{1,0:T(8,128)(2,1)S(1)}, f16[144,256]{1,0:T(8,128)(2,1)S(1)}, u32[]{:S(2)}, u32[]{:S(2)}) collective-permute-start(f16[144,256]{1,0:T(8,128)(2,1)S(1)} %convert_element_type.50), channel_id=1, source_target_pairs={{0,3},{1,2},{2,1},{3,0},{4,7},{5,6},{6,5},{7,4},{8,11},{9,10},{10,... | collective-permute-start | bytes 221192 | tf_op jit(solution)/shard_map/ppermute | solution.py:19
  15.7 0.5 collective-permute-start.4
  16.2 1.6 %collective-permute-start.3 = (f16[288,256]{1,0:T(8,128)(2,1)S(1)}, f16[288,256]{1,0:T(8,128)(2,1)S(1)}, u32[]{:S(2)}, u32[]{:S(2)}) collective-permute-start(f16[288,256]{1,0:T(8,128)(2,1)S(1)} %convert_element_type.48), channel_id=1, source_target_pairs={{0,1},{1,0},{2,3},{3,2},{4,5},{5,4},{6,7},{7,6},{8,9},{9,8},{10,11... | collective-permute-start | bytes 442376 | tf_op jit(solution)/shard_map/ppermute | solution.py:19
  17.8 1.5 %shard_map.76.left = f32[128,1024]{1,0:T(8,128)S(1)} custom-call(bf16[128,2048]{1,0:T(8,128)(2,1)S(1)} %get-tuple-element.62.cols_ref, bf16[1,2048,2048]{2,1,0:T(8,128)(2,1)S(1)} %bitcast.1), custom_call_target="tpu_custom_call" | custom-call | flops 536870912 | bytes 4980736 | tf_op jit(solution)/shard_map/pallas_call | solution.py:59
  19.4 0.6 %collective-permute-done.5 = f16[144,256]{1,0:T(8,128)(2,1)S(1)} collective-permute-done((f16[144,256]{1,0:T(8,128)(2,1)S(1)}, f16[144,256]{1,0:T(8,128)(2,1)S(1)}, u32[]{:S(2)}, u32[]{:S(2)}) %collective-permute-start.5) | collective-permute-done | bytes 73760 | tf_op jit(solution)/shard_map/ppermute | solution.py:19
  20.5 1.4 %collective-permute-done.3 = f16[288,256]{1,0:T(8,128)(2,1)S(1)} collective-permute-done((f16[288,256]{1,0:T(8,128)(2,1)S(1)}, f16[288,256]{1,0:T(8,128)(2,1)S(1)}, u32[]{:S(2)}, u32[]{:S(2)}) %collective-permute-start.3) | collective-permute-done | bytes 147488 | tf_op jit(solution)/shard_map/ppermute | solution.py:19
  22.2 2.0 %collective-permute-start.9 = (f16[144,256]{1,0:T(8,128)(2,1)S(1)}, f16[144,256]{1,0:T(8,128)(2,1)S(1)}, u32[]{:S(2)}, u32[]{:S(2)}) collective-permute-start(f16[144,256]{1,0:T(8,128)(2,1)S(1)} %convert_element_type.56), channel_id=1, source_target_pairs={{0,8},{4,20},{8,0},{12,28},{16,24},{20,4},{24,16},{28,12},{32,40},... | collective-permute-start | bytes 221192 | tf_op jit(solution)/shard_map/ppermute | solution.py:79
  24.2 2.5 %collective-permute-start.11 = (f16[144,256]{1,0:T(8,128)(2,1)S(1)}, f16[144,256]{1,0:T(8,128)(2,1)S(1)}, u32[]{:S(2)}, u32[]{:S(2)}) collective-permute-start(f16[144,256]{1,0:T(8,128)(2,1)S(1)} %convert_element_type.56), channel_id=1, source_target_pairs={{0,24},{4,28},{8,16},{12,20},{16,8},{20,12},{24,0},{28,4},{32,56},... | collective-permute-start | bytes 221192 | tf_op jit(solution)/shard_map/ppermute | solution.py:19
  26.8 0.9 %collective-permute-start.10 = (f16[144,256]{1,0:T(8,128)(2,1)S(1)}, f16[144,256]{1,0:T(8,128)(2,1)S(1)}, u32[]{:S(2)}, u32[]{:S(2)}) collective-permute-start(f16[144,256]{1,0:T(8,128)(2,1)S(1)} %collective-permute-done.9), channel_id=1, source_target_pairs={{0,4},{4,0},{8,12},{12,8},{16,20},{20,16},{24,28},{28,24},{32,36},... | collective-permute-start | bytes 221192 | tf_op jit(solution)/shard_map/ppermute | solution.py:19
  27.7 2.0 %collective-permute-start.8 = (f16[144,256]{1,0:T(8,128)(2,1)S(1)}, f16[144,256]{1,0:T(8,128)(2,1)S(1)}, u32[]{:S(2)}, u32[]{:S(2)}) collective-permute-start(f16[144,256]{1,0:T(8,128)(2,1)S(1)} %convert_element_type.54), channel_id=1, source_target_pairs={{0,3},{1,2},{2,1},{3,0},{4,7},{5,6},{6,5},{7,4},{8,11},{9,10},{10,... | collective-permute-start | bytes 221192 | tf_op jit(solution)/shard_map/ppermute | solution.py:19
  30.4 1.6 %collective-permute-start.12 = (f16[144,256]{1,0:T(8,128)(2,1)S(1)}, f16[144,256]{1,0:T(8,128)(2,1)S(1)}, u32[]{:S(2)}, u32[]{:S(2)}) collective-permute-start(f16[144,256]{1,0:T(8,128)(2,1)S(1)} %convert_element_type.60), channel_id=1, source_target_pairs={{0,32},{4,68},{8,40},{12,76},{16,48},{20,84},{24,56},{28,92},{32,0... | collective-permute-start | bytes 221192 | tf_op jit(solution)/shard_map/ppermute | solution.py:79
  32.0 1.4 %collective-permute-done.8 = f16[144,256]{1,0:T(8,128)(2,1)S(1)} collective-permute-done((f16[144,256]{1,0:T(8,128)(2,1)S(1)}, f16[144,256]{1,0:T(8,128)(2,1)S(1)}, u32[]{:S(2)}, u32[]{:S(2)}) %collective-permute-start.8) | collective-permute-done | bytes 73760 | tf_op jit(solution)/shard_map/ppermute | solution.py:19
  33.4 2.8 %collective-permute-start.14 = (f16[144,256]{1,0:T(8,128)(2,1)S(1)}, f16[144,256]{1,0:T(8,128)(2,1)S(1)}, u32[]{:S(2)}, u32[]{:S(2)}) collective-permute-start(f16[144,256]{1,0:T(8,128)(2,1)S(1)} %convert_element_type.60), channel_id=1, source_target_pairs={{0,96},{4,100},{8,104},{12,108},{16,112},{20,116},{24,120},{28,124... | collective-permute-start | bytes 221192 | tf_op jit(solution)/shard_map/ppermute | solution.py:19
  36.2 0.5 shard_map.79.part_ref
  36.7 1.5 %shard_map.81.right = f32[128,1024]{1,0:T(8,128)S(1)} custom-call(bf16[128,2048]{1,0:T(8,128)(2,1)S(1)} %get-tuple-element.62.cols_ref, bf16[1,2048,2048]{2,1,0:T(8,128)(2,1)S(1)} %bitcast.1), custom_call_target="tpu_custom_call" | custom-call | flops 536870912 | bytes 4980736 | tf_op jit(solution)/shard_map/pallas_call | solution.py:59
  38.2 1.0 %collective-permute-done.14 = f16[144,256]{1,0:T(8,128)(2,1)S(1)} collective-permute-done((f16[144,256]{1,0:T(8,128)(2,1)S(1)}, f16[144,256]{1,0:T(8,128)(2,1)S(1)}, u32[]{:S(2)}, u32[]{:S(2)}) %collective-permute-start.14) | collective-permute-done | bytes 73760 | tf_op jit(solution)/shard_map/ppermute | solution.py:19
  39.2 1.0 %shard_map.82 = (f32[32,2048]{1,0:T(8,128)S(1)}, bf16[32,2048]{1,0:T(8,128)(2,1)S(1)}, bf16[32,2048]{1,0:T(8,128)(2,1)S(1)}, bf16[32,2048]{1,0:T(8,128)(2,1)S(1)}) custom-call(f32[128,256]{1,0:T(8,128)S(1)} %shard_map.79.part_ref, f32[144,256]{1,0:T(8,128)S(1)} %convert_element_type.61.a, f32[144,256]{1,0:T(8,128)S(1)} %convert_element_type.62.b, ...), custom_call_target="tpu_custom_call" | custom-call | flops 134217728 | bytes 4194304 | tf_op jit(solution)/shard_map/pallas_call | solution.py:59
  40.2 1.2 %collective-permute-start.16 = (bf16[32,2048]{1,0:T(8,128)(2,1)S(1)}, bf16[32,2048]{1,0:T(8,128)(2,1)S(1)}, u32[]{:S(2)}, u32[]{:S(2)}) collective-permute-start(bf16[32,2048]{1,0:T(8,128)(2,1)S(1)} %get-tuple-element.65), channel_id=1, source_target_pairs={{0,2},{1,3},{2,0},{3,1},{4,6},{5,7},{6,4},{7,5},{8,10},{9,11},{10,... | collective-permute-start | bytes 393224 | tf_op jit(solution)/shard_map/ppermute | solution.py:19
  41.4 1.7 %collective-permute-start.17 = (bf16[32,2048]{1,0:T(8,128)(2,1)S(1)}, bf16[32,2048]{1,0:T(8,128)(2,1)S(1)}, u32[]{:S(2)}, u32[]{:S(2)}) collective-permute-start(bf16[32,2048]{1,0:T(8,128)(2,1)S(1)} %get-tuple-element.66), channel_id=1, source_target_pairs={{0,1},{1,0},{2,3},{3,2},{4,5},{5,4},{6,7},{7,6},{8,9},{9,8},{10,11... | collective-permute-start | bytes 393224 | tf_op jit(solution)/shard_map/ppermute | solution.py:19
  43.1 1.3 %collective-permute-start.15 = (bf16[32,2048]{1,0:T(8,128)(2,1)S(1)}, bf16[32,2048]{1,0:T(8,128)(2,1)S(1)}, u32[]{:S(2)}, u32[]{:S(2)}) collective-permute-start(bf16[32,2048]{1,0:T(8,128)(2,1)S(1)} %get-tuple-element.63), channel_id=1, source_target_pairs={{0,3},{1,2},{2,1},{3,0},{4,7},{5,6},{6,5},{7,4},{8,11},{9,10},{10,... | collective-permute-start | bytes 393224 | tf_op jit(solution)/shard_map/ppermute | solution.py:19
  44.4 3.9 %collective-permute-done.16.refs_1_ = bf16[32,2048]{1,0:T(8,128)(2,1)S(1)} collective-permute-done((bf16[32,2048]{1,0:T(8,128)(2,1)S(1)}, bf16[32,2048]{1,0:T(8,128)(2,1)S(1)}, u32[]{:S(2)}, u32[]{:S(2)}) %collective-permute-start.16) | collective-permute-done | bytes 131104 | tf_op jit(solution)/shard_map/ppermute | solution.py:19
  48.3 0.6 %collective-permute-done.17.refs_2_ = bf16[32,2048]{1,0:T(8,128)(2,1)S(1)} collective-permute-done((bf16[32,2048]{1,0:T(8,128)(2,1)S(1)}, bf16[32,2048]{1,0:T(8,128)(2,1)S(1)}, u32[]{:S(2)}, u32[]{:S(2)}) %collective-permute-start.17) | collective-permute-done | bytes 131104 | tf_op jit(solution)/shard_map/ppermute | solution.py:19
  48.8 0.9 %shard_map.83.refs_1_ = f32[32,8192]{1,0:T(8,128)} custom-call(f32[32,2048]{1,0:T(8,128)S(1)} %get-tuple-element.64.refs_0_, bf16[32,2048]{1,0:T(8,128)(2,1)S(1)} %collective-permute-done.16.refs_1_, bf16[32,2048]{1,0:T(8,128)(2,1)S(1)} %collective-permute-done.17.refs_2_), custom_call_target="tpu_custom_call" | custom-call | bytes 1179648 | tf_op jit(solution)/shard_map/pallas_call | solution.py:59
  49.9 0.7 %shard_map.84 = f32[32,8192]{1,0:T(8,128)} custom-call(bf16[32,2048]{1,0:T(8,128)(2,1)S(1)} %collective-permute-done.15.refs_0_, f32[32,8192]{1,0:T(8,128)} %shard_map.83.refs_1_), custom_call_target="tpu_custom_call", output_to_operand_aliasing={{}: (1, {})} | custom-call | bytes 393216 | tf_op jit(solution)/shard_map/pallas_call | solution.py:59
  (37 shorter events, 1.6 us)
Async XLA Ops:
  1.1 9.4 %collective-permute-start = (bf16[32,2048]{1,0:T(8,128)(2,1)S(1)}, bf16[32,2048]{1,0:T(8,128)(2,1)S(1)}, u32[]{:S(2)}, u32[]{:S(2)}) collective-permute-start(bf16[32,2048]{1,0:T(8,128)(2,1)S(1)} %get-tuple-element.37), channel_id=1, source_target_pairs={{0,1},{1,0},{2,3},{3,2},{4,5},{5,4},{6,7},{7,6},{8,9},{9,8},{10,11... | collective-permute-start | bytes 393224 | tf_op jit(solution)/shard_map/ppermute | solution.py:19
  2.9 7.7 %collective-permute-start.1 = (bf16[32,2048]{1,0:T(8,128)(2,1)S(1)}, bf16[32,2048]{1,0:T(8,128)(2,1)S(1)}, u32[]{:S(2)}, u32[]{:S(2)}) collective-permute-start(bf16[32,2048]{1,0:T(8,128)(2,1)S(1)} %get-tuple-element.38), channel_id=1, source_target_pairs={{0,3},{1,2},{2,1},{3,0},{4,7},{5,6},{6,5},{7,4},{8,11},{9,10},{10,... | collective-permute-start | bytes 393224 | tf_op jit(solution)/shard_map/ppermute | solution.py:19
  5.1 12.8 %slice-start = ((s8[8388608]{0:T(1024)(128)(4,1)}), s8[4194304]{0:T(1024)(128)(4,1)S(1)}, s32[]{:S(2)}) async-start(s8[8388608]{0:T(1024)(128)(4,1)} %bitcast), calls=%async_computation | async-start | bytes 8388608
  5.1 12.8 %slice-start.1 = ((s8[8388608]{0:T(1024)(128)(4,1)}), s8[4194304]{0:T(1024)(128)(4,1)S(1)}, s32[]{:S(2)}) async-start(s8[8388608]{0:T(1024)(128)(4,1)} %bitcast), calls=%async_computation.1 | async-start | bytes 8388608
  5.1 6.8 %collective-permute-start.2 = (bf16[32,2048]{1,0:T(8,128)(2,1)S(1)}, bf16[32,2048]{1,0:T(8,128)(2,1)S(1)}, u32[]{:S(2)}, u32[]{:S(2)}) collective-permute-start(bf16[32,2048]{1,0:T(8,128)(2,1)S(1)} %get-tuple-element.39), channel_id=1, source_target_pairs={{0,2},{1,3},{2,0},{3,1},{4,6},{5,7},{6,4},{7,5},{8,10},{9,11},{10,... | collective-permute-start | bytes 393224 | tf_op jit(solution)/shard_map/ppermute | solution.py:19
  12.6 6.8 %collective-permute-start.6 = (f16[144,256]{1,0:T(8,128)(2,1)S(1)}, f16[144,256]{1,0:T(8,128)(2,1)S(1)}, u32[]{:S(2)}, u32[]{:S(2)}) collective-permute-start(f16[144,256]{1,0:T(8,128)(2,1)S(1)} %convert_element_type.50), channel_id=1, source_target_pairs={{0,2},{1,3},{2,0},{3,1},{4,6},{5,7},{6,4},{7,5},{8,10},{9,11},{10,... | collective-permute-start | bytes 221192 | tf_op jit(solution)/shard_map/ppermute | solution.py:19
  14.4 5.7 %collective-permute-start.5 = (f16[144,256]{1,0:T(8,128)(2,1)S(1)}, f16[144,256]{1,0:T(8,128)(2,1)S(1)}, u32[]{:S(2)}, u32[]{:S(2)}) collective-permute-start(f16[144,256]{1,0:T(8,128)(2,1)S(1)} %convert_element_type.50), channel_id=1, source_target_pairs={{0,3},{1,2},{2,1},{3,0},{4,7},{5,6},{6,5},{7,4},{8,11},{9,10},{10,... | collective-permute-start | bytes 221192 | tf_op jit(solution)/shard_map/ppermute | solution.py:19
  15.7 4.6 %collective-permute-start.4 = (f16[144,256]{1,0:T(8,128)(2,1)S(1)}, f16[144,256]{1,0:T(8,128)(2,1)S(1)}, u32[]{:S(2)}, u32[]{:S(2)}) collective-permute-start(f16[144,256]{1,0:T(8,128)(2,1)S(1)} %convert_element_type.50), channel_id=1, source_target_pairs={{0,1},{1,0},{2,3},{3,2},{4,5},{5,4},{6,7},{7,6},{8,9},{9,8},{10,11... | collective-permute-start | bytes 221192 | tf_op jit(solution)/shard_map/ppermute | solution.py:19
  16.2 5.7 %collective-permute-start.3 = (f16[288,256]{1,0:T(8,128)(2,1)S(1)}, f16[288,256]{1,0:T(8,128)(2,1)S(1)}, u32[]{:S(2)}, u32[]{:S(2)}) collective-permute-start(f16[288,256]{1,0:T(8,128)(2,1)S(1)} %convert_element_type.48), channel_id=1, source_target_pairs={{0,1},{1,0},{2,3},{3,2},{4,5},{5,4},{6,7},{7,6},{8,9},{9,8},{10,11... | collective-permute-start | bytes 442376 | tf_op jit(solution)/shard_map/ppermute | solution.py:19
  20.4 1.5 %collective-permute-start.7 = (f32[128,256]{1,0:T(8,128)S(1)}, f32[128,256]{1,0:T(8,128)S(1)}, u32[]{:S(2)}, u32[]{:S(2)}) collective-permute-start(f32[128,256]{1,0:T(8,128)S(1)} %shard_map.77.own), channel_id=1, source_target_pairs={{0,4},{4,0},{8,12},{12,8},{16,20},{20,16},{24,28},{28,24},{32,36},... | collective-permute-start | bytes 393224 | tf_op jit(solution)/shard_map/ppermute | solution.py:19
  22.2 4.5 %collective-permute-start.9 = (f16[144,256]{1,0:T(8,128)(2,1)S(1)}, f16[144,256]{1,0:T(8,128)(2,1)S(1)}, u32[]{:S(2)}, u32[]{:S(2)}) collective-permute-start(f16[144,256]{1,0:T(8,128)(2,1)S(1)} %convert_element_type.56), channel_id=1, source_target_pairs={{0,8},{4,20},{8,0},{12,28},{16,24},{20,4},{24,16},{28,12},{32,40},... | collective-permute-start | bytes 221192 | tf_op jit(solution)/shard_map/ppermute | solution.py:79
  24.2 5.7 %collective-permute-start.11 = (f16[144,256]{1,0:T(8,128)(2,1)S(1)}, f16[144,256]{1,0:T(8,128)(2,1)S(1)}, u32[]{:S(2)}, u32[]{:S(2)}) collective-permute-start(f16[144,256]{1,0:T(8,128)(2,1)S(1)} %convert_element_type.56), channel_id=1, source_target_pairs={{0,24},{4,28},{8,16},{12,20},{16,8},{20,12},{24,0},{28,4},{32,56},... | collective-permute-start | bytes 221192 | tf_op jit(solution)/shard_map/ppermute | solution.py:19
  26.8 3.2 %collective-permute-start.10 = (f16[144,256]{1,0:T(8,128)(2,1)S(1)}, f16[144,256]{1,0:T(8,128)(2,1)S(1)}, u32[]{:S(2)}, u32[]{:S(2)}) collective-permute-start(f16[144,256]{1,0:T(8,128)(2,1)S(1)} %collective-permute-done.9), channel_id=1, source_target_pairs={{0,4},{4,0},{8,12},{12,8},{16,20},{20,16},{24,28},{28,24},{32,36},... | collective-permute-start | bytes 221192 | tf_op jit(solution)/shard_map/ppermute | solution.py:19
  27.7 5.6 %collective-permute-start.8 = (f16[144,256]{1,0:T(8,128)(2,1)S(1)}, f16[144,256]{1,0:T(8,128)(2,1)S(1)}, u32[]{:S(2)}, u32[]{:S(2)}) collective-permute-start(f16[144,256]{1,0:T(8,128)(2,1)S(1)} %convert_element_type.54), channel_id=1, source_target_pairs={{0,3},{1,2},{2,1},{3,0},{4,7},{5,6},{6,5},{7,4},{8,11},{9,10},{10,... | collective-permute-start | bytes 221192 | tf_op jit(solution)/shard_map/ppermute | solution.py:19
  30.4 5.8 %collective-permute-start.12 = (f16[144,256]{1,0:T(8,128)(2,1)S(1)}, f16[144,256]{1,0:T(8,128)(2,1)S(1)}, u32[]{:S(2)}, u32[]{:S(2)}) collective-permute-start(f16[144,256]{1,0:T(8,128)(2,1)S(1)} %convert_element_type.60), channel_id=1, source_target_pairs={{0,32},{4,68},{8,40},{12,76},{16,48},{20,84},{24,56},{28,92},{32,0... | collective-permute-start | bytes 221192 | tf_op jit(solution)/shard_map/ppermute | solution.py:79
  33.4 5.8 %collective-permute-start.14 = (f16[144,256]{1,0:T(8,128)(2,1)S(1)}, f16[144,256]{1,0:T(8,128)(2,1)S(1)}, u32[]{:S(2)}, u32[]{:S(2)}) collective-permute-start(f16[144,256]{1,0:T(8,128)(2,1)S(1)} %convert_element_type.60), channel_id=1, source_target_pairs={{0,96},{4,100},{8,104},{12,108},{16,112},{20,116},{24,120},{28,124... | collective-permute-start | bytes 221192 | tf_op jit(solution)/shard_map/ppermute | solution.py:19
  36.2 3.0 %collective-permute-start.13 = (f16[144,256]{1,0:T(8,128)(2,1)S(1)}, f16[144,256]{1,0:T(8,128)(2,1)S(1)}, u32[]{:S(2)}, u32[]{:S(2)}) collective-permute-start(f16[144,256]{1,0:T(8,128)(2,1)S(1)} %collective-permute-done.12), channel_id=1, source_target_pairs={{0,4},{4,0},{8,12},{12,8},{16,20},{20,16},{24,28},{28,24},{32,36},... | collective-permute-start | bytes 221192 | tf_op jit(solution)/shard_map/ppermute | solution.py:19
  40.2 8.1 %collective-permute-start.16 = (bf16[32,2048]{1,0:T(8,128)(2,1)S(1)}, bf16[32,2048]{1,0:T(8,128)(2,1)S(1)}, u32[]{:S(2)}, u32[]{:S(2)}) collective-permute-start(bf16[32,2048]{1,0:T(8,128)(2,1)S(1)} %get-tuple-element.65), channel_id=1, source_target_pairs={{0,2},{1,3},{2,0},{3,1},{4,6},{5,7},{6,4},{7,5},{8,10},{9,11},{10,... | collective-permute-start | bytes 393224 | tf_op jit(solution)/shard_map/ppermute | solution.py:19
  41.4 7.5 %collective-permute-start.17 = (bf16[32,2048]{1,0:T(8,128)(2,1)S(1)}, bf16[32,2048]{1,0:T(8,128)(2,1)S(1)}, u32[]{:S(2)}, u32[]{:S(2)}) collective-permute-start(bf16[32,2048]{1,0:T(8,128)(2,1)S(1)} %get-tuple-element.66), channel_id=1, source_target_pairs={{0,1},{1,0},{2,3},{3,2},{4,5},{5,4},{6,7},{7,6},{8,9},{9,8},{10,11... | collective-permute-start | bytes 393224 | tf_op jit(solution)/shard_map/ppermute | solution.py:19
  43.1 6.8 %collective-permute-start.15 = (bf16[32,2048]{1,0:T(8,128)(2,1)S(1)}, bf16[32,2048]{1,0:T(8,128)(2,1)S(1)}, u32[]{:S(2)}, u32[]{:S(2)}) collective-permute-start(bf16[32,2048]{1,0:T(8,128)(2,1)S(1)} %get-tuple-element.63), channel_id=1, source_target_pairs={{0,3},{1,2},{2,1},{3,0},{4,7},{5,6},{6,5},{7,4},{8,11},{9,10},{10,... | collective-permute-start | bytes 393224 | tf_op jit(solution)/shard_map/ppermute | solution.py:19

commit v5 on v4

--- a/solution.py
+++ b/solution.py
@@ -29,13 +29,13 @@
 
 
 def dot_narrow(value, matrix):
-    high, low = split(value)
-    return dot(high, matrix) + dot(low, matrix)
+    rows = value.shape[0]
+    both = dot(jnp.concatenate(split(value), axis=0), matrix)
+    return both[:rows] + both[rows:]
 
 
 def dot_wide(value, high_matrix, low_matrix):
-    high, low = split(value)
-    return dot(high, high_matrix) + (dot(low, high_matrix) + dot(high, low_matrix))
+    return dot_narrow(value, high_matrix) + dot(value.astype(BF16), low_matrix)
 
 
 def encode(value):
@@ -137,8 +137,8 @@
     n_all = n_up + COUPLED
 
     def body(basis_hbm, low_t_hbm, low_b_hbm, up_t_hbm, up_b_hbm, *rest):
-        basis, lower_t, pair, up_high, up_low, acc_high, acc_low, top_high, top_low = rest[:9]
-        lower_b, uppers, couplings, sems = rest[9:]
+        basis, lower_t, lower_down, coupled, pair, up_high, up_low, acc_high, acc_low, top_high, top_low = rest[:11]
+        lower_b, uppers, couplings, sems = rest[11:]
         rhs_pos = lax.axis_index("rhs")
         node = lax.axis_index("leaf") + lax.axis_size("leaf")
         copies = {}
@@ -173,22 +173,21 @@
 
         copies["t"].wait()
         copies["b"].wait()
-        put(acc_high, acc_low, 0, oriented(lower_b[0], rhs_pos & 1).astype(F32))
-        down = split(transposed(lower_t[0]).astype(F32))
-        put(acc_high, acc_low, 1, times(oriented(lower_b[1], rhs_pos >> 1 & 1), down))
-        down = split(times(transposed(lower_t[1]), down))
+        for level in range(2):
+            coupled[level] = oriented(lower_b[level], rhs_pos >> level & 1)
+            lower_down[level] = transposed(lower_t[level])
         own2 = upper(0)
         pair[:rank, :] = own2
         pair[rank:, :] = upper(1)
         level3 = [upper(slot) for slot in range(2, 6)]
         own4, sib4, own5, third5, fourth5 = [upper(slot) for slot in range(6, 11)]
-        put(acc_high, acc_low, 2, times(oriented(coupling(0), node & 1), down))
-        down = split(times(transposed(own2), down))
-        put(acc_high, acc_low, 3 + first, times(oriented(coupling(1), node >> 1 & 1), down))
-        down = split(times(transposed(level3[0]), down))
+        coupled[2] = oriented(coupling(0), node & 1)
+        down = transposed(own2)
+        put(acc_high, acc_low, first, dot(oriented(coupling(1), node >> 1 & 1), down))
+        down = split(dot(transposed(level3[0]), down))
         across = split(times(oriented(coupling(2), node >> 2 & 1), down))
-        put(acc_high, acc_low, 3 + second, times(level3[2], across))
-        put(acc_high, acc_low, 5, times(level3[3], across))
+        put(acc_high, acc_low, second, times(level3[2], across))
+        put(acc_high, acc_low, 2, times(level3[3], across))
         down = split(times(transposed(own4), down))
         put(top_high, top_low, first, times(oriented(coupling(3), node >> 3 & 1), down))
         down = split(times(transposed(own5), down))
@@ -201,15 +200,16 @@
         put(up_high, up_low, 3, dot(level3[3], sib4))
         copies["basis"].wait()
 
-    stacked = [shape(n * rank, rank, dtype=BF16) for n in (2, 4, 4, 6, 6, 3, 3)]
+    stacked = [shape(n * rank, rank, dtype=BF16) for n in (2, 4, 4, 3, 3, 3, 3)]
+    lower = shape(2, rank, rank, dtype=BF16)
     return call(
         body,
-        [shape(leaf, rank, dtype=BF16), shape(2, rank, rank, dtype=BF16)] + stacked,
+        [shape(leaf, rank, dtype=BF16), lower, lower, shape(3, rank, rank, dtype=BF16)] + stacked,
         (leaf_basis, lower_transfer, lower_coupling, upper_transfer, upper_coupling),
         flops=34 * 2 * rank**3,
         moved=2**22,
         in_specs=[HBM] * 5,
-        out_specs=[VMEM] * 9,
+        out_specs=[VMEM] * 11,
         scratch_shapes=[
             pltpu.VMEM((2, rank, rank), BF16),
             pltpu.VMEM((n_up, rank, rank), BF16),
@@ -234,44 +234,55 @@
         pltpu.with_memory_space_constraint(array, pltpu.HBM)
         for array in (leaf_basis, lower_transfer, lower_coupling, upper_transfer, upper_coupling)
     ]
-    basis, low, pair, up_high, up_low, acc_high, acc_low, top_high, top_low = compose(
+    basis, low, low_down, coupled, pair, up_high, up_low, acc_high, acc_low, top_high, top_low = compose(
         leaf_basis, lower_transfer, lower_coupling, upper_transfer, upper_coupling
     )
     message = shape(total + EXTRA, rank)
 
-    def leaf_body(own, first, second, third, basis_ref, transfer, cols, up_msg, low_msg, up_ref, mid_ref):
+    def place(ref, value):
         position = lax.axis_index("rhs")
+        for slot, mask in enumerate(masks):
+            ref[aligned(position ^ mask, part), :] = value[slot * part : (slot + 1) * part, :]
+
+    def leaf_body(own, first, second, third, basis_ref, transfer, cols, up_msg, coeff_ref, mid_ref, up_ref):
         for slot, ref in enumerate((own, first, second, third)):
             cols[slot * part : (slot + 1) * part, :] = ref[...]
         coeffs = dot(cols[...], basis_ref[...])
+        place(coeff_ref, coeffs)
         middle = dot_narrow(coeffs, transfer[0])
+        place(mid_ref, middle)
         upward = dot_narrow(middle, transfer[1])
-
-        def place(ref, value, start=0):
-            for slot, mask in enumerate(masks):
-                rows = value[slot * part : (slot + 1) * part, :]
-                ref[pl.ds(pl.multiple_of(start + (position ^ mask) * part, 16), part), :] = rows
-
-        for msg, value, start in ((up_msg, upward, 0), (low_msg, coeffs, 0), (low_msg, middle, total + EXTRA)):
-            scaled, power = encode(value)
-            place(msg, scaled, start)
-            msg[start + total : start + total + EXTRA, :] = power
         place(up_ref, upward)
-        place(mid_ref, middle)
+        scaled, power = encode(upward)
+        place(up_msg, scaled)
+        up_msg[total:, :] = power
 
     plain = shape(total, rank)
-    cols, up_msg, low_msg, upward, middle = call(
+    cols, up_msg, coeffs, middle, upward = call(
         leaf_body,
-        (shape(total, leaf, dtype=BF16), message, shape(2 * (total + EXTRA), rank), plain, plain),
+        (shape(total, leaf, dtype=BF16), message, plain, plain, plain),
         (blocks[0], *came, basis, low),
         flops=2 * total * leaf * rank,
         moved=2**21,
         in_specs=[VMEM] * 6,
         out_specs=[VMEM] * 5,
     )
-    up_msg, low_msg = up_msg.astype(F16), low_msg.astype(F16)
+    up_msg = up_msg.astype(F16)
     ups = [swap(up_msg, "rhs", mask).astype(F32) for mask in masks[1:]]
-    low_sib = swap(low_msg, "rhs", 1).astype(F32)
+
+    def low_body(coeff_ref, mid_ref, low_msg):
+        put_encoded(low_msg.at[: total + EXTRA, :], coeff_ref[...])
+        put_encoded(low_msg.at[total + EXTRA :, :], mid_ref[...])
+
+    low_msg = call(
+        low_body,
+        shape(2 * (total + EXTRA), rank),
+        (coeffs, middle),
+        moved=2**20,
+        in_specs=[VMEM] * 2,
+        out_specs=VMEM,
+    )
+    low_sib = swap(low_msg.astype(F16), "rhs", 1).astype(F32)
 
     def near_half(cols, half):
         width = leaf // 8
@@ -293,8 +304,21 @@
             out_specs=VMEM,
         )
 
+    def flip_body(basis_ref, out):
+        for step in range(8):
+            rows = slice(step * leaf // 8, (step + 1) * leaf // 8)
+            out[:, rows] = basis_ref[rows, :].astype(F32).T.astype(BF16)
+
+    flipped = call(
+        flip_body,
+        shape(rank, leaf, dtype=BF16),
+        (basis,),
+        moved=2**21,
+        in_specs=[VMEM],
+        out_specs=VMEM,
+    )
     near_left = near_half(cols, 0)
-    ups, near_left = lax.optimization_barrier((ups, near_left))
+    ups, near_left, flipped = lax.optimization_barrier((ups, near_left, flipped))
 
     def group_body(own, a, b, c, out):
         out[...] = own[...] + decode(a) + (decode(b) + decode(c))
@@ -345,38 +369,35 @@
         out_specs=VMEM,
     )
     line_msg, cols = lax.optimization_barrier((line_msg.astype(F16), cols))
-    def partial_body(sibling, others, core, z1, z2, z3, high, low, out):
-        value = jnp.concatenate(
-            [decode(sibling.at[: total + EXTRA, :]), decode(others), core[...]]
-            + [decode(ref) for ref in (z1, z2, z3)],
-            axis=1,
-        )
-        out[...] = dot_wide(value, high[...], low[...])
-
-    partial = call(
+    def partial_body(sibling, others, core, z1, z2, z3, pairs, high, low, at_leaf, at_pair, at_group):
+        at_leaf[...] = dot_narrow(decode(sibling.at[: total + EXTRA, :]), pairs[0])
+        at_pair[...] = dot_narrow(decode(others), pairs[1])
+        value = jnp.concatenate([decode(ref) for ref in (z1, z2, z3)], axis=1)
+        at_group[...] = dot_narrow(core[...], pairs[2]) + dot_wide(value, high[...], low[...])
+
+    partials = call(
         partial_body,
-        plain,
-        (low_sib, cousin, group_sib, *chips, acc_high, acc_low),
+        (plain, plain, plain),
+        (low_sib, cousin, group_sib, *chips, coupled, acc_high, acc_low),
         flops=36 * total * rank * rank,
         moved=2**21,
-        in_specs=[VMEM] * 8,
-        out_specs=VMEM,
-    )
-
+        in_specs=[VMEM] * 9,
+        out_specs=[VMEM] * 3,
+    )
     lines, _ = line(line_msg, "leaf", 8)
     lines = [got.astype(F32) for got in lines]
     near_right = near_half(cols, 1)
 
     out_masks = (0, 2, 1, 3)
 
-    def last_body(part_ref, a, b, c, high, low, basis_ref, left, right, own, first, second, third, inner):
+    def last_body(at_leaf, at_pair, at_group, a, b, c, high, low, steps, basis_ref, left, right, own, first, second, third, inner):
         position = lax.axis_index("rhs")
         value = jnp.concatenate([decode(ref) for ref in (a, b, c)], axis=1)
-        inner[...] = part_ref[...] + dot_wide(value, high[...], low[...])
+        value = at_group[...] + dot_wide(value, high[...], low[...])
+        value = at_pair[...] + dot_narrow(value, steps[1])
+        inner[...] = at_leaf[...] + dot_narrow(value, steps[0])
         coeffs = jnp.concatenate([inner[aligned(position ^ mask, part), :] for mask in masks], axis=0)
-        far = lax.dot_general(
-            coeffs.astype(BF16), basis_ref[...], (((1,), (1,)), ((), ())), preferred_element_type=F32
-        )
+        far = dot(coeffs.astype(BF16), basis_ref[...])
         for mask, ref in zip(out_masks, (own, first, second, third)):
             slot = masks.index(mask)
             rows = slice(slot * part, (slot + 1) * part)
@@ -387,10 +408,10 @@
     own, *blocks = call(
         last_body,
         (shape(part, leaf), sent, sent, sent),
-        (partial, *lines, top_high, top_low, basis, near_left, near_right),
+        (*partials, *lines, top_high, top_low, low_down, flipped, near_left, near_right),
         flops=2 * total * leaf * rank,
         moved=2**22,
-        in_specs=[VMEM] * 9,
+        in_specs=[VMEM] * 12,
         out_specs=[VMEM] * 4,
         scratch_shapes=[pltpu.VMEM((total, rank), F32)],
     )
@@ -425,8 +446,8 @@
             input_output_aliases={} if under is None else {count: 0},
         )
 
-    most = join((own, blocks[0], blocks[1]), (0, 1, 2))
-    return join((blocks[2],), (3,), most)
+    most = join((own, blocks[0]), (0, 1))
+    return join(blocks[1:], (2, 3), most)
 
 
 def solution(mesh):

time: 50.7 us -> 51.2 us (level)
  waiting for transfers between devices: 10.7 us -> 11.4 us
    ppermute x16, waiting for transfers between devices: 10.7 us -> 11.4 us  [swap(): return lax.ppermute(value, axis, pairs)]
    pallas_call x12 -> x14, Pallas kernels: 13.4 us -> 13.5 us  [call(): pl.pallas_call(body, out_shape=outs, compiler_params=pltpu.CompilerParams...]
  transfers between devices with their start and end apart: 18 -> 18, of which waited for: 10 -> 11; matrix products, arithmetic and copies ran while one was open for 0% -> 0% of each run, Pallas kernels for 19% -> 19%
where the time goes in v5:
time: 51.2 us; the launch traced here: 51 us
  starting transfers between devices  25.6 us (50%)
  Pallas kernels  13.5 us (26%)
  waiting for transfers between devices  11.4 us (22%)
    ppermute x16, starting transfers between devices, swap(): return lax.ppermute(value, axis, pairs)  22 us
    pallas_call x14, Pallas kernels, call(): pl.pallas_call(body, out_shape=outs, compiler_params=pltpu.CompilerParams...  13.5 us
    ppermute x16, waiting for transfers between devices, swap(): return lax.ppermute(value, axis, pairs)  11.4 us
    ppermute x2, starting transfers between devices, line(): mine = lax.ppermute(message, axis, pairs)  3.56 us
  transfers between devices with their start and end apart: 18, of which 11 were waited for; matrix products, arithmetic and copies ran while one was open for 0% of the time, Pallas kernels for 19%

profile of v5, /device:TPU:0, one launch (start us, length us, event | category | flops | bytes accessed | tf_op | source)
XLA Modules:
  0.0 51.0 jit_solution(17217404572789969203)
XLA Ops:
  0.0 1.1 %shard_map.73 = (bf16[32,2048]{1,0:T(8,128)(2,1)S(1)}, bf16[32,2048]{1,0:T(8,128)(2,1)S(1)}, bf16[32,2048]{1,0:T(8,128)(2,1)S(1)}, bf16[32,2048]{1,0:T(8,128)(2,1)S(1)}) custom-call(bf16[32,8192]{1,0:T(8,128)(2,1)} %source.1), custom_call_target="tpu_custom_call" | custom-call | bytes 1048576 | tf_op jit(solution)/shard_map/pallas_call | solution.py:59
  1.1 1.7 %collective-permute-start = (bf16[32,2048]{1,0:T(8,128)(2,1)S(1)}, bf16[32,2048]{1,0:T(8,128)(2,1)S(1)}, u32[]{:S(2)}, u32[]{:S(2)}) collective-permute-start(bf16[32,2048]{1,0:T(8,128)(2,1)S(1)} %get-tuple-element.43), channel_id=1, source_target_pairs={{0,1},{1,0},{2,3},{3,2},{4,5},{5,4},{6,7},{7,6},{8,9},{9,8},{10,11... | collective-permute-start | bytes 393224 | tf_op jit(solution)/shard_map/ppermute | solution.py:19
  2.9 2.2 %collective-permute-start.1 = (bf16[32,2048]{1,0:T(8,128)(2,1)S(1)}, bf16[32,2048]{1,0:T(8,128)(2,1)S(1)}, u32[]{:S(2)}, u32[]{:S(2)}) collective-permute-start(bf16[32,2048]{1,0:T(8,128)(2,1)S(1)} %get-tuple-element.44), channel_id=1, source_target_pairs={{0,3},{1,2},{2,1},{3,0},{4,7},{5,6},{6,5},{7,4},{8,11},{9,10},{10,... | collective-permute-start | bytes 393224 | tf_op jit(solution)/shard_map/ppermute | solution.py:19
  5.1 0.7 %collective-permute-start.2 = (bf16[32,2048]{1,0:T(8,128)(2,1)S(1)}, bf16[32,2048]{1,0:T(8,128)(2,1)S(1)}, u32[]{:S(2)}, u32[]{:S(2)}) collective-permute-start(bf16[32,2048]{1,0:T(8,128)(2,1)S(1)} %get-tuple-element.45), channel_id=1, source_target_pairs={{0,2},{1,3},{2,0},{3,1},{4,6},{5,7},{6,4},{7,5},{8,10},{9,11},{10,... | collective-permute-start | bytes 393224 | tf_op jit(solution)/shard_map/ppermute | solution.py:19
  5.8 4.4 %shard_map.74 = (bf16[2048,256]{1,0:T(8,128)(2,1)S(1)}, bf16[2,256,256]{2,1,0:T(8,128)(2,1)S(1)}, bf16[2,256,256]{2,1,0:T(8,128)(2,1)S(1)}, bf16[3,256,256]{2,1,...) custom-call(bf16[1,2048,256]{2,1,0:T(8,128)(2,1)} %basis_hbm.1, ...), custom_call_target="tpu_custom_call" | custom-call | flops 1140850688 | bytes 4194304 | tf_op jit(solution)/shard_map/pallas_call | solution.py:59
  10.3 1.5 %collective-permute-done.2.third = bf16[32,2048]{1,0:T(8,128)(2,1)S(1)} collective-permute-done((bf16[32,2048]{1,0:T(8,128)(2,1)S(1)}, bf16[32,2048]{1,0:T(8,128)(2,1)S(1)}, u32[]{:S(2)}, u32[]{:S(2)}) %collective-permute-start.2) | collective-permute-done | bytes 131104 | tf_op jit(solution)/shard_map/ppermute | solution.py:19
  11.9 0.7 %shard_map.75 = (bf16[128,2048]{1,0:T(8,128)(2,1)S(1)}, f32[144,256]{1,0:T(8,128)S(1)}, f32[128,256]{1,0:T(8,128)S(1)}, f32[128,256]{1,0:T(8,128)S(1)}, f32[128,256]{1,0:T(8,128)S(1)}) custom-call(bf16[32,2048]{1,0:T(8,128)(2,1)S(1)} %get-tuple-element.42.own, bf16[32,2048]{1,0:T(8,128)(2,1)S(1)} %collective-permute-done.first, ...), custom_call_target="tpu_custom_call" | custom-call | flops 134217728 | bytes 2097152 | tf_op jit(solution)/shard_map/pallas_call | solution.py:59
  12.6 1.8 %collective-permute-start.6 = (f16[144,256]{1,0:T(8,128)(2,1)S(1)}, f16[144,256]{1,0:T(8,128)(2,1)S(1)}, u32[]{:S(2)}, u32[]{:S(2)}) collective-permute-start(f16[144,256]{1,0:T(8,128)(2,1)S(1)} %convert_element_type.50), channel_id=1, source_target_pairs={{0,2},{1,3},{2,0},{3,1},{4,6},{5,7},{6,4},{7,5},{8,10},{9,11},{10,... | collective-permute-start | bytes 221192 | tf_op jit(solution)/shard_map/ppermute | solution.py:19
  14.4 1.3 %collective-permute-start.5 = (f16[144,256]{1,0:T(8,128)(2,1)S(1)}, f16[144,256]{1,0:T(8,128)(2,1)S(1)}, u32[]{:S(2)}, u32[]{:S(2)}) collective-permute-start(f16[144,256]{1,0:T(8,128)(2,1)S(1)} %convert_element_type.50), channel_id=1, source_target_pairs={{0,3},{1,2},{2,1},{3,0},{4,7},{5,6},{6,5},{7,4},{8,11},{9,10},{10,... | collective-permute-start | bytes 221192 | tf_op jit(solution)/shard_map/ppermute | solution.py:19
  15.7 0.5 collective-permute-start.4
  16.6 1.6 %collective-permute-start.3 = (f16[288,256]{1,0:T(8,128)(2,1)S(1)}, f16[288,256]{1,0:T(8,128)(2,1)S(1)}, u32[]{:S(2)}, u32[]{:S(2)}) collective-permute-start(f16[288,256]{1,0:T(8,128)(2,1)S(1)} %convert_element_type.48), channel_id=1, source_target_pairs={{0,1},{1,0},{2,3},{3,2},{4,5},{5,4},{6,7},{7,6},{8,9},{9,8},{10,11... | collective-permute-start | bytes 442376 | tf_op jit(solution)/shard_map/ppermute | solution.py:19
  18.2 1.5 %shard_map.77.left = f32[128,1024]{1,0:T(8,128)S(1)} custom-call(bf16[128,2048]{1,0:T(8,128)(2,1)S(1)} %get-tuple-element.74.cols_ref, bf16[1,2048,2048]{2,1,0:T(8,128)(2,1)S(1)} %bitcast.1), custom_call_target="tpu_custom_call" | custom-call | flops 536870912 | bytes 4980736 | tf_op jit(solution)/shard_map/pallas_call | solution.py:59
  20.6 1.4 %collective-permute-done.3 = f16[288,256]{1,0:T(8,128)(2,1)S(1)} collective-permute-done((f16[288,256]{1,0:T(8,128)(2,1)S(1)}, f16[288,256]{1,0:T(8,128)(2,1)S(1)}, u32[]{:S(2)}, u32[]{:S(2)}) %collective-permute-start.3) | collective-permute-done | bytes 147488 | tf_op jit(solution)/shard_map/ppermute | solution.py:19
  22.3 2.0 %collective-permute-start.9 = (f16[144,256]{1,0:T(8,128)(2,1)S(1)}, f16[144,256]{1,0:T(8,128)(2,1)S(1)}, u32[]{:S(2)}, u32[]{:S(2)}) collective-permute-start(f16[144,256]{1,0:T(8,128)(2,1)S(1)} %convert_element_type.56), channel_id=1, source_target_pairs={{0,8},{4,20},{8,0},{12,28},{16,24},{20,4},{24,16},{28,12},{32,40},... | collective-permute-start | bytes 221192 | tf_op jit(solution)/shard_map/ppermute | solution.py:79
  24.3 2.5 %collective-permute-start.11 = (f16[144,256]{1,0:T(8,128)(2,1)S(1)}, f16[144,256]{1,0:T(8,128)(2,1)S(1)}, u32[]{:S(2)}, u32[]{:S(2)}) collective-permute-start(f16[144,256]{1,0:T(8,128)(2,1)S(1)} %convert_element_type.56), channel_id=1, source_target_pairs={{0,24},{4,28},{8,16},{12,20},{16,8},{20,12},{24,0},{28,4},{32,56},... | collective-permute-start | bytes 221192 | tf_op jit(solution)/shard_map/ppermute | solution.py:19
  26.8 0.9 %collective-permute-start.10 = (f16[144,256]{1,0:T(8,128)(2,1)S(1)}, f16[144,256]{1,0:T(8,128)(2,1)S(1)}, u32[]{:S(2)}, u32[]{:S(2)}) collective-permute-start(f16[144,256]{1,0:T(8,128)(2,1)S(1)} %collective-permute-done.9), channel_id=1, source_target_pairs={{0,4},{4,0},{8,12},{12,8},{16,20},{20,16},{24,28},{28,24},{32,36},... | collective-permute-start | bytes 221192 | tf_op jit(solution)/shard_map/ppermute | solution.py:19
  27.8 1.6 %collective-permute-start.8 = (f16[144,256]{1,0:T(8,128)(2,1)S(1)}, f16[144,256]{1,0:T(8,128)(2,1)S(1)}, u32[]{:S(2)}, u32[]{:S(2)}) collective-permute-start(f16[144,256]{1,0:T(8,128)(2,1)S(1)} %convert_element_type.54), channel_id=1, source_target_pairs={{0,3},{1,2},{2,1},{3,0},{4,7},{5,6},{6,5},{7,4},{8,11},{9,10},{10,... | collective-permute-start | bytes 221192 | tf_op jit(solution)/shard_map/ppermute | solution.py:19
  29.4 0.6 %collective-permute-done.11 = f16[144,256]{1,0:T(8,128)(2,1)S(1)} collective-permute-done((f16[144,256]{1,0:T(8,128)(2,1)S(1)}, f16[144,256]{1,0:T(8,128)(2,1)S(1)}, u32[]{:S(2)}, u32[]{:S(2)}) %collective-permute-start.11) | collective-permute-done | bytes 73760 | tf_op jit(solution)/shard_map/ppermute | solution.py:19
  30.5 1.6 %collective-permute-start.12 = (f16[144,256]{1,0:T(8,128)(2,1)S(1)}, f16[144,256]{1,0:T(8,128)(2,1)S(1)}, u32[]{:S(2)}, u32[]{:S(2)}) collective-permute-start(f16[144,256]{1,0:T(8,128)(2,1)S(1)} %convert_element_type.60), channel_id=1, source_target_pairs={{0,32},{4,68},{8,40},{12,76},{16,48},{20,84},{24,56},{28,92},{32,0... | collective-permute-start | bytes 221192 | tf_op jit(solution)/shard_map/ppermute | solution.py:79
  32.0 1.4 %collective-permute-done.8 = f16[144,256]{1,0:T(8,128)(2,1)S(1)} collective-permute-done((f16[144,256]{1,0:T(8,128)(2,1)S(1)}, f16[144,256]{1,0:T(8,128)(2,1)S(1)}, u32[]{:S(2)}, u32[]{:S(2)}) %collective-permute-start.8) | collective-permute-done | bytes 73760 | tf_op jit(solution)/shard_map/ppermute | solution.py:19
  33.4 2.8 %collective-permute-start.14 = (f16[144,256]{1,0:T(8,128)(2,1)S(1)}, f16[144,256]{1,0:T(8,128)(2,1)S(1)}, u32[]{:S(2)}, u32[]{:S(2)}) collective-permute-start(f16[144,256]{1,0:T(8,128)(2,1)S(1)} %convert_element_type.60), channel_id=1, source_target_pairs={{0,96},{4,100},{8,104},{12,108},{16,112},{20,116},{24,120},{28,124... | collective-permute-start | bytes 221192 | tf_op jit(solution)/shard_map/ppermute | solution.py:19
  36.7 1.5 %shard_map.83.right = f32[128,1024]{1,0:T(8,128)S(1)} custom-call(bf16[128,2048]{1,0:T(8,128)(2,1)S(1)} %get-tuple-element.74.cols_ref, bf16[1,2048,2048]{2,1,0:T(8,128)(2,1)S(1)} %bitcast.1), custom_call_target="tpu_custom_call" | custom-call | flops 536870912 | bytes 4980736 | tf_op jit(solution)/shard_map/pallas_call | solution.py:59
  38.3 1.0 %collective-permute-done.14 = f16[144,256]{1,0:T(8,128)(2,1)S(1)} collective-permute-done((f16[144,256]{1,0:T(8,128)(2,1)S(1)}, f16[144,256]{1,0:T(8,128)(2,1)S(1)}, u32[]{:S(2)}, u32[]{:S(2)}) %collective-permute-start.14) | collective-permute-done | bytes 73760 | tf_op jit(solution)/shard_map/ppermute | solution.py:19
  39.3 1.1 %shard_map.84 = (f32[32,2048]{1,0:T(8,128)S(1)}, bf16[32,2048]{1,0:T(8,128)(2,1)S(1)}, bf16[32,2048]{1,0:T(8,128)(2,1)S(1)}, bf16[32,2048]{1,0:T(8,128)(2,1)S(1)}) custom-call(f32[128,256]{1,0:T(8,128)S(1)} %get-tuple-element.62.at_leaf, f32[128,256]{1,0:T(8,128)S(1)} %get-tuple-element.63.at_pair, f32[128,256]{1,0:T(8,128)S(1)} %get-tuple-element.64.at_group, ...), custom_call_target="tpu_custom_call" | custom-call | flops 134217728 | bytes 4194304 | tf_op jit(solution)/shard_map/pallas_call | solution.py:59
  40.5 2.2 %collective-permute-start.17 = (bf16[32,2048]{1,0:T(8,128)(2,1)S(1)}, bf16[32,2048]{1,0:T(8,128)(2,1)S(1)}, u32[]{:S(2)}, u32[]{:S(2)}) collective-permute-start(bf16[32,2048]{1,0:T(8,128)(2,1)S(1)} %get-tuple-element.78), channel_id=1, source_target_pairs={{0,2},{1,3},{2,0},{3,1},{4,6},{5,7},{6,4},{7,5},{8,10},{9,11},{10,... | collective-permute-start | bytes 393224 | tf_op jit(solution)/shard_map/ppermute | solution.py:19
  42.6 0.8 %collective-permute-start.15 = (bf16[32,2048]{1,0:T(8,128)(2,1)S(1)}, bf16[32,2048]{1,0:T(8,128)(2,1)S(1)}, u32[]{:S(2)}, u32[]{:S(2)}) collective-permute-start(bf16[32,2048]{1,0:T(8,128)(2,1)S(1)} %get-tuple-element.75), channel_id=1, source_target_pairs={{0,1},{1,0},{2,3},{3,2},{4,5},{5,4},{6,7},{7,6},{8,9},{9,8},{10,11... | collective-permute-start | bytes 393224 | tf_op jit(solution)/shard_map/ppermute | solution.py:19
  43.4 1.2 %collective-permute-start.16 = (bf16[32,2048]{1,0:T(8,128)(2,1)S(1)}, bf16[32,2048]{1,0:T(8,128)(2,1)S(1)}, u32[]{:S(2)}, u32[]{:S(2)}) collective-permute-start(bf16[32,2048]{1,0:T(8,128)(2,1)S(1)} %get-tuple-element.76), channel_id=1, source_target_pairs={{0,3},{1,2},{2,1},{3,0},{4,7},{5,6},{6,5},{7,4},{8,11},{9,10},{10,... | collective-permute-start | bytes 393224 | tf_op jit(solution)/shard_map/ppermute | solution.py:19
  44.6 3.4 %collective-permute-done.17.refs_1_ = bf16[32,2048]{1,0:T(8,128)(2,1)S(1)} collective-permute-done((bf16[32,2048]{1,0:T(8,128)(2,1)S(1)}, bf16[32,2048]{1,0:T(8,128)(2,1)S(1)}, u32[]{:S(2)}, u32[]{:S(2)}) %collective-permute-start.17) | collective-permute-done | bytes 131104 | tf_op jit(solution)/shard_map/ppermute | solution.py:19
  48.1 0.8 %shard_map.85.refs_2_ = f32[32,8192]{1,0:T(8,128)} custom-call(f32[32,2048]{1,0:T(8,128)S(1)} %get-tuple-element.77.refs_0_, bf16[32,2048]{1,0:T(8,128)(2,1)S(1)} %collective-permute-done.17.refs_1_), custom_call_target="tpu_custom_call" | custom-call | bytes 786432 | tf_op jit(solution)/shard_map/pallas_call | solution.py:59
  48.9 0.7 %collective-permute-done.15.refs_0_ = bf16[32,2048]{1,0:T(8,128)(2,1)S(1)} collective-permute-done((bf16[32,2048]{1,0:T(8,128)(2,1)S(1)}, bf16[32,2048]{1,0:T(8,128)(2,1)S(1)}, u32[]{:S(2)}, u32[]{:S(2)}) %collective-permute-start.15) | collective-permute-done | bytes 131104 | tf_op jit(solution)/shard_map/ppermute | solution.py:19
  49.6 0.6 %collective-permute-done.16.refs_1_ = bf16[32,2048]{1,0:T(8,128)(2,1)S(1)} collective-permute-done((bf16[32,2048]{1,0:T(8,128)(2,1)S(1)}, bf16[32,2048]{1,0:T(8,128)(2,1)S(1)}, u32[]{:S(2)}, u32[]{:S(2)}) %collective-permute-start.16) | collective-permute-done | bytes 131104 | tf_op jit(solution)/shard_map/ppermute | solution.py:19
  50.2 0.8 %shard_map.86 = f32[32,8192]{1,0:T(8,128)} custom-call(bf16[32,2048]{1,0:T(8,128)(2,1)S(1)} %collective-permute-done.15.refs_0_, bf16[32,2048]{1,0:T(8,128)(2,1)S(1)} %collective-permute-done.16.refs_1_, f32[32,8192]{1,0:T(8,128)} %shard_map.85.refs_2_), custom_call_target="tpu_custom_call", output_to_operand_aliasing={{}: (2, {})} | custom-call | bytes 786432 | tf_op jit(solution)/shard_map/pallas_call | solution.py:59
  (39 shorter events, 2.6 us)
Async XLA Ops:
  1.1 9.0 %collective-permute-start = (bf16[32,2048]{1,0:T(8,128)(2,1)S(1)}, bf16[32,2048]{1,0:T(8,128)(2,1)S(1)}, u32[]{:S(2)}, u32[]{:S(2)}) collective-permute-start(bf16[32,2048]{1,0:T(8,128)(2,1)S(1)} %get-tuple-element.43), channel_id=1, source_target_pairs={{0,1},{1,0},{2,3},{3,2},{4,5},{5,4},{6,7},{7,6},{8,9},{9,8},{10,11... | collective-permute-start | bytes 393224 | tf_op jit(solution)/shard_map/ppermute | solution.py:19
  2.9 7.5 %collective-permute-start.1 = (bf16[32,2048]{1,0:T(8,128)(2,1)S(1)}, bf16[32,2048]{1,0:T(8,128)(2,1)S(1)}, u32[]{:S(2)}, u32[]{:S(2)}) collective-permute-start(bf16[32,2048]{1,0:T(8,128)(2,1)S(1)} %get-tuple-element.44), channel_id=1, source_target_pairs={{0,3},{1,2},{2,1},{3,0},{4,7},{5,6},{6,5},{7,4},{8,11},{9,10},{10,... | collective-permute-start | bytes 393224 | tf_op jit(solution)/shard_map/ppermute | solution.py:19
  5.1 13.2 %slice-start = ((s8[8388608]{0:T(1024)(128)(4,1)}), s8[4194304]{0:T(1024)(128)(4,1)S(1)}, s32[]{:S(2)}) async-start(s8[8388608]{0:T(1024)(128)(4,1)} %bitcast), calls=%async_computation | async-start | bytes 8388608
  5.1 13.2 %slice-start.1 = ((s8[8388608]{0:T(1024)(128)(4,1)}), s8[4194304]{0:T(1024)(128)(4,1)S(1)}, s32[]{:S(2)}) async-start(s8[8388608]{0:T(1024)(128)(4,1)} %bitcast), calls=%async_computation.1 | async-start | bytes 8388608
  5.1 6.8 %collective-permute-start.2 = (bf16[32,2048]{1,0:T(8,128)(2,1)S(1)}, bf16[32,2048]{1,0:T(8,128)(2,1)S(1)}, u32[]{:S(2)}, u32[]{:S(2)}) collective-permute-start(bf16[32,2048]{1,0:T(8,128)(2,1)S(1)} %get-tuple-element.45), channel_id=1, source_target_pairs={{0,2},{1,3},{2,0},{3,1},{4,6},{5,7},{6,4},{7,5},{8,10},{9,11},{10,... | collective-permute-start | bytes 393224 | tf_op jit(solution)/shard_map/ppermute | solution.py:19
  12.6 7.2 %collective-permute-start.6 = (f16[144,256]{1,0:T(8,128)(2,1)S(1)}, f16[144,256]{1,0:T(8,128)(2,1)S(1)}, u32[]{:S(2)}, u32[]{:S(2)}) collective-permute-start(f16[144,256]{1,0:T(8,128)(2,1)S(1)} %convert_element_type.50), channel_id=1, source_target_pairs={{0,2},{1,3},{2,0},{3,1},{4,6},{5,7},{6,4},{7,5},{8,10},{9,11},{10,... | collective-permute-start | bytes 221192 | tf_op jit(solution)/shard_map/ppermute | solution.py:19
  14.4 5.6 %collective-permute-start.5 = (f16[144,256]{1,0:T(8,128)(2,1)S(1)}, f16[144,256]{1,0:T(8,128)(2,1)S(1)}, u32[]{:S(2)}, u32[]{:S(2)}) collective-permute-start(f16[144,256]{1,0:T(8,128)(2,1)S(1)} %convert_element_type.50), channel_id=1, source_target_pairs={{0,3},{1,2},{2,1},{3,0},{4,7},{5,6},{6,5},{7,4},{8,11},{9,10},{10,... | collective-permute-start | bytes 221192 | tf_op jit(solution)/shard_map/ppermute | solution.py:19
  15.7 4.7 %collective-permute-start.4 = (f16[144,256]{1,0:T(8,128)(2,1)S(1)}, f16[144,256]{1,0:T(8,128)(2,1)S(1)}, u32[]{:S(2)}, u32[]{:S(2)}) collective-permute-start(f16[144,256]{1,0:T(8,128)(2,1)S(1)} %convert_element_type.50), channel_id=1, source_target_pairs={{0,1},{1,0},{2,3},{3,2},{4,5},{5,4},{6,7},{7,6},{8,9},{9,8},{10,11... | collective-permute-start | bytes 221192 | tf_op jit(solution)/shard_map/ppermute | solution.py:19
  16.6 5.4 %collective-permute-start.3 = (f16[288,256]{1,0:T(8,128)(2,1)S(1)}, f16[288,256]{1,0:T(8,128)(2,1)S(1)}, u32[]{:S(2)}, u32[]{:S(2)}) collective-permute-start(f16[288,256]{1,0:T(8,128)(2,1)S(1)} %convert_element_type.48), channel_id=1, source_target_pairs={{0,1},{1,0},{2,3},{3,2},{4,5},{5,4},{6,7},{7,6},{8,9},{9,8},{10,11... | collective-permute-start | bytes 442376 | tf_op jit(solution)/shard_map/ppermute | solution.py:19
  20.5 1.5 %collective-permute-start.7 = (f32[128,256]{1,0:T(8,128)S(1)}, f32[128,256]{1,0:T(8,128)S(1)}, u32[]{:S(2)}, u32[]{:S(2)}) collective-permute-start(f32[128,256]{1,0:T(8,128)S(1)} %shard_map.79.own), channel_id=1, source_target_pairs={{0,4},{4,0},{8,12},{12,8},{16,20},{20,16},{24,28},{28,24},{32,36},... | collective-permute-start | bytes 393224 | tf_op jit(solution)/shard_map/ppermute | solution.py:19
  22.3 4.5 %collective-permute-start.9 = (f16[144,256]{1,0:T(8,128)(2,1)S(1)}, f16[144,256]{1,0:T(8,128)(2,1)S(1)}, u32[]{:S(2)}, u32[]{:S(2)}) collective-permute-start(f16[144,256]{1,0:T(8,128)(2,1)S(1)} %convert_element_type.56), channel_id=1, source_target_pairs={{0,8},{4,20},{8,0},{12,28},{16,24},{20,4},{24,16},{28,12},{32,40},... | collective-permute-start | bytes 221192 | tf_op jit(solution)/shard_map/ppermute | solution.py:79
  24.3 5.7 %collective-permute-start.11 = (f16[144,256]{1,0:T(8,128)(2,1)S(1)}, f16[144,256]{1,0:T(8,128)(2,1)S(1)}, u32[]{:S(2)}, u32[]{:S(2)}) collective-permute-start(f16[144,256]{1,0:T(8,128)(2,1)S(1)} %convert_element_type.56), channel_id=1, source_target_pairs={{0,24},{4,28},{8,16},{12,20},{16,8},{20,12},{24,0},{28,4},{32,56},... | collective-permute-start | bytes 221192 | tf_op jit(solution)/shard_map/ppermute | solution.py:19
  26.8 3.2 %collective-permute-start.10 = (f16[144,256]{1,0:T(8,128)(2,1)S(1)}, f16[144,256]{1,0:T(8,128)(2,1)S(1)}, u32[]{:S(2)}, u32[]{:S(2)}) collective-permute-start(f16[144,256]{1,0:T(8,128)(2,1)S(1)} %collective-permute-done.9), channel_id=1, source_target_pairs={{0,4},{4,0},{8,12},{12,8},{16,20},{20,16},{24,28},{28,24},{32,36},... | collective-permute-start | bytes 221192 | tf_op jit(solution)/shard_map/ppermute | solution.py:19
  27.8 5.6 %collective-permute-start.8 = (f16[144,256]{1,0:T(8,128)(2,1)S(1)}, f16[144,256]{1,0:T(8,128)(2,1)S(1)}, u32[]{:S(2)}, u32[]{:S(2)}) collective-permute-start(f16[144,256]{1,0:T(8,128)(2,1)S(1)} %convert_element_type.54), channel_id=1, source_target_pairs={{0,3},{1,2},{2,1},{3,0},{4,7},{5,6},{6,5},{7,4},{8,11},{9,10},{10,... | collective-permute-start | bytes 221192 | tf_op jit(solution)/shard_map/ppermute | solution.py:19
  30.5 5.8 %collective-permute-start.12 = (f16[144,256]{1,0:T(8,128)(2,1)S(1)}, f16[144,256]{1,0:T(8,128)(2,1)S(1)}, u32[]{:S(2)}, u32[]{:S(2)}) collective-permute-start(f16[144,256]{1,0:T(8,128)(2,1)S(1)} %convert_element_type.60), channel_id=1, source_target_pairs={{0,32},{4,68},{8,40},{12,76},{16,48},{20,84},{24,56},{28,92},{32,0... | collective-permute-start | bytes 221192 | tf_op jit(solution)/shard_map/ppermute | solution.py:79
  33.4 5.9 %collective-permute-start.14 = (f16[144,256]{1,0:T(8,128)(2,1)S(1)}, f16[144,256]{1,0:T(8,128)(2,1)S(1)}, u32[]{:S(2)}, u32[]{:S(2)}) collective-permute-start(f16[144,256]{1,0:T(8,128)(2,1)S(1)} %convert_element_type.60), channel_id=1, source_target_pairs={{0,96},{4,100},{8,104},{12,108},{16,112},{20,116},{24,120},{28,124... | collective-permute-start | bytes 221192 | tf_op jit(solution)/shard_map/ppermute | solution.py:19
  36.3 3.0 %collective-permute-start.13 = (f16[144,256]{1,0:T(8,128)(2,1)S(1)}, f16[144,256]{1,0:T(8,128)(2,1)S(1)}, u32[]{:S(2)}, u32[]{:S(2)}) collective-permute-start(f16[144,256]{1,0:T(8,128)(2,1)S(1)} %collective-permute-done.12), channel_id=1, source_target_pairs={{0,4},{4,0},{8,12},{12,8},{16,20},{20,16},{24,28},{28,24},{32,36},... | collective-permute-start | bytes 221192 | tf_op jit(solution)/shard_map/ppermute | solution.py:19
  40.5 7.6 %collective-permute-start.17 = (bf16[32,2048]{1,0:T(8,128)(2,1)S(1)}, bf16[32,2048]{1,0:T(8,128)(2,1)S(1)}, u32[]{:S(2)}, u32[]{:S(2)}) collective-permute-start(bf16[32,2048]{1,0:T(8,128)(2,1)S(1)} %get-tuple-element.78), channel_id=1, source_target_pairs={{0,2},{1,3},{2,0},{3,1},{4,6},{5,7},{6,4},{7,5},{8,10},{9,11},{10,... | collective-permute-start | bytes 393224 | tf_op jit(solution)/shard_map/ppermute | solution.py:19
  42.6 6.9 %collective-permute-start.15 = (bf16[32,2048]{1,0:T(8,128)(2,1)S(1)}, bf16[32,2048]{1,0:T(8,128)(2,1)S(1)}, u32[]{:S(2)}, u32[]{:S(2)}) collective-permute-start(bf16[32,2048]{1,0:T(8,128)(2,1)S(1)} %get-tuple-element.75), channel_id=1, source_target_pairs={{0,1},{1,0},{2,3},{3,2},{4,5},{5,4},{6,7},{7,6},{8,9},{9,8},{10,11... | collective-permute-start | bytes 393224 | tf_op jit(solution)/shard_map/ppermute | solution.py:19
  43.4 6.8 %collective-permute-start.16 = (bf16[32,2048]{1,0:T(8,128)(2,1)S(1)}, bf16[32,2048]{1,0:T(8,128)(2,1)S(1)}, u32[]{:S(2)}, u32[]{:S(2)}) collective-permute-start(bf16[32,2048]{1,0:T(8,128)(2,1)S(1)} %get-tuple-element.76), channel_id=1, source_target_pairs={{0,3},{1,2},{2,1},{3,0},{4,7},{5,6},{6,5},{7,4},{8,11},{9,10},{10,... | collective-permute-start | bytes 393224 | tf_op jit(solution)/shard_map/ppermute | solution.py:19

commit v6 on v5

--- a/solution.py
+++ b/solution.py
@@ -93,9 +93,13 @@
     def body(source, *rest):
         blocks, sems = rest[:-1], rest[-1]
         position = lax.axis_index("rhs")
+        half = part // 2
         copies = [
-            pltpu.make_async_copy(source.at[:, aligned(position ^ mask, leaf)], block, sems.at[slot])
+            pltpu.make_async_copy(
+                source.at[rows, aligned(position ^ mask, leaf)], block.at[rows, :], sems.at[2 * slot + side]
+            )
             for slot, (mask, block) in enumerate(zip(masks, blocks))
+            for side, rows in enumerate((slice(0, half), slice(half, part)))
         ]
         for copy in copies:
             copy.start()
@@ -110,7 +114,7 @@
         moved=4 * count * part * leaf,
         in_specs=[HBM],
         out_specs=[VMEM] * count,
-        scratch_shapes=[pltpu.SemaphoreType.DMA((count,))],
+        scratch_shapes=[pltpu.SemaphoreType.DMA((2 * count,))],
     )
 
 
@@ -131,14 +135,14 @@
 COUPLED = 5
 
 
-def compose(leaf_basis, lower_transfer, lower_coupling, upper_transfer, upper_coupling):
+def compose(vectors, leaf_basis, lower_transfer, lower_coupling, upper_transfer, upper_coupling):
     leaf, rank = leaf_basis.shape[1:]
     n_up = len(PICKS)
     n_all = n_up + COUPLED
 
-    def body(basis_hbm, low_t_hbm, low_b_hbm, up_t_hbm, up_b_hbm, *rest):
-        basis, lower_t, lower_down, coupled, pair, up_high, up_low, acc_high, acc_low, top_high, top_low = rest[:11]
-        lower_b, uppers, couplings, sems = rest[11:]
+    def body(vectors_hbm, basis_hbm, low_t_hbm, low_b_hbm, up_t_hbm, up_b_hbm, *rest):
+        own_block, basis, lower_t, lower_down, coupled, pair, up_high, up_low, acc_high, acc_low, top_high, top_low = rest[:12]
+        lower_b, uppers, couplings, sems = rest[12:]
         rhs_pos = lax.axis_index("rhs")
         node = lax.axis_index("leaf") + lax.axis_size("leaf")
         copies = {}
@@ -154,6 +158,7 @@
         for height in range(COUPLED):
             start(n_up + height, up_b_hbm.at[(node >> (height + 1)) - 1], couplings.at[height])
         start("basis", basis_hbm.at[0], basis)
+        start("own", vectors_hbm.at[:, aligned(rhs_pos, leaf)], own_block)
 
         def upper(slot):
             copies[slot].wait()
@@ -199,22 +204,23 @@
         put(up_high, up_low, 1 + second, dot(level3[2], sib4))
         put(up_high, up_low, 3, dot(level3[3], sib4))
         copies["basis"].wait()
+        copies["own"].wait()
 
     stacked = [shape(n * rank, rank, dtype=BF16) for n in (2, 4, 4, 3, 3, 3, 3)]
     lower = shape(2, rank, rank, dtype=BF16)
     return call(
         body,
-        [shape(leaf, rank, dtype=BF16), lower, lower, shape(3, rank, rank, dtype=BF16)] + stacked,
-        (leaf_basis, lower_transfer, lower_coupling, upper_transfer, upper_coupling),
+        [shape(vectors.shape[0], leaf, dtype=BF16), shape(leaf, rank, dtype=BF16), lower, lower, shape(3, rank, rank, dtype=BF16)] + stacked,
+        (vectors, leaf_basis, lower_transfer, lower_coupling, upper_transfer, upper_coupling),
         flops=34 * 2 * rank**3,
         moved=2**22,
-        in_specs=[HBM] * 5,
-        out_specs=[VMEM] * 11,
+        in_specs=[HBM] * 6,
+        out_specs=[VMEM] * 12,
         scratch_shapes=[
             pltpu.VMEM((2, rank, rank), BF16),
             pltpu.VMEM((n_up, rank, rank), BF16),
             pltpu.VMEM((COUPLED, rank, rank), BF16),
-            pltpu.SemaphoreType.DMA((n_all + 3,)),
+            pltpu.SemaphoreType.DMA((n_all + 4,)),
         ],
     )
 
@@ -228,14 +234,14 @@
     masks = (0, 1, 3, 2)
 
     vectors = pltpu.with_memory_space_constraint(vectors, pltpu.HBM)
-    blocks = cut(vectors, leaf, masks)
-    came = [swap(block, "rhs", mask) for block, mask in zip(blocks[1:], masks[1:])]
+    blocks = cut(vectors, leaf, masks[1:])
+    came = [swap(block, "rhs", mask) for block, mask in zip(blocks, masks[1:])]
     leaf_basis, lower_transfer, lower_coupling, upper_transfer, upper_coupling = [
         pltpu.with_memory_space_constraint(array, pltpu.HBM)
         for array in (leaf_basis, lower_transfer, lower_coupling, upper_transfer, upper_coupling)
     ]
-    basis, low, low_down, coupled, pair, up_high, up_low, acc_high, acc_low, top_high, top_low = compose(
-        leaf_basis, lower_transfer, lower_coupling, upper_transfer, upper_coupling
+    own_block, basis, low, low_down, coupled, pair, up_high, up_low, acc_high, acc_low, top_high, top_low = compose(
+        vectors, leaf_basis, lower_transfer, lower_coupling, upper_transfer, upper_coupling
     )
     message = shape(total + EXTRA, rank)
 
@@ -261,7 +267,7 @@
     cols, up_msg, coeffs, middle, upward = call(
         leaf_body,
         (shape(total, leaf, dtype=BF16), message, plain, plain, plain),
-        (blocks[0], *came, basis, low),
+        (own_block, *came, basis, low),
         flops=2 * total * leaf * rank,
         moved=2**21,
         in_specs=[VMEM] * 6,

time: 51.2 us -> 51.2 us (level)
  no operation moved by 1% of the time
where the time goes in v6:
time: 51.2 us; the launch traced here: 50.9 us
  starting transfers between devices  25.6 us (50%)
  Pallas kernels  13.5 us (26%)
  waiting for transfers between devices  11.4 us (22%)
    ppermute x16, starting transfers between devices, swap(): return lax.ppermute(value, axis, pairs)  22 us
    pallas_call x14, Pallas kernels, call(): pl.pallas_call(body, out_shape=outs, compiler_params=pltpu.CompilerParams...  13.5 us
    ppermute x16, waiting for transfers between devices, swap(): return lax.ppermute(value, axis, pairs)  11.4 us
    ppermute x2, starting transfers between devices, line(): mine = lax.ppermute(message, axis, pairs)  3.56 us
  transfers between devices with their start and end apart: 18, of which 11 were waited for; matrix products, arithmetic and copies ran while one was open for 0% of the time, Pallas kernels for 19%

profile of v6, /device:TPU:0, one launch (start us, length us, event | category | flops | bytes accessed | tf_op | source)
XLA Modules:
  0.0 50.9 jit_solution(5537452997168354361)
XLA Ops:
  0.0 1.1 %shard_map.74 = (bf16[32,2048]{1,0:T(8,128)(2,1)S(1)}, bf16[32,2048]{1,0:T(8,128)(2,1)S(1)}, bf16[32,2048]{1,0:T(8,128)(2,1)S(1)}) custom-call(bf16[32,8192]{1,0:T(8,128)(2,1)} %source.1), custom_call_target="tpu_custom_call" | custom-call | bytes 786432 | tf_op jit(solution)/shard_map/pallas_call | solution.py:59
  1.1 1.7 %collective-permute-start = (bf16[32,2048]{1,0:T(8,128)(2,1)S(1)}, bf16[32,2048]{1,0:T(8,128)(2,1)S(1)}, u32[]{:S(2)}, u32[]{:S(2)}) collective-permute-start(bf16[32,2048]{1,0:T(8,128)(2,1)S(1)} %get-tuple-element.43), channel_id=1, source_target_pairs={{0,1},{1,0},{2,3},{3,2},{4,5},{5,4},{6,7},{7,6},{8,9},{9,8},{10,11... | collective-permute-start | bytes 393224 | tf_op jit(solution)/shard_map/ppermute | solution.py:19
  2.8 2.2 %collective-permute-start.1 = (bf16[32,2048]{1,0:T(8,128)(2,1)S(1)}, bf16[32,2048]{1,0:T(8,128)(2,1)S(1)}, u32[]{:S(2)}, u32[]{:S(2)}) collective-permute-start(bf16[32,2048]{1,0:T(8,128)(2,1)S(1)} %get-tuple-element.44), channel_id=1, source_target_pairs={{0,3},{1,2},{2,1},{3,0},{4,7},{5,6},{6,5},{7,4},{8,11},{9,10},{10,... | collective-permute-start | bytes 393224 | tf_op jit(solution)/shard_map/ppermute | solution.py:19
  5.0 0.7 %collective-permute-start.2 = (bf16[32,2048]{1,0:T(8,128)(2,1)S(1)}, bf16[32,2048]{1,0:T(8,128)(2,1)S(1)}, u32[]{:S(2)}, u32[]{:S(2)}) collective-permute-start(bf16[32,2048]{1,0:T(8,128)(2,1)S(1)} %get-tuple-element.45), channel_id=1, source_target_pairs={{0,2},{1,3},{2,0},{3,1},{4,6},{5,7},{6,4},{7,5},{8,10},{9,11},{10,... | collective-permute-start | bytes 393224 | tf_op jit(solution)/shard_map/ppermute | solution.py:19
  5.7 4.4 %shard_map.73 = (bf16[32,2048]{1,0:T(8,128)(2,1)S(1)}, bf16[2048,256]{1,0:T(8,128)(2,1)S(1)}, bf16[2,256,256]{2,1,0:T(8,128)(2,1)S(1)}, bf16[2,256,256]{2,1,0:T(...) custom-call(bf16[32,8192]{1,0:T(8,128)(2,1)} %source.1, ...), custom_call_target="tpu_custom_call" | custom-call | flops 1140850688 | bytes 4194304 | tf_op jit(solution)/shard_map/pallas_call | solution.py:59
  10.3 1.5 %collective-permute-done.2.third = bf16[32,2048]{1,0:T(8,128)(2,1)S(1)} collective-permute-done((bf16[32,2048]{1,0:T(8,128)(2,1)S(1)}, bf16[32,2048]{1,0:T(8,128)(2,1)S(1)}, u32[]{:S(2)}, u32[]{:S(2)}) %collective-permute-start.2) | collective-permute-done | bytes 131104 | tf_op jit(solution)/shard_map/ppermute | solution.py:19
  11.8 0.7 %shard_map.75 = (bf16[128,2048]{1,0:T(8,128)(2,1)S(1)}, f32[144,256]{1,0:T(8,128)S(1)}, f32[128,256]{1,0:T(8,128)S(1)}, f32[128,256]{1,0:T(8,128)S(1)}, f32[128,256]{1,0:T(8,128)S(1)}) custom-call(bf16[32,2048]{1,0:T(8,128)(2,1)S(1)} %get-tuple-element.42.own, bf16[32,2048]{1,0:T(8,128)(2,1)S(1)} %collective-permute-done.first, ...), custom_call_target="tpu_custom_call" | custom-call | flops 134217728 | bytes 2097152 | tf_op jit(solution)/shard_map/pallas_call | solution.py:59
  12.5 1.8 %collective-permute-start.6 = (f16[144,256]{1,0:T(8,128)(2,1)S(1)}, f16[144,256]{1,0:T(8,128)(2,1)S(1)}, u32[]{:S(2)}, u32[]{:S(2)}) collective-permute-start(f16[144,256]{1,0:T(8,128)(2,1)S(1)} %convert_element_type.50), channel_id=1, source_target_pairs={{0,2},{1,3},{2,0},{3,1},{4,6},{5,7},{6,4},{7,5},{8,10},{9,11},{10,... | collective-permute-start | bytes 221192 | tf_op jit(solution)/shard_map/ppermute | solution.py:19
  14.3 1.3 %collective-permute-start.5 = (f16[144,256]{1,0:T(8,128)(2,1)S(1)}, f16[144,256]{1,0:T(8,128)(2,1)S(1)}, u32[]{:S(2)}, u32[]{:S(2)}) collective-permute-start(f16[144,256]{1,0:T(8,128)(2,1)S(1)} %convert_element_type.50), channel_id=1, source_target_pairs={{0,3},{1,2},{2,1},{3,0},{4,7},{5,6},{6,5},{7,4},{8,11},{9,10},{10,... | collective-permute-start | bytes 221192 | tf_op jit(solution)/shard_map/ppermute | solution.py:19
  15.6 0.5 collective-permute-start.4
  16.5 1.6 %collective-permute-start.3 = (f16[288,256]{1,0:T(8,128)(2,1)S(1)}, f16[288,256]{1,0:T(8,128)(2,1)S(1)}, u32[]{:S(2)}, u32[]{:S(2)}) collective-permute-start(f16[288,256]{1,0:T(8,128)(2,1)S(1)} %convert_element_type.48), channel_id=1, source_target_pairs={{0,1},{1,0},{2,3},{3,2},{4,5},{5,4},{6,7},{7,6},{8,9},{9,8},{10,11... | collective-permute-start | bytes 442376 | tf_op jit(solution)/shard_map/ppermute | solution.py:19
  18.2 1.5 %shard_map.77.left = f32[128,1024]{1,0:T(8,128)S(1)} custom-call(bf16[128,2048]{1,0:T(8,128)(2,1)S(1)} %get-tuple-element.74.cols_ref, bf16[1,2048,2048]{2,1,0:T(8,128)(2,1)S(1)} %bitcast.1), custom_call_target="tpu_custom_call" | custom-call | flops 536870912 | bytes 4980736 | tf_op jit(solution)/shard_map/pallas_call | solution.py:59
  20.5 1.4 %collective-permute-done.3 = f16[288,256]{1,0:T(8,128)(2,1)S(1)} collective-permute-done((f16[288,256]{1,0:T(8,128)(2,1)S(1)}, f16[288,256]{1,0:T(8,128)(2,1)S(1)}, u32[]{:S(2)}, u32[]{:S(2)}) %collective-permute-start.3) | collective-permute-done | bytes 147488 | tf_op jit(solution)/shard_map/ppermute | solution.py:19
  22.2 2.0 %collective-permute-start.9 = (f16[144,256]{1,0:T(8,128)(2,1)S(1)}, f16[144,256]{1,0:T(8,128)(2,1)S(1)}, u32[]{:S(2)}, u32[]{:S(2)}) collective-permute-start(f16[144,256]{1,0:T(8,128)(2,1)S(1)} %convert_element_type.56), channel_id=1, source_target_pairs={{0,8},{4,20},{8,0},{12,28},{16,24},{20,4},{24,16},{28,12},{32,40},... | collective-permute-start | bytes 221192 | tf_op jit(solution)/shard_map/ppermute | solution.py:79
  24.2 2.5 %collective-permute-start.11 = (f16[144,256]{1,0:T(8,128)(2,1)S(1)}, f16[144,256]{1,0:T(8,128)(2,1)S(1)}, u32[]{:S(2)}, u32[]{:S(2)}) collective-permute-start(f16[144,256]{1,0:T(8,128)(2,1)S(1)} %convert_element_type.56), channel_id=1, source_target_pairs={{0,24},{4,28},{8,16},{12,20},{16,8},{20,12},{24,0},{28,4},{32,56},... | collective-permute-start | bytes 221192 | tf_op jit(solution)/shard_map/ppermute | solution.py:19
  26.8 0.9 %collective-permute-start.10 = (f16[144,256]{1,0:T(8,128)(2,1)S(1)}, f16[144,256]{1,0:T(8,128)(2,1)S(1)}, u32[]{:S(2)}, u32[]{:S(2)}) collective-permute-start(f16[144,256]{1,0:T(8,128)(2,1)S(1)} %collective-permute-done.9), channel_id=1, source_target_pairs={{0,4},{4,0},{8,12},{12,8},{16,20},{20,16},{24,28},{28,24},{32,36},... | collective-permute-start | bytes 221192 | tf_op jit(solution)/shard_map/ppermute | solution.py:19
  27.7 1.6 %collective-permute-start.8 = (f16[144,256]{1,0:T(8,128)(2,1)S(1)}, f16[144,256]{1,0:T(8,128)(2,1)S(1)}, u32[]{:S(2)}, u32[]{:S(2)}) collective-permute-start(f16[144,256]{1,0:T(8,128)(2,1)S(1)} %convert_element_type.54), channel_id=1, source_target_pairs={{0,3},{1,2},{2,1},{3,0},{4,7},{5,6},{6,5},{7,4},{8,11},{9,10},{10,... | collective-permute-start | bytes 221192 | tf_op jit(solution)/shard_map/ppermute | solution.py:19
  29.3 0.6 %collective-permute-done.11 = f16[144,256]{1,0:T(8,128)(2,1)S(1)} collective-permute-done((f16[144,256]{1,0:T(8,128)(2,1)S(1)}, f16[144,256]{1,0:T(8,128)(2,1)S(1)}, u32[]{:S(2)}, u32[]{:S(2)}) %collective-permute-start.11) | collective-permute-done | bytes 73760 | tf_op jit(solution)/shard_map/ppermute | solution.py:19
  30.4 1.6 %collective-permute-start.12 = (f16[144,256]{1,0:T(8,128)(2,1)S(1)}, f16[144,256]{1,0:T(8,128)(2,1)S(1)}, u32[]{:S(2)}, u32[]{:S(2)}) collective-permute-start(f16[144,256]{1,0:T(8,128)(2,1)S(1)} %convert_element_type.60), channel_id=1, source_target_pairs={{0,32},{4,68},{8,40},{12,76},{16,48},{20,84},{24,56},{28,92},{32,0... | collective-permute-start | bytes 221192 | tf_op jit(solution)/shard_map/ppermute | solution.py:79
  32.0 1.4 %collective-permute-done.8 = f16[144,256]{1,0:T(8,128)(2,1)S(1)} collective-permute-done((f16[144,256]{1,0:T(8,128)(2,1)S(1)}, f16[144,256]{1,0:T(8,128)(2,1)S(1)}, u32[]{:S(2)}, u32[]{:S(2)}) %collective-permute-start.8) | collective-permute-done | bytes 73760 | tf_op jit(solution)/shard_map/ppermute | solution.py:19
  33.3 2.8 %collective-permute-start.14 = (f16[144,256]{1,0:T(8,128)(2,1)S(1)}, f16[144,256]{1,0:T(8,128)(2,1)S(1)}, u32[]{:S(2)}, u32[]{:S(2)}) collective-permute-start(f16[144,256]{1,0:T(8,128)(2,1)S(1)} %convert_element_type.60), channel_id=1, source_target_pairs={{0,96},{4,100},{8,104},{12,108},{16,112},{20,116},{24,120},{28,124... | collective-permute-start | bytes 221192 | tf_op jit(solution)/shard_map/ppermute | solution.py:19
  36.6 1.5 %shard_map.83.right = f32[128,1024]{1,0:T(8,128)S(1)} custom-call(bf16[128,2048]{1,0:T(8,128)(2,1)S(1)} %get-tuple-element.74.cols_ref, bf16[1,2048,2048]{2,1,0:T(8,128)(2,1)S(1)} %bitcast.1), custom_call_target="tpu_custom_call" | custom-call | flops 536870912 | bytes 4980736 | tf_op jit(solution)/shard_map/pallas_call | solution.py:59
  38.2 1.0 %collective-permute-done.14 = f16[144,256]{1,0:T(8,128)(2,1)S(1)} collective-permute-done((f16[144,256]{1,0:T(8,128)(2,1)S(1)}, f16[144,256]{1,0:T(8,128)(2,1)S(1)}, u32[]{:S(2)}, u32[]{:S(2)}) %collective-permute-start.14) | collective-permute-done | bytes 73760 | tf_op jit(solution)/shard_map/ppermute | solution.py:19
  39.2 1.1 %shard_map.84 = (f32[32,2048]{1,0:T(8,128)S(1)}, bf16[32,2048]{1,0:T(8,128)(2,1)S(1)}, bf16[32,2048]{1,0:T(8,128)(2,1)S(1)}, bf16[32,2048]{1,0:T(8,128)(2,1)S(1)}) custom-call(f32[128,256]{1,0:T(8,128)S(1)} %get-tuple-element.62.at_leaf, f32[128,256]{1,0:T(8,128)S(1)} %get-tuple-element.63.at_pair, f32[128,256]{1,0:T(8,128)S(1)} %get-tuple-element.64.at_group, ...), custom_call_target="tpu_custom_call" | custom-call | flops 134217728 | bytes 4194304 | tf_op jit(solution)/shard_map/pallas_call | solution.py:59
  40.4 2.1 %collective-permute-start.17 = (bf16[32,2048]{1,0:T(8,128)(2,1)S(1)}, bf16[32,2048]{1,0:T(8,128)(2,1)S(1)}, u32[]{:S(2)}, u32[]{:S(2)}) collective-permute-start(bf16[32,2048]{1,0:T(8,128)(2,1)S(1)} %get-tuple-element.78), channel_id=1, source_target_pairs={{0,2},{1,3},{2,0},{3,1},{4,6},{5,7},{6,4},{7,5},{8,10},{9,11},{10,... | collective-permute-start | bytes 393224 | tf_op jit(solution)/shard_map/ppermute | solution.py:19
  42.5 0.8 %collective-permute-start.15 = (bf16[32,2048]{1,0:T(8,128)(2,1)S(1)}, bf16[32,2048]{1,0:T(8,128)(2,1)S(1)}, u32[]{:S(2)}, u32[]{:S(2)}) collective-permute-start(bf16[32,2048]{1,0:T(8,128)(2,1)S(1)} %get-tuple-element.75), channel_id=1, source_target_pairs={{0,1},{1,0},{2,3},{3,2},{4,5},{5,4},{6,7},{7,6},{8,9},{9,8},{10,11... | collective-permute-start | bytes 393224 | tf_op jit(solution)/shard_map/ppermute | solution.py:19
  43.3 1.2 %collective-permute-start.16 = (bf16[32,2048]{1,0:T(8,128)(2,1)S(1)}, bf16[32,2048]{1,0:T(8,128)(2,1)S(1)}, u32[]{:S(2)}, u32[]{:S(2)}) collective-permute-start(bf16[32,2048]{1,0:T(8,128)(2,1)S(1)} %get-tuple-element.76), channel_id=1, source_target_pairs={{0,3},{1,2},{2,1},{3,0},{4,7},{5,6},{6,5},{7,4},{8,11},{9,10},{10,... | collective-permute-start | bytes 393224 | tf_op jit(solution)/shard_map/ppermute | solution.py:19
  44.5 3.4 %collective-permute-done.17.refs_1_ = bf16[32,2048]{1,0:T(8,128)(2,1)S(1)} collective-permute-done((bf16[32,2048]{1,0:T(8,128)(2,1)S(1)}, bf16[32,2048]{1,0:T(8,128)(2,1)S(1)}, u32[]{:S(2)}, u32[]{:S(2)}) %collective-permute-start.17) | collective-permute-done | bytes 131104 | tf_op jit(solution)/shard_map/ppermute | solution.py:19
  48.0 0.8 %shard_map.85.refs_2_ = f32[32,8192]{1,0:T(8,128)} custom-call(f32[32,2048]{1,0:T(8,128)S(1)} %get-tuple-element.77.refs_0_, bf16[32,2048]{1,0:T(8,128)(2,1)S(1)} %collective-permute-done.17.refs_1_), custom_call_target="tpu_custom_call" | custom-call | bytes 786432 | tf_op jit(solution)/shard_map/pallas_call | solution.py:59
  48.8 0.7 %collective-permute-done.15.refs_0_ = bf16[32,2048]{1,0:T(8,128)(2,1)S(1)} collective-permute-done((bf16[32,2048]{1,0:T(8,128)(2,1)S(1)}, bf16[32,2048]{1,0:T(8,128)(2,1)S(1)}, u32[]{:S(2)}, u32[]{:S(2)}) %collective-permute-start.15) | collective-permute-done | bytes 131104 | tf_op jit(solution)/shard_map/ppermute | solution.py:19
  49.5 0.6 %collective-permute-done.16.refs_1_ = bf16[32,2048]{1,0:T(8,128)(2,1)S(1)} collective-permute-done((bf16[32,2048]{1,0:T(8,128)(2,1)S(1)}, bf16[32,2048]{1,0:T(8,128)(2,1)S(1)}, u32[]{:S(2)}, u32[]{:S(2)}) %collective-permute-start.16) | collective-permute-done | bytes 131104 | tf_op jit(solution)/shard_map/ppermute | solution.py:19
  50.1 0.8 %shard_map.86 = f32[32,8192]{1,0:T(8,128)} custom-call(bf16[32,2048]{1,0:T(8,128)(2,1)S(1)} %collective-permute-done.15.refs_0_, bf16[32,2048]{1,0:T(8,128)(2,1)S(1)} %collective-permute-done.16.refs_1_, f32[32,8192]{1,0:T(8,128)} %shard_map.85.refs_2_), custom_call_target="tpu_custom_call", output_to_operand_aliasing={{}: (2, {})} | custom-call | bytes 786432 | tf_op jit(solution)/shard_map/pallas_call | solution.py:59
  (39 shorter events, 2.6 us)
Async XLA Ops:
  1.1 9.0 %collective-permute-start = (bf16[32,2048]{1,0:T(8,128)(2,1)S(1)}, bf16[32,2048]{1,0:T(8,128)(2,1)S(1)}, u32[]{:S(2)}, u32[]{:S(2)}) collective-permute-start(bf16[32,2048]{1,0:T(8,128)(2,1)S(1)} %get-tuple-element.43), channel_id=1, source_target_pairs={{0,1},{1,0},{2,3},{3,2},{4,5},{5,4},{6,7},{7,6},{8,9},{9,8},{10,11... | collective-permute-start | bytes 393224 | tf_op jit(solution)/shard_map/ppermute | solution.py:19
  2.8 7.5 %collective-permute-start.1 = (bf16[32,2048]{1,0:T(8,128)(2,1)S(1)}, bf16[32,2048]{1,0:T(8,128)(2,1)S(1)}, u32[]{:S(2)}, u32[]{:S(2)}) collective-permute-start(bf16[32,2048]{1,0:T(8,128)(2,1)S(1)} %get-tuple-element.44), channel_id=1, source_target_pairs={{0,3},{1,2},{2,1},{3,0},{4,7},{5,6},{6,5},{7,4},{8,11},{9,10},{10,... | collective-permute-start | bytes 393224 | tf_op jit(solution)/shard_map/ppermute | solution.py:19
  5.0 13.2 %slice-start = ((s8[8388608]{0:T(1024)(128)(4,1)}), s8[4194304]{0:T(1024)(128)(4,1)S(1)}, s32[]{:S(2)}) async-start(s8[8388608]{0:T(1024)(128)(4,1)} %bitcast), calls=%async_computation | async-start | bytes 8388608
  5.0 13.2 %slice-start.1 = ((s8[8388608]{0:T(1024)(128)(4,1)}), s8[4194304]{0:T(1024)(128)(4,1)S(1)}, s32[]{:S(2)}) async-start(s8[8388608]{0:T(1024)(128)(4,1)} %bitcast), calls=%async_computation.1 | async-start | bytes 8388608
  5.0 6.8 %collective-permute-start.2 = (bf16[32,2048]{1,0:T(8,128)(2,1)S(1)}, bf16[32,2048]{1,0:T(8,128)(2,1)S(1)}, u32[]{:S(2)}, u32[]{:S(2)}) collective-permute-start(bf16[32,2048]{1,0:T(8,128)(2,1)S(1)} %get-tuple-element.45), channel_id=1, source_target_pairs={{0,2},{1,3},{2,0},{3,1},{4,6},{5,7},{6,4},{7,5},{8,10},{9,11},{10,... | collective-permute-start | bytes 393224 | tf_op jit(solution)/shard_map/ppermute | solution.py:19
  12.5 7.2 %collective-permute-start.6 = (f16[144,256]{1,0:T(8,128)(2,1)S(1)}, f16[144,256]{1,0:T(8,128)(2,1)S(1)}, u32[]{:S(2)}, u32[]{:S(2)}) collective-permute-start(f16[144,256]{1,0:T(8,128)(2,1)S(1)} %convert_element_type.50), channel_id=1, source_target_pairs={{0,2},{1,3},{2,0},{3,1},{4,6},{5,7},{6,4},{7,5},{8,10},{9,11},{10,... | collective-permute-start | bytes 221192 | tf_op jit(solution)/shard_map/ppermute | solution.py:19
  14.3 5.6 %collective-permute-start.5 = (f16[144,256]{1,0:T(8,128)(2,1)S(1)}, f16[144,256]{1,0:T(8,128)(2,1)S(1)}, u32[]{:S(2)}, u32[]{:S(2)}) collective-permute-start(f16[144,256]{1,0:T(8,128)(2,1)S(1)} %convert_element_type.50), channel_id=1, source_target_pairs={{0,3},{1,2},{2,1},{3,0},{4,7},{5,6},{6,5},{7,4},{8,11},{9,10},{10,... | collective-permute-start | bytes 221192 | tf_op jit(solution)/shard_map/ppermute | solution.py:19
  15.6 4.7 %collective-permute-start.4 = (f16[144,256]{1,0:T(8,128)(2,1)S(1)}, f16[144,256]{1,0:T(8,128)(2,1)S(1)}, u32[]{:S(2)}, u32[]{:S(2)}) collective-permute-start(f16[144,256]{1,0:T(8,128)(2,1)S(1)} %convert_element_type.50), channel_id=1, source_target_pairs={{0,1},{1,0},{2,3},{3,2},{4,5},{5,4},{6,7},{7,6},{8,9},{9,8},{10,11... | collective-permute-start | bytes 221192 | tf_op jit(solution)/shard_map/ppermute | solution.py:19
  16.5 5.4 %collective-permute-start.3 = (f16[288,256]{1,0:T(8,128)(2,1)S(1)}, f16[288,256]{1,0:T(8,128)(2,1)S(1)}, u32[]{:S(2)}, u32[]{:S(2)}) collective-permute-start(f16[288,256]{1,0:T(8,128)(2,1)S(1)} %convert_element_type.48), channel_id=1, source_target_pairs={{0,1},{1,0},{2,3},{3,2},{4,5},{5,4},{6,7},{7,6},{8,9},{9,8},{10,11... | collective-permute-start | bytes 442376 | tf_op jit(solution)/shard_map/ppermute | solution.py:19
  20.4 1.5 %collective-permute-start.7 = (f32[128,256]{1,0:T(8,128)S(1)}, f32[128,256]{1,0:T(8,128)S(1)}, u32[]{:S(2)}, u32[]{:S(2)}) collective-permute-start(f32[128,256]{1,0:T(8,128)S(1)} %shard_map.79.own), channel_id=1, source_target_pairs={{0,4},{4,0},{8,12},{12,8},{16,20},{20,16},{24,28},{28,24},{32,36},... | collective-permute-start | bytes 393224 | tf_op jit(solution)/shard_map/ppermute | solution.py:19
  22.2 4.5 %collective-permute-start.9 = (f16[144,256]{1,0:T(8,128)(2,1)S(1)}, f16[144,256]{1,0:T(8,128)(2,1)S(1)}, u32[]{:S(2)}, u32[]{:S(2)}) collective-permute-start(f16[144,256]{1,0:T(8,128)(2,1)S(1)} %convert_element_type.56), channel_id=1, source_target_pairs={{0,8},{4,20},{8,0},{12,28},{16,24},{20,4},{24,16},{28,12},{32,40},... | collective-permute-start | bytes 221192 | tf_op jit(solution)/shard_map/ppermute | solution.py:79
  24.2 5.7 %collective-permute-start.11 = (f16[144,256]{1,0:T(8,128)(2,1)S(1)}, f16[144,256]{1,0:T(8,128)(2,1)S(1)}, u32[]{:S(2)}, u32[]{:S(2)}) collective-permute-start(f16[144,256]{1,0:T(8,128)(2,1)S(1)} %convert_element_type.56), channel_id=1, source_target_pairs={{0,24},{4,28},{8,16},{12,20},{16,8},{20,12},{24,0},{28,4},{32,56},... | collective-permute-start | bytes 221192 | tf_op jit(solution)/shard_map/ppermute | solution.py:19
  26.8 3.2 %collective-permute-start.10 = (f16[144,256]{1,0:T(8,128)(2,1)S(1)}, f16[144,256]{1,0:T(8,128)(2,1)S(1)}, u32[]{:S(2)}, u32[]{:S(2)}) collective-permute-start(f16[144,256]{1,0:T(8,128)(2,1)S(1)} %collective-permute-done.9), channel_id=1, source_target_pairs={{0,4},{4,0},{8,12},{12,8},{16,20},{20,16},{24,28},{28,24},{32,36},... | collective-permute-start | bytes 221192 | tf_op jit(solution)/shard_map/ppermute | solution.py:19
  27.7 5.6 %collective-permute-start.8 = (f16[144,256]{1,0:T(8,128)(2,1)S(1)}, f16[144,256]{1,0:T(8,128)(2,1)S(1)}, u32[]{:S(2)}, u32[]{:S(2)}) collective-permute-start(f16[144,256]{1,0:T(8,128)(2,1)S(1)} %convert_element_type.54), channel_id=1, source_target_pairs={{0,3},{1,2},{2,1},{3,0},{4,7},{5,6},{6,5},{7,4},{8,11},{9,10},{10,... | collective-permute-start | bytes 221192 | tf_op jit(solution)/shard_map/ppermute | solution.py:19
  30.4 5.8 %collective-permute-start.12 = (f16[144,256]{1,0:T(8,128)(2,1)S(1)}, f16[144,256]{1,0:T(8,128)(2,1)S(1)}, u32[]{:S(2)}, u32[]{:S(2)}) collective-permute-start(f16[144,256]{1,0:T(8,128)(2,1)S(1)} %convert_element_type.60), channel_id=1, source_target_pairs={{0,32},{4,68},{8,40},{12,76},{16,48},{20,84},{24,56},{28,92},{32,0... | collective-permute-start | bytes 221192 | tf_op jit(solution)/shard_map/ppermute | solution.py:79
  33.3 5.8 %collective-permute-start.14 = (f16[144,256]{1,0:T(8,128)(2,1)S(1)}, f16[144,256]{1,0:T(8,128)(2,1)S(1)}, u32[]{:S(2)}, u32[]{:S(2)}) collective-permute-start(f16[144,256]{1,0:T(8,128)(2,1)S(1)} %convert_element_type.60), channel_id=1, source_target_pairs={{0,96},{4,100},{8,104},{12,108},{16,112},{20,116},{24,120},{28,124... | collective-permute-start | bytes 221192 | tf_op jit(solution)/shard_map/ppermute | solution.py:19
  36.2 3.0 %collective-permute-start.13 = (f16[144,256]{1,0:T(8,128)(2,1)S(1)}, f16[144,256]{1,0:T(8,128)(2,1)S(1)}, u32[]{:S(2)}, u32[]{:S(2)}) collective-permute-start(f16[144,256]{1,0:T(8,128)(2,1)S(1)} %collective-permute-done.12), channel_id=1, source_target_pairs={{0,4},{4,0},{8,12},{12,8},{16,20},{20,16},{24,28},{28,24},{32,36},... | collective-permute-start | bytes 221192 | tf_op jit(solution)/shard_map/ppermute | solution.py:19
  40.4 7.6 %collective-permute-start.17 = (bf16[32,2048]{1,0:T(8,128)(2,1)S(1)}, bf16[32,2048]{1,0:T(8,128)(2,1)S(1)}, u32[]{:S(2)}, u32[]{:S(2)}) collective-permute-start(bf16[32,2048]{1,0:T(8,128)(2,1)S(1)} %get-tuple-element.78), channel_id=1, source_target_pairs={{0,2},{1,3},{2,0},{3,1},{4,6},{5,7},{6,4},{7,5},{8,10},{9,11},{10,... | collective-permute-start | bytes 393224 | tf_op jit(solution)/shard_map/ppermute | solution.py:19
  42.5 7.0 %collective-permute-start.15 = (bf16[32,2048]{1,0:T(8,128)(2,1)S(1)}, bf16[32,2048]{1,0:T(8,128)(2,1)S(1)}, u32[]{:S(2)}, u32[]{:S(2)}) collective-permute-start(bf16[32,2048]{1,0:T(8,128)(2,1)S(1)} %get-tuple-element.75), channel_id=1, source_target_pairs={{0,1},{1,0},{2,3},{3,2},{4,5},{5,4},{6,7},{7,6},{8,9},{9,8},{10,11... | collective-permute-start | bytes 393224 | tf_op jit(solution)/shard_map/ppermute | solution.py:19
  43.3 6.7 %collective-permute-start.16 = (bf16[32,2048]{1,0:T(8,128)(2,1)S(1)}, bf16[32,2048]{1,0:T(8,128)(2,1)S(1)}, u32[]{:S(2)}, u32[]{:S(2)}) collective-permute-start(bf16[32,2048]{1,0:T(8,128)(2,1)S(1)} %get-tuple-element.76), channel_id=1, source_target_pairs={{0,3},{1,2},{2,1},{3,0},{4,7},{5,6},{6,5},{7,4},{8,11},{9,10},{10,... | collective-permute-start | bytes 393224 | tf_op jit(solution)/shard_map/ppermute | solution.py:19

commit v7 on v6

--- a/solution.py
+++ b/solution.py
@@ -452,8 +452,8 @@
             input_output_aliases={} if under is None else {count: 0},
         )
 
-    most = join((own, blocks[0]), (0, 1))
-    return join(blocks[1:], (2, 3), most)
+    most = join((own, blocks[0], blocks[1]), (0, 1, 2))
+    return join((blocks[2],), (3,), most)
 
 
 def solution(mesh):

time: 51.2 us -> 51.3 us (level)
  transfers between devices with their start and end apart: 18 -> 18, of which waited for: 11 -> 10; matrix products, arithmetic and copies ran while one was open for 0% -> 0% of each run, Pallas kernels for 19% -> 19%
where the time goes in v7:
time: 51.3 us; the launch traced here: 51.2 us
  starting transfers between devices  25.6 us (50%)
  Pallas kernels  13.5 us (26%)
  waiting for transfers between devices  11.6 us (23%)
    ppermute x16, starting transfers between devices, swap(): return lax.ppermute(value, axis, pairs)  22 us
    pallas_call x14, Pallas kernels, call(): pl.pallas_call(body, out_shape=outs, compiler_params=pltpu.CompilerParams...  13.5 us
    ppermute x16, waiting for transfers between devices, swap(): return lax.ppermute(value, axis, pairs)  11.6 us
    ppermute x2, starting transfers between devices, line(): mine = lax.ppermute(message, axis, pairs)  3.56 us
  transfers between devices with their start and end apart: 18, of which 10 were waited for; matrix products, arithmetic and copies ran while one was open for 0% of the time, Pallas kernels for 19%

profile of v7, /device:TPU:0, one launch (start us, length us, event | category | flops | bytes accessed | tf_op | source)
XLA Modules:
  0.0 51.2 jit_solution(17377514828197926264)
XLA Ops:
  0.0 1.1 %shard_map.74 = (bf16[32,2048]{1,0:T(8,128)(2,1)S(1)}, bf16[32,2048]{1,0:T(8,128)(2,1)S(1)}, bf16[32,2048]{1,0:T(8,128)(2,1)S(1)}) custom-call(bf16[32,8192]{1,0:T(8,128)(2,1)} %source.1), custom_call_target="tpu_custom_call" | custom-call | bytes 786432 | tf_op jit(solution)/shard_map/pallas_call | solution.py:59
  1.1 1.7 %collective-permute-start = (bf16[32,2048]{1,0:T(8,128)(2,1)S(1)}, bf16[32,2048]{1,0:T(8,128)(2,1)S(1)}, u32[]{:S(2)}, u32[]{:S(2)}) collective-permute-start(bf16[32,2048]{1,0:T(8,128)(2,1)S(1)} %get-tuple-element.43), channel_id=1, source_target_pairs={{0,1},{1,0},{2,3},{3,2},{4,5},{5,4},{6,7},{7,6},{8,9},{9,8},{10,11... | collective-permute-start | bytes 393224 | tf_op jit(solution)/shard_map/ppermute | solution.py:19
  2.8 2.2 %collective-permute-start.1 = (bf16[32,2048]{1,0:T(8,128)(2,1)S(1)}, bf16[32,2048]{1,0:T(8,128)(2,1)S(1)}, u32[]{:S(2)}, u32[]{:S(2)}) collective-permute-start(bf16[32,2048]{1,0:T(8,128)(2,1)S(1)} %get-tuple-element.44), channel_id=1, source_target_pairs={{0,3},{1,2},{2,1},{3,0},{4,7},{5,6},{6,5},{7,4},{8,11},{9,10},{10,... | collective-permute-start | bytes 393224 | tf_op jit(solution)/shard_map/ppermute | solution.py:19
  5.0 0.7 %collective-permute-start.2 = (bf16[32,2048]{1,0:T(8,128)(2,1)S(1)}, bf16[32,2048]{1,0:T(8,128)(2,1)S(1)}, u32[]{:S(2)}, u32[]{:S(2)}) collective-permute-start(bf16[32,2048]{1,0:T(8,128)(2,1)S(1)} %get-tuple-element.45), channel_id=1, source_target_pairs={{0,2},{1,3},{2,0},{3,1},{4,6},{5,7},{6,4},{7,5},{8,10},{9,11},{10,... | collective-permute-start | bytes 393224 | tf_op jit(solution)/shard_map/ppermute | solution.py:19
  5.7 4.4 %shard_map.73 = (bf16[32,2048]{1,0:T(8,128)(2,1)S(1)}, bf16[2048,256]{1,0:T(8,128)(2,1)S(1)}, bf16[2,256,256]{2,1,0:T(8,128)(2,1)S(1)}, bf16[2,256,256]{2,1,0:T(...) custom-call(bf16[32,8192]{1,0:T(8,128)(2,1)} %source.1, ...), custom_call_target="tpu_custom_call" | custom-call | flops 1140850688 | bytes 4194304 | tf_op jit(solution)/shard_map/pallas_call | solution.py:59
  10.3 1.5 %collective-permute-done.2.third = bf16[32,2048]{1,0:T(8,128)(2,1)S(1)} collective-permute-done((bf16[32,2048]{1,0:T(8,128)(2,1)S(1)}, bf16[32,2048]{1,0:T(8,128)(2,1)S(1)}, u32[]{:S(2)}, u32[]{:S(2)}) %collective-permute-start.2) | collective-permute-done | bytes 131104 | tf_op jit(solution)/shard_map/ppermute | solution.py:19
  11.8 0.7 %shard_map.75 = (bf16[128,2048]{1,0:T(8,128)(2,1)S(1)}, f32[144,256]{1,0:T(8,128)S(1)}, f32[128,256]{1,0:T(8,128)S(1)}, f32[128,256]{1,0:T(8,128)S(1)}, f32[128,256]{1,0:T(8,128)S(1)}) custom-call(bf16[32,2048]{1,0:T(8,128)(2,1)S(1)} %get-tuple-element.42.own, bf16[32,2048]{1,0:T(8,128)(2,1)S(1)} %collective-permute-done.first, ...), custom_call_target="tpu_custom_call" | custom-call | flops 134217728 | bytes 2097152 | tf_op jit(solution)/shard_map/pallas_call | solution.py:59
  12.5 1.8 %collective-permute-start.6 = (f16[144,256]{1,0:T(8,128)(2,1)S(1)}, f16[144,256]{1,0:T(8,128)(2,1)S(1)}, u32[]{:S(2)}, u32[]{:S(2)}) collective-permute-start(f16[144,256]{1,0:T(8,128)(2,1)S(1)} %convert_element_type.50), channel_id=1, source_target_pairs={{0,2},{1,3},{2,0},{3,1},{4,6},{5,7},{6,4},{7,5},{8,10},{9,11},{10,... | collective-permute-start | bytes 221192 | tf_op jit(solution)/shard_map/ppermute | solution.py:19
  14.3 1.3 %collective-permute-start.5 = (f16[144,256]{1,0:T(8,128)(2,1)S(1)}, f16[144,256]{1,0:T(8,128)(2,1)S(1)}, u32[]{:S(2)}, u32[]{:S(2)}) collective-permute-start(f16[144,256]{1,0:T(8,128)(2,1)S(1)} %convert_element_type.50), channel_id=1, source_target_pairs={{0,3},{1,2},{2,1},{3,0},{4,7},{5,6},{6,5},{7,4},{8,11},{9,10},{10,... | collective-permute-start | bytes 221192 | tf_op jit(solution)/shard_map/ppermute | solution.py:19
  15.6 0.5 collective-permute-start.4
  16.5 1.6 %collective-permute-start.3 = (f16[288,256]{1,0:T(8,128)(2,1)S(1)}, f16[288,256]{1,0:T(8,128)(2,1)S(1)}, u32[]{:S(2)}, u32[]{:S(2)}) collective-permute-start(f16[288,256]{1,0:T(8,128)(2,1)S(1)} %convert_element_type.48), channel_id=1, source_target_pairs={{0,1},{1,0},{2,3},{3,2},{4,5},{5,4},{6,7},{7,6},{8,9},{9,8},{10,11... | collective-permute-start | bytes 442376 | tf_op jit(solution)/shard_map/ppermute | solution.py:19
  18.2 1.5 %shard_map.77.left = f32[128,1024]{1,0:T(8,128)S(1)} custom-call(bf16[128,2048]{1,0:T(8,128)(2,1)S(1)} %get-tuple-element.74.cols_ref, bf16[1,2048,2048]{2,1,0:T(8,128)(2,1)S(1)} %bitcast.1), custom_call_target="tpu_custom_call" | custom-call | flops 536870912 | bytes 4980736 | tf_op jit(solution)/shard_map/pallas_call | solution.py:59
  19.9 0.5 collective-permute-done.4
  20.5 1.4 %collective-permute-done.3 = f16[288,256]{1,0:T(8,128)(2,1)S(1)} collective-permute-done((f16[288,256]{1,0:T(8,128)(2,1)S(1)}, f16[288,256]{1,0:T(8,128)(2,1)S(1)}, u32[]{:S(2)}, u32[]{:S(2)}) %collective-permute-start.3) | collective-permute-done | bytes 147488 | tf_op jit(solution)/shard_map/ppermute | solution.py:19
  22.2 2.0 %collective-permute-start.9 = (f16[144,256]{1,0:T(8,128)(2,1)S(1)}, f16[144,256]{1,0:T(8,128)(2,1)S(1)}, u32[]{:S(2)}, u32[]{:S(2)}) collective-permute-start(f16[144,256]{1,0:T(8,128)(2,1)S(1)} %convert_element_type.56), channel_id=1, source_target_pairs={{0,8},{4,20},{8,0},{12,28},{16,24},{20,4},{24,16},{28,12},{32,40},... | collective-permute-start | bytes 221192 | tf_op jit(solution)/shard_map/ppermute | solution.py:79
  24.2 2.5 %collective-permute-start.11 = (f16[144,256]{1,0:T(8,128)(2,1)S(1)}, f16[144,256]{1,0:T(8,128)(2,1)S(1)}, u32[]{:S(2)}, u32[]{:S(2)}) collective-permute-start(f16[144,256]{1,0:T(8,128)(2,1)S(1)} %convert_element_type.56), channel_id=1, source_target_pairs={{0,24},{4,28},{8,16},{12,20},{16,8},{20,12},{24,0},{28,4},{32,56},... | collective-permute-start | bytes 221192 | tf_op jit(solution)/shard_map/ppermute | solution.py:19
  26.8 0.9 %collective-permute-start.10 = (f16[144,256]{1,0:T(8,128)(2,1)S(1)}, f16[144,256]{1,0:T(8,128)(2,1)S(1)}, u32[]{:S(2)}, u32[]{:S(2)}) collective-permute-start(f16[144,256]{1,0:T(8,128)(2,1)S(1)} %collective-permute-done.9), channel_id=1, source_target_pairs={{0,4},{4,0},{8,12},{12,8},{16,20},{20,16},{24,28},{28,24},{32,36},... | collective-permute-start | bytes 221192 | tf_op jit(solution)/shard_map/ppermute | solution.py:19
  27.7 1.6 %collective-permute-start.8 = (f16[144,256]{1,0:T(8,128)(2,1)S(1)}, f16[144,256]{1,0:T(8,128)(2,1)S(1)}, u32[]{:S(2)}, u32[]{:S(2)}) collective-permute-start(f16[144,256]{1,0:T(8,128)(2,1)S(1)} %convert_element_type.54), channel_id=1, source_target_pairs={{0,3},{1,2},{2,1},{3,0},{4,7},{5,6},{6,5},{7,4},{8,11},{9,10},{10,... | collective-permute-start | bytes 221192 | tf_op jit(solution)/shard_map/ppermute | solution.py:19
  29.3 0.6 %collective-permute-done.11 = f16[144,256]{1,0:T(8,128)(2,1)S(1)} collective-permute-done((f16[144,256]{1,0:T(8,128)(2,1)S(1)}, f16[144,256]{1,0:T(8,128)(2,1)S(1)}, u32[]{:S(2)}, u32[]{:S(2)}) %collective-permute-start.11) | collective-permute-done | bytes 73760 | tf_op jit(solution)/shard_map/ppermute | solution.py:19
  30.4 1.6 %collective-permute-start.12 = (f16[144,256]{1,0:T(8,128)(2,1)S(1)}, f16[144,256]{1,0:T(8,128)(2,1)S(1)}, u32[]{:S(2)}, u32[]{:S(2)}) collective-permute-start(f16[144,256]{1,0:T(8,128)(2,1)S(1)} %convert_element_type.60), channel_id=1, source_target_pairs={{0,32},{4,68},{8,40},{12,76},{16,48},{20,84},{24,56},{28,92},{32,0... | collective-permute-start | bytes 221192 | tf_op jit(solution)/shard_map/ppermute | solution.py:79
  32.0 1.4 %collective-permute-done.8 = f16[144,256]{1,0:T(8,128)(2,1)S(1)} collective-permute-done((f16[144,256]{1,0:T(8,128)(2,1)S(1)}, f16[144,256]{1,0:T(8,128)(2,1)S(1)}, u32[]{:S(2)}, u32[]{:S(2)}) %collective-permute-start.8) | collective-permute-done | bytes 73760 | tf_op jit(solution)/shard_map/ppermute | solution.py:19
  33.3 2.8 %collective-permute-start.14 = (f16[144,256]{1,0:T(8,128)(2,1)S(1)}, f16[144,256]{1,0:T(8,128)(2,1)S(1)}, u32[]{:S(2)}, u32[]{:S(2)}) collective-permute-start(f16[144,256]{1,0:T(8,128)(2,1)S(1)} %convert_element_type.60), channel_id=1, source_target_pairs={{0,96},{4,100},{8,104},{12,108},{16,112},{20,116},{24,120},{28,124... | collective-permute-start | bytes 221192 | tf_op jit(solution)/shard_map/ppermute | solution.py:19
  36.6 1.5 %shard_map.83.right = f32[128,1024]{1,0:T(8,128)S(1)} custom-call(bf16[128,2048]{1,0:T(8,128)(2,1)S(1)} %get-tuple-element.74.cols_ref, bf16[1,2048,2048]{2,1,0:T(8,128)(2,1)S(1)} %bitcast.1), custom_call_target="tpu_custom_call" | custom-call | flops 536870912 | bytes 4980736 | tf_op jit(solution)/shard_map/pallas_call | solution.py:59
  38.2 1.0 %collective-permute-done.14 = f16[144,256]{1,0:T(8,128)(2,1)S(1)} collective-permute-done((f16[144,256]{1,0:T(8,128)(2,1)S(1)}, f16[144,256]{1,0:T(8,128)(2,1)S(1)}, u32[]{:S(2)}, u32[]{:S(2)}) %collective-permute-start.14) | collective-permute-done | bytes 73760 | tf_op jit(solution)/shard_map/ppermute | solution.py:19
  39.2 1.1 %shard_map.84 = (f32[32,2048]{1,0:T(8,128)S(1)}, bf16[32,2048]{1,0:T(8,128)(2,1)S(1)}, bf16[32,2048]{1,0:T(8,128)(2,1)S(1)}, bf16[32,2048]{1,0:T(8,128)(2,1)S(1)}) custom-call(f32[128,256]{1,0:T(8,128)S(1)} %get-tuple-element.62.at_leaf, f32[128,256]{1,0:T(8,128)S(1)} %get-tuple-element.63.at_pair, f32[128,256]{1,0:T(8,128)S(1)} %get-tuple-element.64.at_group, ...), custom_call_target="tpu_custom_call" | custom-call | flops 134217728 | bytes 4194304 | tf_op jit(solution)/shard_map/pallas_call | solution.py:59
  40.4 2.1 %collective-permute-start.16 = (bf16[32,2048]{1,0:T(8,128)(2,1)S(1)}, bf16[32,2048]{1,0:T(8,128)(2,1)S(1)}, u32[]{:S(2)}, u32[]{:S(2)}) collective-permute-start(bf16[32,2048]{1,0:T(8,128)(2,1)S(1)} %get-tuple-element.77), channel_id=1, source_target_pairs={{0,2},{1,3},{2,0},{3,1},{4,6},{5,7},{6,4},{7,5},{8,10},{9,11},{10,... | collective-permute-start | bytes 393224 | tf_op jit(solution)/shard_map/ppermute | solution.py:19
  42.5 0.8 %collective-permute-start.17 = (bf16[32,2048]{1,0:T(8,128)(2,1)S(1)}, bf16[32,2048]{1,0:T(8,128)(2,1)S(1)}, u32[]{:S(2)}, u32[]{:S(2)}) collective-permute-start(bf16[32,2048]{1,0:T(8,128)(2,1)S(1)} %get-tuple-element.78), channel_id=1, source_target_pairs={{0,1},{1,0},{2,3},{3,2},{4,5},{5,4},{6,7},{7,6},{8,9},{9,8},{10,11... | collective-permute-start | bytes 393224 | tf_op jit(solution)/shard_map/ppermute | solution.py:19
  43.3 1.2 %collective-permute-start.15 = (bf16[32,2048]{1,0:T(8,128)(2,1)S(1)}, bf16[32,2048]{1,0:T(8,128)(2,1)S(1)}, u32[]{:S(2)}, u32[]{:S(2)}) collective-permute-start(bf16[32,2048]{1,0:T(8,128)(2,1)S(1)} %get-tuple-element.75), channel_id=1, source_target_pairs={{0,3},{1,2},{2,1},{3,0},{4,7},{5,6},{6,5},{7,4},{8,11},{9,10},{10,... | collective-permute-start | bytes 393224 | tf_op jit(solution)/shard_map/ppermute | solution.py:19
  44.5 3.4 %collective-permute-done.16.refs_1_ = bf16[32,2048]{1,0:T(8,128)(2,1)S(1)} collective-permute-done((bf16[32,2048]{1,0:T(8,128)(2,1)S(1)}, bf16[32,2048]{1,0:T(8,128)(2,1)S(1)}, u32[]{:S(2)}, u32[]{:S(2)}) %collective-permute-start.16) | collective-permute-done | bytes 131104 | tf_op jit(solution)/shard_map/ppermute | solution.py:19
  48.0 1.5 %collective-permute-done.17.refs_2_ = bf16[32,2048]{1,0:T(8,128)(2,1)S(1)} collective-permute-done((bf16[32,2048]{1,0:T(8,128)(2,1)S(1)}, bf16[32,2048]{1,0:T(8,128)(2,1)S(1)}, u32[]{:S(2)}, u32[]{:S(2)}) %collective-permute-start.17) | collective-permute-done | bytes 131104 | tf_op jit(solution)/shard_map/ppermute | solution.py:19
  49.5 0.9 %shard_map.85.refs_1_ = f32[32,8192]{1,0:T(8,128)} custom-call(f32[32,2048]{1,0:T(8,128)S(1)} %get-tuple-element.76.refs_0_, bf16[32,2048]{1,0:T(8,128)(2,1)S(1)} %collective-permute-done.16.refs_1_, bf16[32,2048]{1,0:T(8,128)(2,1)S(1)} %collective-permute-done.17.refs_2_), custom_call_target="tpu_custom_call" | custom-call | bytes 1179648 | tf_op jit(solution)/shard_map/pallas_call | solution.py:59
  50.4 0.7 %shard_map.86 = f32[32,8192]{1,0:T(8,128)} custom-call(bf16[32,2048]{1,0:T(8,128)(2,1)S(1)} %collective-permute-done.15.refs_0_, f32[32,8192]{1,0:T(8,128)} %shard_map.85.refs_1_), custom_call_target="tpu_custom_call", output_to_operand_aliasing={{}: (1, {})} | custom-call | bytes 393216 | tf_op jit(solution)/shard_map/pallas_call | solution.py:59
  (39 shorter events, 2.2 us)
Async XLA Ops:
  1.1 9.0 %collective-permute-start = (bf16[32,2048]{1,0:T(8,128)(2,1)S(1)}, bf16[32,2048]{1,0:T(8,128)(2,1)S(1)}, u32[]{:S(2)}, u32[]{:S(2)}) collective-permute-start(bf16[32,2048]{1,0:T(8,128)(2,1)S(1)} %get-tuple-element.43), channel_id=1, source_target_pairs={{0,1},{1,0},{2,3},{3,2},{4,5},{5,4},{6,7},{7,6},{8,9},{9,8},{10,11... | collective-permute-start | bytes 393224 | tf_op jit(solution)/shard_map/ppermute | solution.py:19
  2.8 7.5 %collective-permute-start.1 = (bf16[32,2048]{1,0:T(8,128)(2,1)S(1)}, bf16[32,2048]{1,0:T(8,128)(2,1)S(1)}, u32[]{:S(2)}, u32[]{:S(2)}) collective-permute-start(bf16[32,2048]{1,0:T(8,128)(2,1)S(1)} %get-tuple-element.44), channel_id=1, source_target_pairs={{0,3},{1,2},{2,1},{3,0},{4,7},{5,6},{6,5},{7,4},{8,11},{9,10},{10,... | collective-permute-start | bytes 393224 | tf_op jit(solution)/shard_map/ppermute | solution.py:19
  5.0 13.2 %slice-start = ((s8[8388608]{0:T(1024)(128)(4,1)}), s8[4194304]{0:T(1024)(128)(4,1)S(1)}, s32[]{:S(2)}) async-start(s8[8388608]{0:T(1024)(128)(4,1)} %bitcast), calls=%async_computation | async-start | bytes 8388608
  5.0 13.2 %slice-start.1 = ((s8[8388608]{0:T(1024)(128)(4,1)}), s8[4194304]{0:T(1024)(128)(4,1)S(1)}, s32[]{:S(2)}) async-start(s8[8388608]{0:T(1024)(128)(4,1)} %bitcast), calls=%async_computation.1 | async-start | bytes 8388608
  5.0 6.8 %collective-permute-start.2 = (bf16[32,2048]{1,0:T(8,128)(2,1)S(1)}, bf16[32,2048]{1,0:T(8,128)(2,1)S(1)}, u32[]{:S(2)}, u32[]{:S(2)}) collective-permute-start(bf16[32,2048]{1,0:T(8,128)(2,1)S(1)} %get-tuple-element.45), channel_id=1, source_target_pairs={{0,2},{1,3},{2,0},{3,1},{4,6},{5,7},{6,4},{7,5},{8,10},{9,11},{10,... | collective-permute-start | bytes 393224 | tf_op jit(solution)/shard_map/ppermute | solution.py:19
  12.5 7.2 %collective-permute-start.6 = (f16[144,256]{1,0:T(8,128)(2,1)S(1)}, f16[144,256]{1,0:T(8,128)(2,1)S(1)}, u32[]{:S(2)}, u32[]{:S(2)}) collective-permute-start(f16[144,256]{1,0:T(8,128)(2,1)S(1)} %convert_element_type.50), channel_id=1, source_target_pairs={{0,2},{1,3},{2,0},{3,1},{4,6},{5,7},{6,4},{7,5},{8,10},{9,11},{10,... | collective-permute-start | bytes 221192 | tf_op jit(solution)/shard_map/ppermute | solution.py:19
  14.3 5.6 %collective-permute-start.5 = (f16[144,256]{1,0:T(8,128)(2,1)S(1)}, f16[144,256]{1,0:T(8,128)(2,1)S(1)}, u32[]{:S(2)}, u32[]{:S(2)}) collective-permute-start(f16[144,256]{1,0:T(8,128)(2,1)S(1)} %convert_element_type.50), channel_id=1, source_target_pairs={{0,3},{1,2},{2,1},{3,0},{4,7},{5,6},{6,5},{7,4},{8,11},{9,10},{10,... | collective-permute-start | bytes 221192 | tf_op jit(solution)/shard_map/ppermute | solution.py:19
  15.6 4.7 %collective-permute-start.4 = (f16[144,256]{1,0:T(8,128)(2,1)S(1)}, f16[144,256]{1,0:T(8,128)(2,1)S(1)}, u32[]{:S(2)}, u32[]{:S(2)}) collective-permute-start(f16[144,256]{1,0:T(8,128)(2,1)S(1)} %convert_element_type.50), channel_id=1, source_target_pairs={{0,1},{1,0},{2,3},{3,2},{4,5},{5,4},{6,7},{7,6},{8,9},{9,8},{10,11... | collective-permute-start | bytes 221192 | tf_op jit(solution)/shard_map/ppermute | solution.py:19
  16.5 5.4 %collective-permute-start.3 = (f16[288,256]{1,0:T(8,128)(2,1)S(1)}, f16[288,256]{1,0:T(8,128)(2,1)S(1)}, u32[]{:S(2)}, u32[]{:S(2)}) collective-permute-start(f16[288,256]{1,0:T(8,128)(2,1)S(1)} %convert_element_type.48), channel_id=1, source_target_pairs={{0,1},{1,0},{2,3},{3,2},{4,5},{5,4},{6,7},{7,6},{8,9},{9,8},{10,11... | collective-permute-start | bytes 442376 | tf_op jit(solution)/shard_map/ppermute | solution.py:19
  20.4 1.5 %collective-permute-start.7 = (f32[128,256]{1,0:T(8,128)S(1)}, f32[128,256]{1,0:T(8,128)S(1)}, u32[]{:S(2)}, u32[]{:S(2)}) collective-permute-start(f32[128,256]{1,0:T(8,128)S(1)} %shard_map.79.own), channel_id=1, source_target_pairs={{0,4},{4,0},{8,12},{12,8},{16,20},{20,16},{24,28},{28,24},{32,36},... | collective-permute-start | bytes 393224 | tf_op jit(solution)/shard_map/ppermute | solution.py:19
  22.2 4.5 %collective-permute-start.9 = (f16[144,256]{1,0:T(8,128)(2,1)S(1)}, f16[144,256]{1,0:T(8,128)(2,1)S(1)}, u32[]{:S(2)}, u32[]{:S(2)}) collective-permute-start(f16[144,256]{1,0:T(8,128)(2,1)S(1)} %convert_element_type.56), channel_id=1, source_target_pairs={{0,8},{4,20},{8,0},{12,28},{16,24},{20,4},{24,16},{28,12},{32,40},... | collective-permute-start | bytes 221192 | tf_op jit(solution)/shard_map/ppermute | solution.py:79
  24.2 5.7 %collective-permute-start.11 = (f16[144,256]{1,0:T(8,128)(2,1)S(1)}, f16[144,256]{1,0:T(8,128)(2,1)S(1)}, u32[]{:S(2)}, u32[]{:S(2)}) collective-permute-start(f16[144,256]{1,0:T(8,128)(2,1)S(1)} %convert_element_type.56), channel_id=1, source_target_pairs={{0,24},{4,28},{8,16},{12,20},{16,8},{20,12},{24,0},{28,4},{32,56},... | collective-permute-start | bytes 221192 | tf_op jit(solution)/shard_map/ppermute | solution.py:19
  26.8 3.2 %collective-permute-start.10 = (f16[144,256]{1,0:T(8,128)(2,1)S(1)}, f16[144,256]{1,0:T(8,128)(2,1)S(1)}, u32[]{:S(2)}, u32[]{:S(2)}) collective-permute-start(f16[144,256]{1,0:T(8,128)(2,1)S(1)} %collective-permute-done.9), channel_id=1, source_target_pairs={{0,4},{4,0},{8,12},{12,8},{16,20},{20,16},{24,28},{28,24},{32,36},... | collective-permute-start | bytes 221192 | tf_op jit(solution)/shard_map/ppermute | solution.py:19
  27.7 5.6 %collective-permute-start.8 = (f16[144,256]{1,0:T(8,128)(2,1)S(1)}, f16[144,256]{1,0:T(8,128)(2,1)S(1)}, u32[]{:S(2)}, u32[]{:S(2)}) collective-permute-start(f16[144,256]{1,0:T(8,128)(2,1)S(1)} %convert_element_type.54), channel_id=1, source_target_pairs={{0,3},{1,2},{2,1},{3,0},{4,7},{5,6},{6,5},{7,4},{8,11},{9,10},{10,... | collective-permute-start | bytes 221192 | tf_op jit(solution)/shard_map/ppermute | solution.py:19
  30.4 5.8 %collective-permute-start.12 = (f16[144,256]{1,0:T(8,128)(2,1)S(1)}, f16[144,256]{1,0:T(8,128)(2,1)S(1)}, u32[]{:S(2)}, u32[]{:S(2)}) collective-permute-start(f16[144,256]{1,0:T(8,128)(2,1)S(1)} %convert_element_type.60), channel_id=1, source_target_pairs={{0,32},{4,68},{8,40},{12,76},{16,48},{20,84},{24,56},{28,92},{32,0... | collective-permute-start | bytes 221192 | tf_op jit(solution)/shard_map/ppermute | solution.py:79
  33.3 5.8 %collective-permute-start.14 = (f16[144,256]{1,0:T(8,128)(2,1)S(1)}, f16[144,256]{1,0:T(8,128)(2,1)S(1)}, u32[]{:S(2)}, u32[]{:S(2)}) collective-permute-start(f16[144,256]{1,0:T(8,128)(2,1)S(1)} %convert_element_type.60), channel_id=1, source_target_pairs={{0,96},{4,100},{8,104},{12,108},{16,112},{20,116},{24,120},{28,124... | collective-permute-start | bytes 221192 | tf_op jit(solution)/shard_map/ppermute | solution.py:19
  36.2 3.0 %collective-permute-start.13 = (f16[144,256]{1,0:T(8,128)(2,1)S(1)}, f16[144,256]{1,0:T(8,128)(2,1)S(1)}, u32[]{:S(2)}, u32[]{:S(2)}) collective-permute-start(f16[144,256]{1,0:T(8,128)(2,1)S(1)} %collective-permute-done.12), channel_id=1, source_target_pairs={{0,4},{4,0},{8,12},{12,8},{16,20},{20,16},{24,28},{28,24},{32,36},... | collective-permute-start | bytes 221192 | tf_op jit(solution)/shard_map/ppermute | solution.py:19
  40.4 7.6 %collective-permute-start.16 = (bf16[32,2048]{1,0:T(8,128)(2,1)S(1)}, bf16[32,2048]{1,0:T(8,128)(2,1)S(1)}, u32[]{:S(2)}, u32[]{:S(2)}) collective-permute-start(bf16[32,2048]{1,0:T(8,128)(2,1)S(1)} %get-tuple-element.77), channel_id=1, source_target_pairs={{0,2},{1,3},{2,0},{3,1},{4,6},{5,7},{6,4},{7,5},{8,10},{9,11},{10,... | collective-permute-start | bytes 393224 | tf_op jit(solution)/shard_map/ppermute | solution.py:19
  42.5 7.0 %collective-permute-start.17 = (bf16[32,2048]{1,0:T(8,128)(2,1)S(1)}, bf16[32,2048]{1,0:T(8,128)(2,1)S(1)}, u32[]{:S(2)}, u32[]{:S(2)}) collective-permute-start(bf16[32,2048]{1,0:T(8,128)(2,1)S(1)} %get-tuple-element.78), channel_id=1, source_target_pairs={{0,1},{1,0},{2,3},{3,2},{4,5},{5,4},{6,7},{7,6},{8,9},{9,8},{10,11... | collective-permute-start | bytes 393224 | tf_op jit(solution)/shard_map/ppermute | solution.py:19
  43.3 7.1 %collective-permute-start.15 = (bf16[32,2048]{1,0:T(8,128)(2,1)S(1)}, bf16[32,2048]{1,0:T(8,128)(2,1)S(1)}, u32[]{:S(2)}, u32[]{:S(2)}) collective-permute-start(bf16[32,2048]{1,0:T(8,128)(2,1)S(1)} %get-tuple-element.75), channel_id=1, source_target_pairs={{0,3},{1,2},{2,1},{3,0},{4,7},{5,6},{6,5},{7,4},{8,11},{9,10},{10,... | collective-permute-start | bytes 393224 | tf_op jit(solution)/shard_map/ppermute | solution.py:19
